TPU v7x, 32 devices: a whole 2x2x4 slice. The times are simulated.
32 devices in a mesh: dp: 4 (over z), blk: 4 (over y, x), head: 2 (over core).
Axes of the slice: x: 2, y: 2, z: 4, core: 2. Of those that a mesh axis runs over, the one named last changes fastest.
Arguments:
- layer_input: bfloat16 [4, 2048, 768], P(None, ('dp', 'blk')), may hold values from -6 to 6
- sequence_lengths: int32 [4, 4, 3], P(None, 'dp'), may hold values from 0 to 512, as said below
- alibi_slopes: float32 [12], P('head'), may hold values from 0.0009765625 to 0.12
- project_weight: bfloat16 [768, 3, 768], P('dp', None, 'head'), may hold values from -0.21875 to 0.21875
- project_bias: float32 [2, 768], P(None, 'head'), may hold values from -1.75 to 1.75
- output_weight: bfloat16 [768, 768], P('head', 'dp'), may hold values from -0.875 to 0.875
- output_bias: float32 [768], replicated, may hold values from -1.75 to 1.75
- first_gain: float32 [768], replicated, may hold values from 0.25 to 1.75
- first_shift: float32 [768], replicated, may hold values from -1.75 to 1.75
- expand_weight: bfloat16 [768, 2, 3072], P('dp', None, 'head'), may hold values from -0.21875 to 0.21875
- expand_bias: float32 [2, 3072], P(None, 'head'), may hold values from -1.75 to 1.75
- down_weight: bfloat16 [3072, 768], P('head', 'dp'), may hold values from -0.15625 to 0.15625
- down_bias: float32 [768], replicated, may hold values from -1.75 to 1.75
- second_gain: float32 [768], replicated, may hold values from 0.25 to 1.75
- second_shift: float32 [768], replicated, may hold values from -1.75 to 1.75
- layer_cotangent: bfloat16 [4, 2048, 768], P(None, ('dp', 'blk')), may hold values from -6 to 6
Outputs:
- layer_output: bfloat16 [4, 2048, 768], P(None, ('dp', 'blk'))
- input_gradient: float32 [4, 2048, 768], P(None, ('dp', 'blk'))
- project_weight_gradient: float32 [768, 3, 768], P('dp', None, 'head')
- project_bias_gradient: float32 [2, 768], P(None, 'head')
- output_weight_gradient: float32 [768, 768], P('head', 'dp')
- output_bias_gradient: float32 [768], replicated
- first_gain_gradient: float32 [768], replicated
- first_shift_gradient: float32 [768], replicated
- expand_weight_gradient: float32 [768, 2, 3072], P('dp', None, 'head')
- expand_bias_gradient: float32 [2, 3072], P(None, 'head')
- down_weight_gradient: float32 [3072, 768], P('head', 'dp')
- down_bias_gradient: float32 [768], replicated
- second_gain_gradient: float32 [768], replicated
- second_shift_gradient: float32 [768], replicated
Inputs may be any that keep to these rules, and one draw needn't show every extreme that they name: `sequence_lengths`: for each micro-batch and group, the three slots hold the lengths of one to three sequences laid end to end from the group's first token; used lengths are 128 or more and sum to 512; unused slots are 0 and follow the used ones; in every group some micro-batch holds a single sequence of 512 tokens.
All inputs are finite; a program needn't handle non-finite values.
Results may differ from a plain program's by a relative error of at most 0.025.
Values may be sent and summed in bfloat16 or wider, within the bound.
A program may use at most 128 MiB of HBM per device.

v0:
```python
import math

import jax
import jax.numpy as jnp
from jax import lax
from jax.sharding import PartitionSpec as P

EPSILON = 1e-12
MASKED = -1e30


def shifted(value, axis, steps):
    count = lax.axis_size(axis)
    pairs = [(source, (source + steps) % count) for source in range(count)]
    return lax.ppermute(value, axis, pairs)


def normalize(rows, gain, shift):
    mean = jnp.mean(rows, axis=-1, keepdims=True)
    centered = rows - mean
    spread = jnp.mean(centered * centered, axis=-1, keepdims=True)
    return centered * lax.rsqrt(spread + EPSILON) * gain + shift


def gelu_product(gate_part, up_part):
    return jax.nn.gelu(gate_part, approximate=False) * up_part


def sequence_ids(lengths, positions):
    first = lengths[:, 0:1]
    second = first + lengths[:, 1:2]
    later = (positions[None, :] >= first).astype(jnp.int32)
    return later + (positions[None, :] >= second).astype(jnp.int32)


def block_scores(query, keys, slopes, query_pos, key_pos, query_seq, key_seq):
    scale = query.shape[-1] ** (-0.5)
    raw = jnp.einsum("mqhd,mkhd->mhqk", query, keys, preferred_element_type=jnp.float32)
    distance = jnp.abs(query_pos[:, None] - key_pos[None, :]).astype(jnp.float32)
    scores = raw * scale - slopes[None, :, None, None] * distance[None, None]
    same = (query_seq[:, :, None] == key_seq[:, None, :])[:, None]
    return (jnp.where(same, scores, MASKED), same)


def forward_update(state, query, keys, values, slopes, query_pos, key_pos, query_seq, key_seq):
    top, total, accum = state
    scores, same = block_scores(query, keys, slopes, query_pos, key_pos, query_seq, key_seq)
    new_top = jnp.maximum(top, jnp.max(scores, axis=-1))
    weights = jnp.where(same, jnp.exp(scores - new_top[..., None]), 0.0)
    factor = jnp.exp(top - new_top)
    total = total * factor + jnp.sum(weights, axis=-1)
    update = jnp.einsum(
        "mhqk,mkhd->mqhd", weights.astype(jnp.bfloat16), values, preferred_element_type=jnp.float32
    )
    accum = accum * jnp.transpose(factor, (0, 2, 1))[..., None] + update
    return (new_top, total, accum)


def over_blocks(function, state, arrays, start):
    count_rows = arrays[0].shape[1]
    block = math.gcd(count_rows, 512)
    if block == count_rows:
        return function(state, arrays, start)

    def step(index, carry):
        offset = index * block
        blocks = tuple((lax.dynamic_slice_in_dim(item, offset, block, 1) for item in arrays))
        return function(carry, blocks, start + offset)

    return lax.fori_loop(0, count_rows // block, step, state)


def local(
    layer_input,
    sequence_lengths,
    alibi_slopes,
    project_weight,
    project_bias,
    output_weight,
    output_bias,
    first_gain,
    first_shift,
    expand_weight,
    expand_bias,
    down_weight,
    down_bias,
    second_gain,
    second_shift,
    layer_cotangent,
):
    batches, tokens, width = layer_input.shape
    heads = alibi_slopes.shape[0]
    local_width = project_weight.shape[2]
    head_size = local_width // heads
    units = expand_weight.shape[2]
    rows_all = batches * tokens
    scale = head_size ** (-0.5)
    project_full, output_full, expand_full, down_full = (
        lax.all_gather(project_weight, "dp", axis=0, tiled=True),
        lax.all_gather(output_weight, "dp", axis=1, tiled=True),
        lax.all_gather(expand_weight, "dp", axis=0, tiled=True),
        lax.all_gather(down_weight, "dp", axis=1, tiled=True),
    )
    lengths = sequence_lengths.reshape(batches, 3)
    cycle_index = lax.axis_index("blk")
    cycle_size = lax.axis_size("blk")
    own_pos = cycle_index * tokens + jnp.arange(tokens, dtype=jnp.int32)
    own_seq = sequence_ids(lengths, own_pos)

    def split_heads(item):
        return item.reshape(item.shape[0], item.shape[1], heads, head_size)

    flat_input = layer_input.reshape(rows_all, width)
    mixed = jnp.dot(
        flat_input, project_full.reshape(width, 3 * local_width), preferred_element_type=jnp.float32
    )
    query = (
        (mixed[:, :local_width] + project_bias[0])
        .astype(jnp.bfloat16)
        .reshape(batches, tokens, local_width)
    )
    keys = (
        mixed[:, local_width : 2 * local_width]
        .astype(jnp.bfloat16)
        .reshape(batches, tokens, local_width)
    )
    values = (
        (mixed[:, 2 * local_width :] + project_bias[1])
        .astype(jnp.bfloat16)
        .reshape(batches, tokens, local_width)
    )
    query_heads = split_heads(query)
    initial = (
        jnp.full((batches, heads, tokens), MASKED, jnp.float32),
        jnp.zeros((batches, heads, tokens), jnp.float32),
        jnp.zeros((batches, tokens, heads, head_size), jnp.float32),
    )

    def inner(carry, blocks, block_start):
        key_pos = block_start + jnp.arange(blocks[0].shape[1], dtype=jnp.int32)
        key_seq = sequence_ids(lengths, key_pos)
        return forward_update(
            carry,
            query_heads,
            split_heads(blocks[0]),
            split_heads(blocks[1]),
            alibi_slopes,
            own_pos,
            key_pos,
            own_seq,
            key_seq,
        )

    top, total, accum = over_blocks(
        inner,
        initial,
        (
            lax.all_gather(keys, "blk", axis=1, tiled=True),
            lax.all_gather(values, "blk", axis=1, tiled=True),
        ),
        jnp.int32(0),
    )
    context = accum / jnp.transpose(total, (0, 2, 1))[..., None]
    log_total = top + jnp.log(total)
    context_low = context.astype(jnp.bfloat16).reshape(rows_all, local_width)
    branch_part = jnp.dot(context_low, output_full, preferred_element_type=jnp.float32)
    branch = lax.psum(branch_part.astype(jnp.bfloat16), "head").astype(jnp.float32) + output_bias
    first_in = flat_input.astype(jnp.float32) + branch
    first_out, first_pull = jax.vjp(normalize, first_in, first_gain, first_shift)
    first_low = first_out.astype(jnp.bfloat16)
    expanded = jnp.dot(
        first_low, expand_full.reshape(width, 2 * units), preferred_element_type=jnp.float32
    )
    expanded = expanded + expand_bias.reshape(2 * units)
    hidden_act, gelu_pull = jax.vjp(gelu_product, expanded[:, :units], expanded[:, units:])
    hidden_low = hidden_act.astype(jnp.bfloat16)
    feed_part = jnp.dot(hidden_low, down_full, preferred_element_type=jnp.float32)
    feed = lax.psum(feed_part.astype(jnp.bfloat16), "head").astype(jnp.float32) + down_bias
    second_in = first_out + feed
    result, second_pull = jax.vjp(normalize, second_in, second_gain, second_shift)
    layer_output = result.astype(jnp.bfloat16).reshape(batches, tokens, width)
    grad_result = layer_cotangent.reshape(rows_all, width).astype(jnp.float32)
    grad_second, second_gain_grad, second_shift_grad = second_pull(grad_result)
    grad_feed = grad_second.astype(jnp.bfloat16)
    down_bias_grad = jnp.sum(grad_feed.astype(jnp.float32), axis=0)
    down_part = jnp.einsum("rf,rd->fd", hidden_low, grad_feed, preferred_element_type=jnp.float32)
    grad_hidden = jnp.einsum("rd,fd->rf", grad_feed, down_full, preferred_element_type=jnp.float32)
    grad_gate, grad_up = gelu_pull(grad_hidden)
    grad_expanded = jnp.concatenate([grad_gate, grad_up], axis=1).astype(jnp.bfloat16)
    expand_bias_grad = jnp.sum(grad_expanded.astype(jnp.float32), axis=0).reshape(2, units)
    expand_part = jnp.einsum(
        "rd,rf->df", first_low, grad_expanded, preferred_element_type=jnp.float32
    ).reshape(width, 2, units)
    first_back = jnp.einsum(
        "rf,df->rd",
        grad_expanded,
        expand_full.reshape(width, 2 * units),
        preferred_element_type=jnp.float32,
    )
    grad_first = grad_second + lax.psum(first_back.astype(jnp.bfloat16), "head").astype(jnp.float32)
    grad_first_in, first_gain_grad, first_shift_grad = first_pull(grad_first)
    grad_branch = grad_first_in.astype(jnp.bfloat16)
    output_bias_grad = jnp.sum(grad_branch.astype(jnp.float32), axis=0)
    output_part = jnp.einsum(
        "rc,rd->cd", context_low, grad_branch, preferred_element_type=jnp.float32
    )
    grad_context = jnp.einsum(
        "rd,cd->rc", grad_branch, output_full, preferred_element_type=jnp.float32
    )
    grad_context = grad_context.astype(jnp.bfloat16).reshape(batches, tokens, local_width)
    grad_heads = split_heads(grad_context)
    delta_rows = jnp.sum(grad_heads.astype(jnp.float32) * context, axis=-1)
    delta_heads = jnp.transpose(delta_rows, (0, 2, 1))
    zeros_heads = jnp.zeros((batches, tokens, heads, head_size), jnp.float32)
    zeros_flat = jnp.zeros((batches, tokens, local_width), jnp.float32)

    def cycle_step(carry, anchor):
        keys_now, values_now, grad_keys_now, grad_values_now, grad_query = carry
        key_pos = anchor * tokens + jnp.arange(tokens, dtype=jnp.int32)
        key_seq = sequence_ids(lengths, key_pos)
        keys_block = split_heads(keys_now)
        values_block = split_heads(values_now)
        scores, same = block_scores(
            query_heads, keys_block, alibi_slopes, own_pos, key_pos, own_seq, key_seq
        )
        weights = jnp.where(same, jnp.exp(scores - log_total[..., None]), 0.0)
        grad_prob = jnp.einsum(
            "mqhd,mkhd->mhqk", grad_heads, values_block, preferred_element_type=jnp.float32
        )
        grad_score = (weights * (grad_prob - delta_heads[..., None])).astype(jnp.bfloat16)
        grad_query = (
            grad_query
            + jnp.einsum(
                "mhqk,mkhd->mqhd", grad_score, keys_block, preferred_element_type=jnp.float32
            )
            * scale
        )
        key_term = (
            jnp.einsum(
                "mhqk,mqhd->mkhd", grad_score, query_heads, preferred_element_type=jnp.float32
            )
            * scale
        )
        value_term = jnp.einsum(
            "mhqk,mqhd->mkhd",
            weights.astype(jnp.bfloat16),
            grad_heads,
            preferred_element_type=jnp.float32,
        )
        grad_keys_now = grad_keys_now + key_term.reshape(grad_keys_now.shape)
        grad_values_now = grad_values_now + value_term.reshape(grad_values_now.shape)
        return (keys_now, values_now, grad_keys_now, grad_values_now, grad_query)

    def cycle_turn(index, carry):
        anchor = (cycle_index - index) % cycle_size
        updated = cycle_step(carry, anchor)
        moved = (
            shifted(updated[0], "blk", 1),
            shifted(updated[1], "blk", 1),
            shifted(updated[2].astype(jnp.bfloat16), "blk", 1).astype(jnp.float32),
            shifted(updated[3].astype(jnp.bfloat16), "blk", 1).astype(jnp.float32),
        )
        return (
            moved[0],
            moved[1],
            moved[2].astype(jnp.float32),
            moved[3].astype(jnp.float32),
            updated[4],
        )

    carry = lax.fori_loop(
        0, cycle_size - 1, cycle_turn, (keys, values, zeros_flat, zeros_flat, zeros_heads)
    )
    final = cycle_step(carry, (cycle_index + 1) % cycle_size)
    returned = (
        shifted(final[2].astype(jnp.bfloat16), "blk", 1).astype(jnp.float32),
        shifted(final[3].astype(jnp.bfloat16), "blk", 1).astype(jnp.float32),
    )
    grad_keys = returned[0].astype(jnp.float32)
    grad_values = returned[1].astype(jnp.float32)
    grad_query = final[4].reshape(batches, tokens, local_width)
    grad_mixed = jnp.concatenate(
        [
            grad_query.reshape(rows_all, local_width),
            grad_keys.reshape(rows_all, local_width),
            grad_values.reshape(rows_all, local_width),
        ],
        axis=1,
    ).astype(jnp.bfloat16)
    project_bias_grad = jnp.stack(
        [
            jnp.sum(grad_mixed[:, :local_width].astype(jnp.float32), axis=0),
            jnp.sum(grad_mixed[:, 2 * local_width :].astype(jnp.float32), axis=0),
        ]
    )
    project_part = jnp.einsum(
        "rd,rc->dc", flat_input, grad_mixed, preferred_element_type=jnp.float32
    ).reshape(width, 3, local_width)
    input_back = jnp.einsum(
        "rc,dc->rd",
        grad_mixed,
        project_full.reshape(width, 3 * local_width),
        preferred_element_type=jnp.float32,
    )
    input_gradient = grad_first_in + lax.psum(input_back.astype(jnp.bfloat16), "head").astype(
        jnp.float32
    )
    shards = (
        lax.psum_scatter(
            project_part.astype(jnp.bfloat16), "dp", scatter_dimension=0, tiled=True
        ).astype(jnp.float32),
        lax.psum_scatter(
            output_part.astype(jnp.bfloat16), "dp", scatter_dimension=1, tiled=True
        ).astype(jnp.float32),
        lax.psum_scatter(
            expand_part.astype(jnp.bfloat16), "dp", scatter_dimension=0, tiled=True
        ).astype(jnp.float32),
        lax.psum_scatter(
            down_part.astype(jnp.bfloat16), "dp", scatter_dimension=1, tiled=True
        ).astype(jnp.float32),
    )
    totals = (
        lax.psum(shards[0].astype(jnp.bfloat16), "blk").astype(jnp.float32),
        lax.psum(shards[1].astype(jnp.bfloat16), "blk").astype(jnp.float32),
        lax.psum(shards[2].astype(jnp.bfloat16), "blk").astype(jnp.float32),
        lax.psum(shards[3].astype(jnp.bfloat16), "blk").astype(jnp.float32),
    )
    small = lax.psum(
        (
            project_bias_grad,
            output_bias_grad,
            first_gain_grad,
            first_shift_grad,
            expand_bias_grad,
            down_bias_grad,
            second_gain_grad,
            second_shift_grad,
        ),
        ("dp", "blk"),
    )
    return (
        layer_output,
        input_gradient.reshape(batches, tokens, width),
        totals[0],
        small[0],
        totals[1],
        small[1],
        small[2],
        small[3],
        totals[2],
        small[4],
        totals[3],
        small[5],
        small[6],
        small[7],
    )


def solution(mesh):
    in_specs = (
        P(None, ("dp", "blk"), None),
        P(None, "dp", None),
        P("head"),
        P("dp", None, "head"),
        P(None, "head"),
        P("head", "dp"),
        P(),
        P(),
        P(),
        P("dp", None, "head"),
        P(None, "head"),
        P("head", "dp"),
        P(),
        P(),
        P(),
        P(None, ("dp", "blk"), None),
    )
    out_specs = (
        P(None, ("dp", "blk"), None),
        P(None, ("dp", "blk"), None),
        P("dp", None, "head"),
        P(None, "head"),
        P("head", "dp"),
        P(),
        P(),
        P(),
        P("dp", None, "head"),
        P(None, "head"),
        P("head", "dp"),
        P(),
        P(),
        P(),
    )
    return jax.shard_map(local, mesh=mesh, in_specs=in_specs, out_specs=out_specs, check_vma=False)
```

profile of v0, /device:TPU:0, one launch (start us, length us, event | category | flops | bytes accessed | tf_op | source)
XLA Modules:
  0.0 758.5 jit_solution(11925193884181000880)
XLA Ops:
  8.0 44.7 %all-gather.6.cloned.1.call-done = bf16[768,3,384]{2,0,1:T(8,128)(2,1)} async-done(((bf16[192,3,384]{2,0,1:T(8,128)(2,1)}), bf16[768,3,384]{2,0,1:T(8,128)(2,1)}) %all-gather.6.cloned.1.call-update) | async-done | bytes 1769488 | tf_op jit(solution)/shard_map/all_gather | solution.py:99
  52.6 2.6 copy.70
  62.3 17.0 %all_gather.21 = bf16[384,768]{0,1:T(8,128)(2,1)} all-gather(bf16[384,192]{0,1:T(8,128)(2,1)S(1)} %copy-done.42), channel_id=1, replica_groups=mesh['dp'=4,'blk'=4,'head'=2] {'dp'}, dimensions={1}, use_global_device_ids=true | all-gather | bytes 737280 | tf_op jit(solution)/shard_map/all_gather | solution.py:100
  80.8 7.3 all-gather.8.cloned.1.call-done
  89.8 2.6 fusion.10
  95.8 25.2 %all-gather.10.cloned.1.call-done = bf16[4,512,384]{2,1,0:T(8,128)(2,1)} async-done(((bf16[4,128,384]{2,1,0:T(8,128)(2,1)}), bf16[4,512,384]{2,1,0:T(8,128)(2,1)}) %all-gather.10.cloned.1.call-update) | async-done | bytes 1572880 | tf_op jit(solution)/shard_map/all_gather | solution.py:159
  123.5 6.4 fusion.75
  134.6 17.3 %all-reduce.10.cloned.1.call-done = bf16[512,768]{1,0:T(8,128)(2,1)} async-done(((bf16[512,768]{1,0:T(8,128)(2,1)}), bf16[512,768]{1,0:T(8,128)(2,1)}) %all-reduce.10.cloned.1.call-update) | async-done | bytes 786448 | tf_op jit(solution)/shard_map/psum | solution.py:167
  154.0 90.1 %all-gather.12.cloned.1.call-done = bf16[768,2,1536]{2,1,0:T(2,128)(2,1)} async-done(((bf16[192,2,1536]{2,1,0:T(2,128)(2,1)}), bf16[768,2,1536]{2,1,0:T(2,128)(2,1)}) %all-gather.12.cloned.1.call-update) | async-done | bytes 4718608 | tf_op jit(solution)/shard_map/all_gather | solution.py:101
  244.1 3.6 copy.98
  247.7 2.7 convolution_add_fusion
  250.4 2.7 copy-done.14
  253.1 7.7 %multiply_convert_fusion.2 = (bf16[512,1536]{1,0:T(8,128)(2,1)S(1)}, f32[512,1536]{1,0:T(8,128)}) fusion(f32[512,3072]{1,0:T(8,128)S(1)} %convolution_add_fusion), kind=kLoop, calls=%fused_computation.37 | loop fusion | flops 51904512 | bytes 11010048 | tf_op jit(solution)/shard_map/convert_element_type | solution.py:176
  260.8 33.7 %all-gather.14.cloned.1.call-done = bf16[1536,768]{0,1:T(8,128)(2,1)} async-done(((bf16[1536,192]{0,1:T(8,128)(2,1)}), bf16[1536,768]{0,1:T(8,128)(2,1)}) %all-gather.14.cloned.1.call-update) | async-done | bytes 2359312 | tf_op jit(solution)/shard_map/all_gather | solution.py:102
  294.5 4.0 convolution_convert_fusion.4
  299.0 17.7 %all-reduce.12.cloned.1.call-done = bf16[512,768]{1,0:T(8,128)(2,1)} async-done(((bf16[512,768]{1,0:T(8,128)(2,1)}), bf16[512,768]{1,0:T(8,128)(2,1)}) %all-reduce.12.cloned.1.call-update) | async-done | bytes 786448 | tf_op jit(solution)/shard_map/psum | solution.py:178
  324.2 4.9 add_convert_fusion
  330.8 3.5 convolution_convert_fusion.3
  334.4 6.8 convolution_convert_fusion
  341.2 11.7 %convert_element_type.344 = bf16[768,2,1536]{2,1,0:T(2,128)(2,1)} reshape(bf16[768,3072]{1,0:T(8,128)(2,1)} %convolution_convert_fusion) | data formatting | bytes 9437184 | tf_op jit(solution)/shard_map/convert_element_type | solution.py:316
  368.2 4.4 convolution_convert_fusion.1
  377.3 132.0 %while.24 = (s32[]{:T(128)}, bf16[4,128,384]{1,2,0:T(8,128)(2,1)}, bf16[4,128,384]{1,2,0:T(8,128)(2,1)}, f32[4,128,384]{1,2,0:T(8,128)S(1)}, f32[4,128,384]{1,2,...) while((s32[]{:T(128)}, bf16[4,128,384]{1,2,0:T(8,128)(2,1)}, ...), condition=%wide.region_15.16_spmd.clone, body=%wide.region_14.15_spmd.clone.sunk | while | flops 257774864 | bytes 31414444 | solution.py:271
  392.0 5.4 collective-permute-done.2
  398.4 7.4 collective-permute-done.3
  406.9 7.4 collective-permute-done
  414.2 7.8 %collective-permute-done.1 = bf16[4,128,384]{1,2,0:T(8,128)(2,1)} collective-permute-done((bf16[4,128,384]{1,2,0:T(8,128)(2,1)S(1)}, bf16[4,128,384]{1,2,0:T(8,128)(2,1)}, u32[]{:S(2)}, u32[]{:S(2)}) %collective-permute-start.1) | collective-permute-done | bytes 393248 | tf_op jit(solution)/shard_map/while/body/eval_jaxpr/ppermute | solution.py:15
  435.2 2.7 fusion.136
  437.9 4.4 collective-permute-done.2
  443.4 7.4 collective-permute-done.3
  451.8 7.3 collective-permute-done
  459.2 6.9 collective-permute-done.1
  474.3 3.2 collective-permute-start.3
  479.3 2.7 fusion.136
  482.0 4.4 collective-permute-done.2
  487.4 7.4 collective-permute-done.3
  495.9 7.4 collective-permute-done
  503.2 6.0 collective-permute-done.1
  523.1 3.3 collective-permute-start.5
  528.5 4.2 collective-permute-done.4
  533.8 3.8 collective-permute-done.5
  540.2 3.8 copy.95
  544.1 3.6 convolution_convert_fusion.5
  549.1 3.1 constant_dynamic-slice_fusion
  553.8 49.4 %reduce-scatter.8.cloned.1.call-done = bf16[1536,192]{0,1:T(8,128)(2,1)} async-done(((bf16[1536,768]{0,1:T(8,128)(2,1)}), bf16[1536,192]{0,1:T(8,128)(2,1)}) %reduce-scatter.8.cloned.1.call-update) | async-done | bytes 589840 | tf_op jit(solution)/shard_map/reduce_scatter | solution.py:318
  603.2 40.2 %reduce-scatter.4.cloned.1.call-done = bf16[192,3,384]{2,0,1:T(8,128)(2,1)} async-done(((bf16[768,3,384]{2,0,1:T(8,128)(2,1)}), bf16[192,3,384]{2,0,1:T(8,128)(2,1)}) %reduce-scatter.4.cloned.1.call-update) | async-done | bytes 442384 | tf_op jit(solution)/shard_map/reduce_scatter | solution.py:309
  647.7 76.8 %all-reduce.1 = (f32[2,384]{1,0:T(2,128)}, f32[768]{0:T(1024)}, f32[768]{0:T(1024)}, f32[768]{0:T(1024)}, f32[2,1536]{1,0:T(2,128)}, /*index=5*/f32[768]{0:T(1024)}, f32[768]{0:T(1024)}, f32[768]{0:T(1024)}) all-reduce(f32[2,384]{1,0:T(2,128)S(1)} %pad_maximum_fusion.6, ...), channel_id=1, replica_groups=mesh['dp'=4,'blk'=4,'head'=2] {'dp','blk'}, use_global_device_ids=true, to_apply=%region_21.22 | all-reduce | flops 8448 | bytes 67584 | tf_op jit(solution)/shard_map/psum | solution.py:328
  726.9 18.4 %all-reduce.20.cloned.1.call-done = (bf16[192,3,384]{2,0,1:T(8,128)(2,1)}, bf16[384,192]{0,1:T(8,128)(2,1)}, bf16[192,2,1536]{2,1,0:T(2,128)(2,1)}, bf16[1536,192]{0,1:T(8,128)(2,1)}) async-done(((bf16[192,3,384]{2,0,1:T(8,128)(2,1)}, bf16[384,192]{0,1:T(8,128)(2,1)}, bf16[192,2,1536]{2,1,0:T(2,128)(2,1)}, bf16[1536,192]{0,1:T(8,128)(2,1)}), (bf16[192,3,384]{2,0,1:T(8,128)(2,1)}, ...) | async-done | bytes 2359312 | tf_op jit(solution)/shard_map/psum | solution.py:323
  745.3 3.5 convert_element_type.345
  (384 shorter events, 127.9 us)
Async XLA Ops:
  7.2 45.5 %all-gather.6.cloned.1.call-start = ((), (), s32[]{:S(2)}) async-start(), calls=%async_computation.3 | async-start | bytes 2211840 | tf_op jit(solution)/shard_map/all_gather | solution.py:99
  7.9 47.4 %copy-start.23 = (bf16[4,128,768]{2,1,0:T(8,128)(2,1)S(1)}, bf16[4,128,768]{2,1,0:T(8,128)(2,1)}, u32[]{:S(2)}) copy-start(bf16[4,128,768]{2,1,0:T(8,128)(2,1)} %param.18) | copy-start | bytes 2359300
  7.9 80.2 %all-gather.8.cloned.1.call-start = ((), (), s32[]{:S(2)}) async-start(), calls=%async_computation.4 | async-start | bytes 1966080 | tf_op jit(solution)/shard_map/all_gather | solution.py:158
  58.1 62.9 %all-gather.10.cloned.1.call-start = ((), (), s32[]{:S(2)}) async-start(), calls=%async_computation.5 | async-start | bytes 1966080 | tf_op jit(solution)/shard_map/all_gather | solution.py:159
  58.3 306.3 %copy-start.43 = (s32[128]{0:T(128)}, s32[128]{0:T(128)S(1)}, u32[]{:S(2)}) copy-start(s32[128]{0:T(128)S(1)} %get-tuple-element.713) | copy-start | bytes 1540
  62.3 89.7 %all-reduce.10.cloned.1.call-start = ((), (), s32[]{:S(2)}) async-start(), calls=%async_computation.6 | async-start | bytes 1572864 | tf_op jit(solution)/shard_map/psum | solution.py:167
  80.8 285.5 %copy-start.10 = (bf16[4,128,6,64]{1,0,3,2:T(4,128)(2,1)}, bf16[4,128,6,64]{1,0,3,2:T(4,128)(2,1)S(1)}, u32[]{:S(2)}) copy-start(bf16[4,128,6,64]{1,0,3,2:T(4,128)(2,1)S(1)} %reshape_reshape.10) | copy-start | bytes 1179652
  95.2 28.4 %copy-start.30 = (pred[4,128,512]{2,1,0:T(8,128)(4,1)S(1)}, pred[4,128,512]{2,1,0:T(8,128)(4,1)}, u32[]{:S(2)}) copy-start(pred[4,128,512]{2,1,0:T(8,128)(4,1)} %broadcast_compare_fusion.1) | copy-start | bytes 786436
  132.6 111.5 %all-gather.12.cloned.1.call-start = ((), (), s32[]{:S(2)}) async-start(), calls=%async_computation.7 | async-start | bytes 5898240 | tf_op jit(solution)/shard_map/all_gather | solution.py:101
  133.2 161.4 %all-gather.14.cloned.1.call-start = ((), (), s32[]{:S(2)}) async-start(), calls=%async_computation.8 | async-start | bytes 2949120 | tf_op jit(solution)/shard_map/all_gather | solution.py:102
  133.7 183.0 %all-reduce.12.cloned.1.call-start = ((), (), s32[]{:S(2)}) async-start(), calls=%async_computation.9 | async-start | bytes 1572864 | tf_op jit(solution)/shard_map/psum | solution.py:178
  154.0 90.1 %copy-start.61 = (f32[512]{0:T(512)}, f32[512]{0:T(512)S(1)}, u32[]{:S(2)}) copy-start(f32[512]{0:T(512)S(1)} %get-tuple-element.568) | copy-start | bytes 6148
  260.8 37.7 %copy-start.37 = (bf16[512,1536]{1,0:T(8,128)(2,1)}, bf16[512,1536]{1,0:T(8,128)(2,1)S(1)}, u32[]{:S(2)}) copy-start(bf16[512,1536]{1,0:T(8,128)(2,1)S(1)} %get-tuple-element.566) | copy-start | bytes 4718596
  298.5 56.4 %all-reduce.14.cloned.1.call-start = ((), (), s32[]{:S(2)}) async-start(), calls=%async_computation.10 | async-start | bytes 1572864 | tf_op jit(solution)/shard_map/psum | solution.py:200
  334.3 214.7 %all-reduce.18.cloned.1.call-start = ((), (), s32[]{:S(2)}) async-start(), calls=%async_computation.15 | async-start | bytes 9437184
  352.9 200.9 %reduce-scatter.6.cloned.1.call-start = ((), (), s32[]{:S(2)}) async-start(), calls=%async_computation.13 | async-start | bytes 737280 | tf_op jit(solution)/shard_map/reduce_scatter | solution.py:312
  363.3 240.0 %reduce-scatter.8.cloned.1.call-start = ((), (), s32[]{:S(2)}) async-start(), calls=%async_computation.14 | async-start | bytes 2949120 | tf_op jit(solution)/shard_map/reduce_scatter | solution.py:318
  372.7 270.7 %reduce-scatter.4.cloned.1.call-start = ((), (), s32[]{:S(2)}) async-start(), calls=%async_computation.12 | async-start | bytes 2211840 | tf_op jit(solution)/shard_map/reduce_scatter | solution.py:309
  384.2 13.2 %collective-permute-start.2 = (bf16[4,128,384]{1,2,0:T(8,128)(2,1)}, bf16[4,128,384]{1,2,0:T(8,128)(2,1)}, u32[]{:S(2)}, u32[]{:S(2)}) collective-permute-start(bf16[4,128,384]{1,2,0:T(8,128)(2,1)} %fusion.133), channel_id=1, source_target_pairs={{0,2},{2,4},{4,6},{6,0},{1,3},{3,5},{5,7},{7,1},{8,10},{10,12},{12... | collective-permute-start | bytes 1179656 | tf_op jit(solution)/shard_map/while/body/eval_jaxpr/ppermute | solution.py:15
  387.2 18.6 %collective-permute-start.3 = (bf16[4,128,384]{1,2,0:T(8,128)(2,1)}, bf16[4,128,384]{1,2,0:T(8,128)(2,1)}, u32[]{:S(2)}, u32[]{:S(2)}) collective-permute-start(bf16[4,128,384]{1,2,0:T(8,128)(2,1)} %fusion.135), channel_id=1, source_target_pairs={{0,2},{2,4},{4,6},{6,0},{1,3},{3,5},{5,7},{7,1},{8,10},{10,12},{12... | collective-permute-start | bytes 1179656 | tf_op jit(solution)/shard_map/while/body/eval_jaxpr/ppermute | solution.py:15
  388.7 25.6 %collective-permute-start = (bf16[4,128,384]{1,2,0:T(8,128)(2,1)S(1)}, bf16[4,128,384]{1,2,0:T(8,128)(2,1)}, u32[]{:S(2)}, u32[]{:S(2)}) collective-permute-start(bf16[4,128,384]{1,2,0:T(8,128)(2,1)S(1)} %copy.137), channel_id=1, source_target_pairs={{0,2},{2,4},{4,6},{6,0},{1,3},{3,5},{5,7},{7,1},{8,10},{10,12},{12... | collective-permute-start | bytes 1179656 | tf_op jit(solution)/shard_map/while/body/eval_jaxpr/ppermute | solution.py:15
  390.1 31.9 %collective-permute-start.1 = (bf16[4,128,384]{1,2,0:T(8,128)(2,1)S(1)}, bf16[4,128,384]{1,2,0:T(8,128)(2,1)}, u32[]{:S(2)}, u32[]{:S(2)}) collective-permute-start(bf16[4,128,384]{1,2,0:T(8,128)(2,1)S(1)} %copy.138), channel_id=1, source_target_pairs={{0,2},{2,4},{4,6},{6,0},{1,3},{3,5},{5,7},{7,1},{8,10},{10,12},{12... | collective-permute-start | bytes 1179656 | tf_op jit(solution)/shard_map/while/body/eval_jaxpr/ppermute | solution.py:15
  391.9 30.1 %copy-start.5 = (bf16[4,128,6,64]{1,3,2,0:T(8,128)(2,1)S(1)}, bf16[4,128,6,64]{1,3,2,0:T(8,128)(2,1)}, u32[]{:S(2)}) copy-start(bf16[4,128,6,64]{1,3,2,0:T(8,128)(2,1)} %copy-done.4) | copy-start | bytes 1179652 | tf_op jit(solution)/shard_map/while
  391.9 30.1 %copy-start.45 = (s32[128]{0:T(128)S(1)}, s32[128]{0:T(128)}, u32[]{:S(2)}) copy-start(s32[128]{0:T(128)} %get-tuple-element.862) | copy-start | bytes 1540 | tf_op jit(solution)/shard_map/while
  391.9 30.1 %copy-start.49 = (s32[4]{0:T(128)S(1)}, s32[4]{0:T(128)}, u32[]{:S(2)}) copy-start(s32[4]{0:T(128)} %get-tuple-element.887) | copy-start | bytes 52 | tf_op jit(solution)/shard_map/while
  391.9 30.2 %copy-start.52 = (s32[4]{0:T(128)S(1)}, s32[4]{0:T(128)}, u32[]{:S(2)}) copy-start(s32[4]{0:T(128)} %get-tuple-element.913) | copy-start | bytes 52 | tf_op jit(solution)/shard_map/while
  391.9 30.2 %copy-start.56 = (f32[6]{0:T(128)S(1)}, f32[6]{0:T(128)}, u32[]{:S(2)}) copy-start(f32[6]{0:T(128)} %get-tuple-element.940) | copy-start | bytes 76 | tf_op jit(solution)/shard_map/while
  391.9 30.2 %copy-start.63 = (s32[4,1]{0,1:T(1,128)S(1)}, s32[4,1]{0,1:T(1,128)}, u32[]{:S(2)}) copy-start(s32[4,1]{0,1:T(1,128)} %get-tuple-element.968) | copy-start | bytes 52 | tf_op jit(solution)/shard_map/while
  392.0 30.2 %copy-start.67 = (f32[4,6,128]{2,1,0:T(8,128)S(1)}, f32[4,6,128]{2,1,0:T(8,128)}, u32[]{:S(2)}) copy-start(f32[4,6,128]{2,1,0:T(8,128)} %get-tuple-element.997) | copy-start | bytes 36868 | tf_op jit(solution)/shard_map/while
  429.1 13.3 %collective-permute-start.2 = (bf16[4,128,384]{1,2,0:T(8,128)(2,1)}, bf16[4,128,384]{1,2,0:T(8,128)(2,1)}, u32[]{:S(2)}, u32[]{:S(2)}) collective-permute-start(bf16[4,128,384]{1,2,0:T(8,128)(2,1)} %fusion.133), channel_id=1, source_target_pairs={{0,2},{2,4},{4,6},{6,0},{1,3},{3,5},{5,7},{7,1},{8,10},{10,12},{12... | collective-permute-start | bytes 1179656 | tf_op jit(solution)/shard_map/while/body/eval_jaxpr/ppermute | solution.py:15
  431.1 19.6 %collective-permute-start.3 = (bf16[4,128,384]{1,2,0:T(8,128)(2,1)}, bf16[4,128,384]{1,2,0:T(8,128)(2,1)}, u32[]{:S(2)}, u32[]{:S(2)}) collective-permute-start(bf16[4,128,384]{1,2,0:T(8,128)(2,1)} %fusion.135), channel_id=1, source_target_pairs={{0,2},{2,4},{4,6},{6,0},{1,3},{3,5},{5,7},{7,1},{8,10},{10,12},{12... | collective-permute-start | bytes 1179656 | tf_op jit(solution)/shard_map/while/body/eval_jaxpr/ppermute | solution.py:15
  433.5 25.7 %collective-permute-start = (bf16[4,128,384]{1,2,0:T(8,128)(2,1)S(1)}, bf16[4,128,384]{1,2,0:T(8,128)(2,1)}, u32[]{:S(2)}, u32[]{:S(2)}) collective-permute-start(bf16[4,128,384]{1,2,0:T(8,128)(2,1)S(1)} %copy.137), channel_id=1, source_target_pairs={{0,2},{2,4},{4,6},{6,0},{1,3},{3,5},{5,7},{7,1},{8,10},{10,12},{12... | collective-permute-start | bytes 1179656 | tf_op jit(solution)/shard_map/while/body/eval_jaxpr/ppermute | solution.py:15
  434.0 32.0 %collective-permute-start.1 = (bf16[4,128,384]{1,2,0:T(8,128)(2,1)S(1)}, bf16[4,128,384]{1,2,0:T(8,128)(2,1)}, u32[]{:S(2)}, u32[]{:S(2)}) collective-permute-start(bf16[4,128,384]{1,2,0:T(8,128)(2,1)S(1)} %copy.138), channel_id=1, source_target_pairs={{0,2},{2,4},{4,6},{6,0},{1,3},{3,5},{5,7},{7,1},{8,10},{10,12},{12... | collective-permute-start | bytes 1179656 | tf_op jit(solution)/shard_map/while/body/eval_jaxpr/ppermute | solution.py:15
  437.9 28.2 %copy-start.56 = (f32[6]{0:T(128)S(1)}, f32[6]{0:T(128)}, u32[]{:S(2)}) copy-start(f32[6]{0:T(128)} %get-tuple-element.940) | copy-start | bytes 76 | tf_op jit(solution)/shard_map/while
  437.9 28.2 %copy-start.63 = (s32[4,1]{0,1:T(1,128)S(1)}, s32[4,1]{0,1:T(1,128)}, u32[]{:S(2)}) copy-start(s32[4,1]{0,1:T(1,128)} %get-tuple-element.968) | copy-start | bytes 52 | tf_op jit(solution)/shard_map/while
  437.9 28.2 %copy-start.67 = (f32[4,6,128]{2,1,0:T(8,128)S(1)}, f32[4,6,128]{2,1,0:T(8,128)}, u32[]{:S(2)}) copy-start(f32[4,6,128]{2,1,0:T(8,128)} %get-tuple-element.997) | copy-start | bytes 36868 | tf_op jit(solution)/shard_map/while
  473.1 13.3 %collective-permute-start.2 = (bf16[4,128,384]{1,2,0:T(8,128)(2,1)}, bf16[4,128,384]{1,2,0:T(8,128)(2,1)}, u32[]{:S(2)}, u32[]{:S(2)}) collective-permute-start(bf16[4,128,384]{1,2,0:T(8,128)(2,1)} %fusion.133), channel_id=1, source_target_pairs={{0,2},{2,4},{4,6},{6,0},{1,3},{3,5},{5,7},{7,1},{8,10},{10,12},{12... | collective-permute-start | bytes 1179656 | tf_op jit(solution)/shard_map/while/body/eval_jaxpr/ppermute | solution.py:15
  474.3 20.5 %collective-permute-start.3 = (bf16[4,128,384]{1,2,0:T(8,128)(2,1)}, bf16[4,128,384]{1,2,0:T(8,128)(2,1)}, u32[]{:S(2)}, u32[]{:S(2)}) collective-permute-start(bf16[4,128,384]{1,2,0:T(8,128)(2,1)} %fusion.135), channel_id=1, source_target_pairs={{0,2},{2,4},{4,6},{6,0},{1,3},{3,5},{5,7},{7,1},{8,10},{10,12},{12... | collective-permute-start | bytes 1179656 | tf_op jit(solution)/shard_map/while/body/eval_jaxpr/ppermute | solution.py:15
  477.5 25.7 %collective-permute-start = (bf16[4,128,384]{1,2,0:T(8,128)(2,1)S(1)}, bf16[4,128,384]{1,2,0:T(8,128)(2,1)}, u32[]{:S(2)}, u32[]{:S(2)}) collective-permute-start(bf16[4,128,384]{1,2,0:T(8,128)(2,1)S(1)} %copy.137), channel_id=1, source_target_pairs={{0,2},{2,4},{4,6},{6,0},{1,3},{3,5},{5,7},{7,1},{8,10},{10,12},{12... | collective-permute-start | bytes 1179656 | tf_op jit(solution)/shard_map/while/body/eval_jaxpr/ppermute | solution.py:15
  477.5 31.7 %collective-permute-start.1 = (bf16[4,128,384]{1,2,0:T(8,128)(2,1)S(1)}, bf16[4,128,384]{1,2,0:T(8,128)(2,1)}, u32[]{:S(2)}, u32[]{:S(2)}) collective-permute-start(bf16[4,128,384]{1,2,0:T(8,128)(2,1)S(1)} %copy.138), channel_id=1, source_target_pairs={{0,2},{2,4},{4,6},{6,0},{1,3},{3,5},{5,7},{7,1},{8,10},{10,12},{12... | collective-permute-start | bytes 1179656 | tf_op jit(solution)/shard_map/while/body/eval_jaxpr/ppermute | solution.py:15
  519.4 13.3 %collective-permute-start.4 = (bf16[4,128,384]{2,1,0:T(8,128)(2,1)}, bf16[4,128,384]{2,1,0:T(8,128)(2,1)}, u32[]{:S(2)}, u32[]{:S(2)}) collective-permute-start(bf16[4,128,384]{2,1,0:T(8,128)(2,1)} %add_convert_fusion.5), channel_id=1, source_target_pairs={{0,2},{2,4},{4,6},{6,0},{1,3},{3,5},{5,7},{7,1},{8,10},{10,12},{12... | collective-permute-start | bytes 1179656 | tf_op jit(solution)/shard_map/ppermute | solution.py:15
  523.1 14.5 %collective-permute-start.5 = (bf16[4,128,384]{2,1,0:T(8,128)(2,1)}, bf16[4,128,384]{2,1,0:T(8,128)(2,1)S(1)}, u32[]{:S(2)}, u32[]{:S(2)}) collective-permute-start(bf16[4,128,384]{2,1,0:T(8,128)(2,1)} %add_convert_fusion.4), channel_id=1, source_target_pairs={{0,2},{2,4},{4,6},{6,0},{1,3},{3,5},{5,7},{7,1},{8,10},{10,12},{12... | collective-permute-start | bytes 1179656 | tf_op jit(solution)/shard_map/ppermute | solution.py:15
  544.0 180.4 %all-reduce.16.cloned.1.call-start = ((), (), s32[]{:S(2)}) async-start(), calls=%async_computation.11 | async-start | bytes 1572864 | tf_op jit(solution)/shard_map/psum | solution.py:305
  547.7 197.6 %all-reduce.20.cloned.1.call-start = ((), (), s32[]{:S(2)}) async-start(), calls=%async_computation.16 | async-start | bytes 4718592 | tf_op jit(solution)/shard_map/psum | solution.py:323
  552.1 91.3 %copy-start.9 = (bf16[4,128,768]{2,1,0:T(8,128)(2,1)S(1)}, bf16[4,128,768]{2,1,0:T(8,128)(2,1)}, u32[]{:S(2)}) copy-start(bf16[4,128,768]{2,1,0:T(8,128)(2,1)} %param.33) | copy-start | bytes 2359300
  552.2 92.1 %copy-start.34 = (bf16[512,1536]{1,0:T(8,128)(2,1)S(1)}, bf16[512,1536]{1,0:T(8,128)(2,1)}, u32[]{:S(2)}) copy-start(bf16[512,1536]{1,0:T(8,128)(2,1)} %copy-done.33) | copy-start | bytes 4718596
  644.2 80.2 %copy-start.3 = (f32[512,768]{1,0:T(8,128)S(1)}, f32[512,768]{1,0:T(8,128)}, u32[]{:S(2)}) copy-start(f32[512,768]{1,0:T(8,128)} %copy-done.2) | copy-start | bytes 4718596
  644.2 80.2 %copy-start.58 = (f32[512]{0:T(512)S(1)}, f32[512]{0:T(512)}, u32[]{:S(2)}) copy-start(f32[512]{0:T(512)} %copy-done.57) | copy-start | bytes 6148
  (79 other events, 649.2 us)
Sparse Core Ops, SparseCore 0:
  9.6 43.0 all-gather.5
  58.2 29.8 all-gather.7
  90.0 30.9 all-gather.9
  132.7 19.1 all-reduce.9
  153.4 90.5 all-gather.11
  245.6 48.9 all-gather.13
  298.6 18.0 all-reduce.11
  334.5 20.3 all-reduce.13
  357.4 173.1 all-reduce.17
  532.8 20.9 reduce-scatter.5
  556.8 46.3 reduce-scatter.7
  605.5 37.8 reduce-scatter.3
  646.4 18.3 all-reduce.15
  668.9 76.4 all-reduce.19
where the time goes:
time: 767 us; the launch traced here: 758 us
  waiting for transfers between devices  436 us (57%)
  blocking collectives  93.7 us (12%)
  matrix products  71 us (9%)
  other arithmetic  61.2 us (8%)
  local copies, waits for them, and re-layouts  60.4 us (8%)
  starting transfers between devices  19.5 us (3%)
  between operations  15.7 us (2%)
    all_gather x1, waiting for transfers between devices, local(): lax.all_gather(expand_weight, 'dp', axis=0, tiled=True)  90.1 us
    ppermute x14, waiting for transfers between devices, shifted(): return lax.ppermute(value, axis, pairs)  87.1 us
    psum x1, blocking collectives, local(): lax.psum((project_bias_grad, output_bias_grad, first_gain_grad, first_shi...  76.8 us
    reduce_scatter x1, waiting for transfers between devices, local(): lax.psum_scatter(down_part.astype(jnp.bfloat16), 'dp', scatter_dimension=...  49.4 us
    all_gather x1, waiting for transfers between devices, local(): lax.all_gather(project_weight, 'dp', axis=0, tiled=True)  44.7 us
    reduce_scatter x1, waiting for transfers between devices, local(): lax.psum_scatter(project_part.astype(jnp.bfloat16), 'dp', scatter_dimensi...  40.2 us
    all_gather x1, waiting for transfers between devices, local(): lax.all_gather(down_weight, 'dp', axis=1, tiled=True)  33.7 us
    all_gather x1, waiting for transfers between devices, local(): lax.all_gather(values, 'blk', axis=1, tiled=True)  25.2 us
  transfers between devices with their start and end apart: 28, of which 26 were waited for; matrix products, arithmetic and copies ran while one was open for 19% of the time, Pallas kernels for 0%

commit v1 on v0

--- a/solution.py
+++ b/solution.py
@@ -3,6 +3,8 @@
 import jax
 import jax.numpy as jnp
 from jax import lax
+from jax.experimental import pallas as pl
+from jax.experimental.pallas import tpu as pltpu
 from jax.sharding import PartitionSpec as P
 
 EPSILON = 1e-12
@@ -70,7 +72,7 @@
     return lax.fori_loop(0, count_rows // block, step, state)
 
 
-def local(
+def general(
     layer_input,
     sequence_lengths,
     alibi_slopes,
@@ -356,6 +358,872 @@
     )
 
 
+MESH = pl.DeviceIdType.MESH
+BF = jnp.bfloat16
+F32 = jnp.float32
+FAR = 1e33
+VMEM_BYTES = 63 << 20
+
+
+def dot(a, b):
+    return lax.dot_general(a, b, (((1,), (0,)), ((), ())), preferred_element_type=F32)
+
+
+def dot_nt(a, b):
+    return lax.dot_general(a, b, (((1,), (1,)), ((), ())), preferred_element_type=F32)
+
+
+def dot_tn(a, b):
+    return lax.dot_general(a, b, (((0,), (0,)), ((), ())), preferred_element_type=F32)
+
+
+def column_sum(rows):
+    return jnp.sum(rows, axis=0, keepdims=True)
+
+
+def row_mean(rows):
+    return jnp.mean(rows, axis=-1, keepdims=True)
+
+
+def standardize(rows):
+    centered = rows - row_mean(rows)
+    inverse = lax.rsqrt(row_mean(centered * centered) + EPSILON)
+    return centered * inverse, inverse
+
+
+def standardize_back(grad, normal, inverse):
+    return inverse * (grad - row_mean(grad) - normal * row_mean(grad * normal))
+
+
+def layer_kernel(
+    x_ref, cot_ref, wa_ref, wf_ref, pack_ref, len_ref,
+    out_ref, ig_ref, ga_ref, gf_ref, sm_ref,
+    x_full, first_full, feed_full, branch_full,
+    w_attn, w_gu, w_down, packs,
+    part, r1x, r1y, r2,
+    q_s, k_s, v_s, g_s, p_s, ctx_s, ctx_cat, dqkv, ds_s, dq_s, far_s,
+    act_s, upd_s, hid_s, dgu_s, eb_acc,
+    first_own, n1_s, a1_s, gr2_s, gr1_s,
+    dwf, dwf_in, zf_in, dwa, dwa_in, zf_a, fin_a,
+    sm_acc, sm_in, slope_s,
+    ag_ss, ag_rs, rs_ss, rs_rs, pk_sem, wa_ss, wa_rs, wf_ss, wf_rs, wl_sem, wc_ss, wc_rs,
+    gc_ss, gc_rs, gz_ss, gz_rs, gp_ss, gp_rs, sm_ss, sm_rs, io_ss, io_rs,
+):
+    z, b, c = lax.axis_index("dp"), lax.axis_index("blk"), lax.axis_index("head")
+    half, odd = b // 2, b % 2
+    xor = jnp.bitwise_xor
+    other = 1 - c
+    sib = (z, b, other)
+    xdev, ydev, ddev = ((z, xor(b, k), c) for k in (1, 2, 3))
+    bx, by, bd = xor(b, 1), xor(b, 2), xor(b, 3)
+    T = x_ref.shape[1]
+    D = x_ref.shape[2]
+    H2 = D // 2
+    ROWS = 4 * T
+    DZ = wa_ref.shape[1]
+    UB = wf_ref.shape[2] // 4
+
+    def remote(src, dst, ss, rs, dev):
+        return pltpu.make_async_remote_copy(
+            src_ref=src, dst_ref=dst, send_sem=ss, recv_sem=rs, device_id=dev, device_id_type=MESH
+        )
+
+    def chunk(index, size):
+        return pl.ds(pl.multiple_of(index * size, size), size)
+
+    partners = [(z, xor(b, k), cc) for k in (1, 2, 3) for cc in (c, other)] + [sib]
+    partners += [(xor(z, k), b, cc) for k in (1, 2, 3) for cc in (c, other)]
+    barrier = pltpu.get_barrier_semaphore()
+    for dev in partners:
+        pl.semaphore_signal(barrier, inc=1, device_id=dev, device_id_type=MESH)
+    pl.semaphore_wait(barrier, len(partners))
+
+    class Gather:
+        def __init__(self, full, phase, m):
+            ss, rs = ag_ss.at[phase, m], ag_rs.at[phase, m]
+            own, sx, sy = m * 4 + b, m * 4 + bx, m * 4 + by
+            lo, hi = pl.ds(0, H2), pl.ds(H2, H2)
+            self.cx = remote(full.at[own], full.at[own], ss.at[0], rs.at[0], xdev)
+            self.cy = remote(full.at[own], full.at[own], ss.at[1], rs.at[1], ydev)
+            self.fx = remote(full.at[sx, :, lo], full.at[sx, :, lo], ss.at[2], rs.at[2], ydev)
+            self.fy = remote(full.at[sy, :, hi], full.at[sy, :, hi], ss.at[3], rs.at[3], xdev)
+
+        def start(self):
+            self.cx.start()
+            self.cy.start()
+
+        def mid(self):
+            self.cx.wait_recv()
+            self.fx.start()
+            self.cy.wait_recv()
+            self.fy.start()
+
+        def end(self):
+            self.fx.wait_recv()
+            self.fy.wait_recv()
+
+        def drain(self):
+            for copy in (self.cx, self.cy, self.fx, self.fy):
+                copy.wait_send()
+
+    class Scatter:
+        def __init__(self, phase, m):
+            ss, rs = rs_ss.at[phase, m], rs_rs.at[phase, m]
+            buf = part.at[phase % 2]
+            lo, hi = pl.ds(0, H2), pl.ds(H2, H2)
+            self.phase, self.m, self.buf = phase, m, buf
+            own, sx, sy, sd = m * 4 + b, m * 4 + bx, m * 4 + by, m * 4 + bd
+            self.own, self.sx, self.sy = own, sx, sy
+            ix, iy, i2 = r1x.at[phase, m], r1y.at[phase, m], r2.at[phase, m]
+            self.ix, self.iy, self.i2 = ix, iy, i2
+            self.xd = remote(buf.at[sd, :, lo], ix.at[1], ss.at[0], rs.at[0], xdev)
+            self.yd = remote(buf.at[sd, :, hi], iy.at[1], ss.at[1], rs.at[1], ydev)
+            self.xo = remote(buf.at[sx, :, lo], ix.at[0], ss.at[2], rs.at[2], xdev)
+            self.yo = remote(buf.at[sy, :, hi], iy.at[0], ss.at[3], rs.at[3], ydev)
+            self.y2 = remote(buf.at[sy, :, lo], i2.at[0], ss.at[4], rs.at[4], ydev)
+            self.x2 = remote(buf.at[sx, :, hi], i2.at[1], ss.at[5], rs.at[5], xdev)
+
+        def start(self):
+            for copy in (self.xd, self.yd, self.xo, self.yo):
+                copy.start()
+
+        def mid(self):
+            buf = self.buf
+            self.xd.wait_recv()
+            buf[self.sy, :, :H2] = (
+                buf[self.sy, :, :H2].astype(F32) + self.ix[1].astype(F32)
+            ).astype(BF)
+            self.y2.start()
+            self.yd.wait_recv()
+            buf[self.sx, :, H2:] = (
+                buf[self.sx, :, H2:].astype(F32) + self.iy[1].astype(F32)
+            ).astype(BF)
+            self.x2.start()
+
+        def end(self):
+            for copy in (self.xo, self.yo, self.y2, self.x2):
+                copy.wait_recv()
+            mine = self.buf[self.own].astype(F32)
+            low = mine[:, :H2] + self.ix[0].astype(F32) + self.i2[0].astype(F32)
+            high = mine[:, H2:] + self.iy[0].astype(F32) + self.i2[1].astype(F32)
+            return jnp.concatenate([low, high], axis=1)
+
+        def drain(self):
+            for copy in (self.xd, self.yd, self.xo, self.yo, self.y2, self.x2):
+                copy.wait_send()
+
+    gather_x = [Gather(x_full, 0, m) for m in (0, 1)]
+    gather_first = [Gather(first_full, 1, m) for m in (0, 1)]
+    gather_feed = [Gather(feed_full, 2, m) for m in (0, 1)]
+    gather_branch = [Gather(branch_full, 3, m) for m in (0, 1)]
+    sum_branch = [Scatter(0, m) for m in (0, 1)]
+    sum_feed = [Scatter(1, m) for m in (0, 1)]
+    sum_first = [Scatter(2, m) for m in (0, 1)]
+    sum_input = [Scatter(3, m) for m in (0, 1)]
+
+    for m in (0, 1):
+        x_full[m * 4 + b] = x_ref[2 * c + m]
+    gather_x[0].start()
+
+    mine_z = chunk(z, DZ)
+    attn_copies = []
+    for kind in range(4):
+        src = wa_ref.at[kind, :, pl.ds(pl.multiple_of(odd * 128, 128), 256)]
+        dst = w_attn.at[mine_z, pl.ds(kind * 256, 256)]
+        row = [
+            remote(src, dst, wa_ss.at[dz, kind], wa_rs.at[dz, kind], (xor(z, dz), b, kind // 2))
+            for dz in (1, 2, 3)
+        ]
+        cross = remote(src, dst, wa_ss.at[0, kind], wa_rs.at[0, kind], sib)
+        local = pltpu.make_async_copy(src, dst, wl_sem.at[kind])
+        attn_copies.append((row, cross, local))
+    pack_copy = remote(pack_ref, packs.at[c], pk_sem.at[0], pk_sem.at[1], sib)
+    pack_copy.start()
+    packs[c] = pack_ref[...]
+
+    @pl.when(c == half)
+    def _():
+        for kind in range(4):
+            row, cross, local = attn_copies[kind]
+            for copy in row:
+                copy.start()
+            for core in (0, 1):
+                if kind // 2 == core:
+
+                    @pl.when(c == core)
+                    def _():
+                        local.start()
+
+                    @pl.when(c != core)
+                    def _():
+                        cross.start()
+
+    gather_x[1].start()
+
+    ffn_copies = []
+    for kind in range(3):
+        src = wf_ref.at[kind, :, chunk(b, UB)]
+        if kind < 2:
+            dst = w_gu.at[c, mine_z, pl.ds(kind * UB, UB)]
+        else:
+            dst = w_down.at[mine_z, chunk(c, UB)]
+        row = [
+            remote(src, dst, wf_ss.at[dz, kind], wf_rs.at[dz, kind], (xor(z, dz), b, c))
+            for dz in (1, 2, 3)
+        ]
+        local = pltpu.make_async_copy(src, dst, wl_sem.at[4 + kind])
+        ffn_copies.append((row, local))
+        for copy in row:
+            copy.start()
+        local.start()
+
+    positions = lax.broadcasted_iota(jnp.int32, (ROWS, ROWS), 0)
+    key_positions = lax.broadcasted_iota(jnp.int32, (ROWS, ROWS), 1)
+    for m in (0, 1):
+        start_one = len_ref[(2 * c + m) * 3]
+        start_two = start_one + len_ref[(2 * c + m) * 3 + 1]
+        for rb in range(4):
+            rows = lax.broadcasted_iota(jnp.int32, (T, ROWS), 0) + rb * T
+            cols = lax.broadcasted_iota(jnp.int32, (T, ROWS), 1)
+            seq_r = (rows >= start_one).astype(jnp.int32) + (rows >= start_two).astype(jnp.int32)
+            seq_c = (cols >= start_one).astype(jnp.int32) + (cols >= start_two).astype(jnp.int32)
+            distance = jnp.abs(rows - cols).astype(F32)
+            far_s[m, pl.ds(rb * T, T), :] = jnp.where(seq_r == seq_c, distance, FAR)
+    sm_acc[...] = jnp.zeros_like(sm_acc)
+    eb_acc[...] = jnp.zeros_like(eb_acc)
+
+    gather_x[0].mid()
+    gather_x[1].mid()
+    pack_copy.wait_recv()
+
+    def small(row):
+        return packs[c, pl.ds(row, 1), pl.ds(0, D)]
+
+    for kind in range(4):
+        row, cross, local = attn_copies[kind]
+
+        @pl.when(c == kind // 2)
+        def _():
+            for copy in row:
+                copy.wait_recv()
+
+            @pl.when(c == half)
+            def _():
+                local.wait()
+
+            @pl.when(c != half)
+            def _():
+                cross.wait_recv()
+
+    pair = w_attn.at[:, chunk(c, 512)]
+    attn_share = remote(pair, pair, wc_ss.at[0], wc_rs.at[0], sib)
+    attn_share.start()
+    attn_share.wait_recv()
+
+    def pick(cols):
+        return [
+            jnp.where(odd == 0, cols[:, i * 64 : i * 64 + 64], cols[:, i * 64 + 64 : i * 64 + 128])
+            for i in range(3)
+        ]
+
+    def place(heads):
+        zero = jnp.zeros_like(heads[0])
+        return jnp.concatenate(
+            [
+                jnp.where(odd == 0, heads[0], zero),
+                jnp.where(odd == 0, heads[1], heads[0]),
+                jnp.where(odd == 0, heads[2], heads[1]),
+                jnp.where(odd == 0, zero, heads[2]),
+            ],
+            axis=1,
+        )
+
+    bias_cols = pl.ds(pl.multiple_of(odd * 128, 128), 256)
+
+    def project(m):
+        query_bias = packs[half, 2:3, bias_cols]
+        value_bias = packs[half, 3:4, bias_cols]
+
+        def rows_of(t, _):
+            rows = x_full[pl.ds(m * 4 + t * 2, 2)].reshape(2 * T, D)
+            at = pl.ds(pl.multiple_of(t * 2 * T, 2 * T), 2 * T)
+            mixed = dot(rows, w_attn[:, 0:768])
+            query = (mixed[:, 0:256] + query_bias).astype(BF) * jnp.asarray(0.125, BF)
+            keys = mixed[:, 256:512].astype(BF)
+            values = (mixed[:, 512:768] + value_bias).astype(BF)
+            for i, item in enumerate(pick(query)):
+                q_s[m * 3 + i, at, :] = item
+            for i, item in enumerate(pick(keys)):
+                k_s[m * 3 + i, at, :] = item
+            for i, item in enumerate(pick(values)):
+                v_s[m * 3 + i, at, :] = item
+            return 0
+
+        lax.fori_loop(0, 2, rows_of, 0)
+
+    for i in range(3):
+        low, high = packs[half, 10 + i : 11 + i, 0:128], packs[half, 13 + i : 14 + i, 0:128]
+        slope_s[i] = jnp.broadcast_to(jnp.where(odd == 0, low, high), (8, 128))
+
+    def slope_of(i):
+        return slope_s[i][0:1, 0:1]
+
+    def attend(m):
+        def one(index, _):
+            i, rb = index // 4, index % 4
+            at = chunk(rb, T)
+            h = m * 3 + i
+            scores = dot_nt(q_s[h, at, :], k_s[h])
+            scores = scores - slope_of(i) * far_s[m, at, :]
+            top = jnp.max(scores, axis=-1, keepdims=True)
+            weights = jnp.exp(scores - top)
+            total = jnp.sum(weights, axis=-1, keepdims=True)
+            probs = (weights * (1.0 / total)).astype(BF)
+            p_s[h, at, :] = probs
+            ctx_s[h, at, :] = dot(probs, v_s[h])
+            return 0
+
+        lax.fori_loop(0, 12, one, 0)
+
+    def put_part(buf, m, t, rows):
+        buf[pl.ds(m * 4 + 2 * t, 2)] = rows.astype(BF).reshape(2, T, D)
+
+    def branch(m):
+        def rows_of(t, _):
+            at = pl.ds(pl.multiple_of(t * 2 * T, 2 * T), 2 * T)
+            cat = place([ctx_s[m * 3 + i, at, :].astype(BF) for i in range(3)])
+            ctx_cat[m, at, :] = cat
+            put_part(sum_branch[m].buf, m, t, dot_nt(cat, w_attn[:, 768:1024]))
+            return 0
+
+        lax.fori_loop(0, 2, rows_of, 0)
+
+    def first_norm(m):
+        rows = x_ref[2 * c + m].astype(F32) + sum_branch[m].end() + small(4)
+        normal, inverse = standardize(rows)
+        first = normal * small(5) + small(6)
+        n1_s[m], a1_s[m] = normal, inverse
+        first_own[m] = first
+        first_full[m * 4 + b] = first.astype(BF)
+
+    def feed_forward(m):
+        def rows_of(t, _):
+            at = pl.ds(pl.multiple_of(m * ROWS + t * 2 * T, 2 * T), 2 * T)
+            rows = first_full[pl.ds(m * 4 + t * 2, 2)].reshape(2 * T, D)
+            for g in (0, 1):
+                cols = pl.ds(g * UB, UB)
+                bias = packs[g, 0:2, chunk(b, UB)]
+                both = dot(rows, w_gu[g])
+                gate = both[:, :UB] + bias[0:1]
+                up = both[:, UB:] + bias[1:2]
+                cdf = 0.5 + 0.5 * lax.erf(gate * 0.7071067811865476)
+                act = gate * cdf
+                slope = cdf + gate * (jnp.exp(-0.5 * gate * gate) * 0.3989422804014327)
+                hid_s[at, cols] = (act * up).astype(BF)
+                act_s[at, cols] = act.astype(BF)
+                upd_s[at, cols] = (up * slope).astype(BF)
+            put_part(sum_feed[m].buf, m, t, dot_nt(hid_s[at, :], w_down[...]))
+            return 0
+
+        lax.fori_loop(0, 2, rows_of, 0)
+
+    def add_small(row, rows):
+        sm_acc[row : row + 1, :] += column_sum(rows)
+
+    def second_norm(m):
+        rows = first_own[m] + sum_feed[m].end() + small(7)
+        normal, inverse = standardize(rows)
+        out_ref[2 * c + m] = (normal * small(8) + small(9)).astype(BF)
+        grad = cot_ref[2 * c + m].astype(F32)
+        add_small(4, grad * normal)
+        add_small(5, grad)
+        back = standardize_back(grad * small(8), normal, inverse)
+        gr2_s[m] = back
+        low = back.astype(BF)
+        feed_full[m * 4 + b] = low
+        add_small(3, low.astype(F32))
+
+    def feed_backward(m):
+        def rows_of(t, _):
+            at = pl.ds(pl.multiple_of(m * ROWS + t * 2 * T, 2 * T), 2 * T)
+            rows = feed_full[pl.ds(m * 4 + t * 2, 2)].reshape(2 * T, D)
+            hidden = dot(rows, w_down[...])
+            dgate = (hidden * upd_s[at, :].astype(F32)).astype(BF)
+            dup = (hidden * act_s[at, :].astype(F32)).astype(BF)
+            for g in (0, 1):
+                cols = slice(g * UB, g * UB + UB)
+                dgu_s[g, at, 0:UB] = dgate[:, cols]
+                dgu_s[g, at, UB : 2 * UB] = dup[:, cols]
+                eb_acc[2 * g : 2 * g + 1, :] += column_sum(dgate[:, cols].astype(F32))
+                eb_acc[2 * g + 1 : 2 * g + 2, :] += column_sum(dup[:, cols].astype(F32))
+            back = dot_nt(dgu_s[0, at, :], w_gu[0]) + dot_nt(dgu_s[1, at, :], w_gu[1])
+            put_part(sum_first[m].buf, m, t, back)
+            return 0
+
+        lax.fori_loop(0, 2, rows_of, 0)
+
+    def feed_weights():
+        def cols_of(t, _):
+            at = chunk(t, 256)
+            rows = first_full[:, :, at].reshape(2 * ROWS, 256)
+            for g in (0, 1):
+                dwf[g, at, 0 : 2 * UB] = dot_tn(rows, dgu_s[g]).astype(BF)
+            rows = feed_full[:, :, at].reshape(2 * ROWS, 256)
+            down = dot_tn(rows, hid_s[...]).astype(BF)
+            for g in (0, 1):
+                dwf[g, at, 2 * UB : 3 * UB] = down[:, g * UB : g * UB + UB]
+            return 0
+
+        lax.fori_loop(0, D // 256, cols_of, 0)
+
+    def first_back(m):
+        grad = gr2_s[m] + sum_first[m].end()
+        normal = n1_s[m]
+        add_small(1, grad * normal)
+        add_small(2, grad)
+        back = standardize_back(grad * small(5), normal, a1_s[m])
+        gr1_s[m] = back
+        low = back.astype(BF)
+        branch_full[m * 4 + b] = low
+        add_small(0, low.astype(F32))
+
+    def context_back(m):
+        def rows_of(t, _):
+            at = pl.ds(pl.multiple_of(t * 2 * T, 2 * T), 2 * T)
+            rows = branch_full[pl.ds(m * 4 + t * 2, 2)].reshape(2 * T, D)
+            grads = dot(rows, w_attn[:, 768:1024]).astype(BF)
+            for i, item in enumerate(pick(grads)):
+                g_s[m * 3 + i, at, :] = item
+            return 0
+
+        lax.fori_loop(0, 2, rows_of, 0)
+
+    def attend_back(m):
+        def one(i, _):
+            h = m * 3 + i
+            query, keys, values, grads = q_s[h], k_s[h], v_s[h], g_s[h]
+
+            def block(rb, _):
+                at = chunk(rb, T)
+                rows = g_s[h, at, :]
+                delta = jnp.sum(rows.astype(F32) * ctx_s[h, at, :], axis=-1, keepdims=True)
+                probs = p_s[h, at, :].astype(F32)
+                score = (probs * (dot_nt(rows, v_s[h]) - delta)).astype(BF)
+                ds_s[at, :] = score
+                dq_s[0, i, at, :] = (dot(score, k_s[h]) * 0.125).astype(BF)
+                return 0
+
+            lax.fori_loop(0, 4, block, 0)
+            dq_s[1, i] = dot_tn(query, ds_s[...]).T.astype(BF)
+            dq_s[2, i] = dot_tn(grads, p_s[h]).T.astype(BF)
+            return 0
+
+        lax.fori_loop(0, 3, one, 0)
+        for kind in range(3):
+            cat = place([dq_s[kind, i] for i in range(3)])
+            dqkv[m, :, kind * 256 : kind * 256 + 256] = cat
+            if kind != 1:
+                lanes = pl.ds(pl.multiple_of(half * H2 + odd * 128, 128), 256)
+                row = 14 + kind // 2
+                sm_acc[row : row + 1, lanes] += column_sum(cat.astype(F32))
+
+    def input_back(m):
+        def rows_of(t, _):
+            at = pl.ds(pl.multiple_of(t * 2 * T, 2 * T), 2 * T)
+            put_part(sum_input[m].buf, m, t, dot_nt(dqkv[m, at, :], w_attn[:, 0:768]))
+            return 0
+
+        lax.fori_loop(0, 2, rows_of, 0)
+
+    def attend_weights():
+        def cols_of(t, _):
+            at = chunk(t, 256)
+            rows = x_full[:, :, at].reshape(2 * ROWS, 256)
+            grads = dot_tn(rows, dqkv[...].reshape(2 * ROWS, 768)).astype(BF)
+            dwa[0, at, :] = grads[:, 0:512]
+            dwa[1, at, 0:256] = grads[:, 512:768]
+            rows = branch_full[:, :, at].reshape(2 * ROWS, 256)
+            dwa[1, at, 256:512] = dot_tn(rows, ctx_cat[...].reshape(2 * ROWS, 256)).astype(BF)
+            return 0
+
+        lax.fori_loop(0, D // 256, cols_of, 0)
+
+    class Reduce:
+        def __init__(self, index, buf, incoming, zin):
+            self.buf, self.incoming, self.zin = buf, incoming, zin
+            self.swap = remote(buf.at[other], incoming, gc_ss.at[index], gc_rs.at[index], sib)
+            self.push = [
+                remote(
+                    buf.at[c, chunk(xor(z, dz), DZ), :],
+                    zin.at[dz - 1],
+                    gz_ss.at[index, dz - 1],
+                    gz_rs.at[index, dz - 1],
+                    (xor(z, dz), b, c),
+                )
+                for dz in (1, 2, 3)
+            ]
+
+        def join(self):
+            self.swap.wait_recv()
+
+            def rows_of(t, _):
+                at = chunk(t, DZ)
+                mine = self.buf[c, at, :].astype(F32)
+                self.buf[c, at, :] = (mine + self.incoming[at, :].astype(F32)).astype(BF)
+                return 0
+
+            lax.fori_loop(0, D // DZ, rows_of, 0)
+            for copy in self.push:
+                copy.start()
+
+        def total(self):
+            for copy in self.push:
+                copy.wait_recv()
+            value = self.buf[c, chunk(z, DZ), :].astype(F32)
+            for dz in (0, 1, 2):
+                value = value + self.zin[dz].astype(F32)
+            return value.astype(BF)
+
+        def drain(self):
+            self.swap.wait_send()
+            for copy in self.push:
+                copy.wait_send()
+
+    reduce_feed = Reduce(0, dwf, dwf_in, zf_in)
+    reduce_attn = Reduce(1, dwa, dwa_in, zf_a)
+
+    gather_x[0].end()
+    project(0)
+    attend(0)
+    branch(0)
+    sum_branch[0].start()
+    gather_x[1].end()
+    project(1)
+    sum_branch[0].mid()
+    attend(1)
+    branch(1)
+    sum_branch[1].start()
+    first_norm(0)
+    gather_first[0].start()
+    for row, local in ffn_copies:
+        for copy in row:
+            copy.wait_recv()
+        local.wait()
+    share_gu = remote(w_gu.at[c], w_gu.at[c], wc_ss.at[1], wc_rs.at[1], sib)
+    lanes = w_down.at[:, chunk(c, UB)]
+    share_down = remote(lanes, lanes, wc_ss.at[2], wc_rs.at[2], sib)
+    share_gu.start()
+    share_down.start()
+    sum_branch[1].mid()
+    gather_first[0].mid()
+    first_norm(1)
+    gather_first[1].start()
+    share_gu.wait_recv()
+    share_down.wait_recv()
+    gather_first[0].end()
+    feed_forward(0)
+    sum_feed[0].start()
+    gather_first[1].mid()
+    gather_first[1].end()
+    sum_feed[0].mid()
+    feed_forward(1)
+    sum_feed[1].start()
+    second_norm(0)
+    gather_feed[0].start()
+    sum_feed[1].mid()
+    gather_feed[0].mid()
+    second_norm(1)
+    gather_feed[1].start()
+    out_copies = [
+        remote(out_ref.at[2 * c + m], out_ref.at[2 * c + m], io_ss.at[0, m], io_rs.at[0, m], sib)
+        for m in (0, 1)
+    ]
+    for copy in out_copies:
+        copy.start()
+    gather_feed[0].end()
+    sum_branch[0].drain()
+    feed_backward(0)
+    sum_first[0].start()
+    gather_feed[1].mid()
+    gather_feed[1].end()
+    sum_first[0].mid()
+    sum_branch[1].drain()
+    feed_backward(1)
+    sum_first[1].start()
+    first_back(0)
+    gather_branch[0].start()
+    feed_weights()
+    reduce_feed.swap.start()
+    sum_first[1].mid()
+    gather_branch[0].mid()
+    first_back(1)
+    gather_branch[1].start()
+    reduce_feed.join()
+    gather_branch[0].end()
+    context_back(0)
+    attend_back(0)
+    sum_feed[0].drain()
+    input_back(0)
+    sum_input[0].start()
+    gather_branch[1].mid()
+    gather_branch[1].end()
+    context_back(1)
+    sum_input[0].mid()
+    attend_back(1)
+    sum_feed[1].drain()
+    input_back(1)
+    sum_input[1].start()
+    attend_weights()
+    reduce_attn.swap.start()
+
+    gf_ref[b] = reduce_feed.total()
+    feed_out = [
+        remote(gf_ref.at[b], gf_ref.at[b], gp_ss.at[0, k - 1], gp_rs.at[0, k - 1], (z, xor(b, k), c))
+        for k in (1, 2, 3)
+    ]
+    for copy in feed_out:
+        copy.start()
+    reduce_attn.join()
+
+    for g in (0, 1):
+        for kind in (0, 1):
+            row = 6 + (2 * g + kind) * 2
+            values = eb_acc[2 * g + kind : 2 * g + kind + 1, :]
+            for h in (0, 1):
+                sm_acc[row + h : row + h + 1, chunk(odd, UB)] = jnp.where(half == h, values, 0.0)
+    sm_copies = []
+    steps = [sib, xdev, ydev, (xor(z, 1), b, c), (xor(z, 2), b, c)]
+    sm_in[0] = sm_acc[...]
+    for index, dev in enumerate(steps):
+        copy = remote(sm_in.at[2 * index], sm_in.at[2 * index + 1], sm_ss.at[index], sm_rs.at[index], dev)
+        copy.start()
+        copy.wait_recv()
+        sm_copies.append(copy)
+        value = sm_in[2 * index] + sm_in[2 * index + 1]
+        if index + 1 < len(steps):
+            sm_in[2 * index + 2] = value
+        else:
+            sm_ref[...] = value
+
+    ig_copies = []
+    for m in (0, 1):
+        if m == 1:
+            sum_input[1].mid()
+        ig_ref[2 * c + m] = gr1_s[m] + sum_input[m].end()
+        copy = remote(ig_ref.at[2 * c + m], ig_ref.at[2 * c + m], io_ss.at[1, m], io_rs.at[1, m], sib)
+        copy.start()
+        ig_copies.append(copy)
+
+    fin_a[...] = reduce_attn.total()
+    slot = ga_ref.at[odd, c]
+    attn_out = [
+        remote(fin_a, slot, gp_ss.at[1, k], gp_rs.at[1 + odd, c], (z, xor(b, k), half))
+        for k in (1, 2, 3)
+    ]
+    for copy in attn_out:
+        copy.start()
+    attn_cross = remote(fin_a, slot, gp_ss.at[1, 0], gp_rs.at[1 + odd, c], sib)
+
+    @pl.when(c != half)
+    def _():
+        attn_cross.start()
+
+    @pl.when(c == half)
+    def _():
+        ga_ref[odd, c] = fin_a[...]
+
+    for parity in (0, 1):
+        for core in (0, 1):
+            mine = jnp.logical_and(c == half, jnp.logical_and(odd == parity, c == core))
+
+            @pl.when(jnp.logical_not(mine))
+            def _():
+                remote(
+                    fin_a, ga_ref.at[parity, core], gp_ss.at[1, 0], gp_rs.at[1 + parity, core], sib
+                ).wait_recv()
+
+    @pl.when(c != half)
+    def _():
+        attn_cross.wait_send()
+
+    for copy in attn_out + sm_copies + [pack_copy, attn_share, share_gu, share_down]:
+        copy.wait_send()
+    for copy in feed_out + out_copies + ig_copies:
+        copy.wait()
+
+    @pl.when(c == half)
+    def _():
+        for kind in range(4):
+            row, cross, local = attn_copies[kind]
+            for copy in row:
+                copy.wait_send()
+
+            @pl.when(c != kind // 2)
+            def _():
+                cross.wait_send()
+
+    for row, local in ffn_copies:
+        for copy in row:
+            copy.wait_send()
+    for item in gather_x + gather_first + gather_feed + gather_branch + sum_first + sum_input:
+        item.drain()
+    reduce_feed.drain()
+    reduce_attn.drain()
+
+
+def planes(
+    layer_input,
+    sequence_lengths,
+    alibi_slopes,
+    project_weight,
+    project_bias,
+    output_weight,
+    output_bias,
+    first_gain,
+    first_shift,
+    expand_weight,
+    expand_bias,
+    down_weight,
+    down_bias,
+    second_gain,
+    second_shift,
+    layer_cotangent,
+):
+    batches, tokens, width = layer_input.shape
+    units = expand_weight.shape[2]
+    shard = project_weight.shape[0]
+    half_width = project_weight.shape[2]
+    heads = alibi_slopes.shape[0]
+    rows = 4 * tokens
+    part_units = units // 4
+    wa = jnp.concatenate([jnp.transpose(project_weight, (1, 0, 2)), output_weight.T[None]], axis=0)
+    wf = jnp.concatenate([jnp.transpose(expand_weight, (1, 0, 2)), down_weight.T[None]], axis=0)
+
+    def padded(item):
+        return jnp.pad(item, ((0, 0), (0, units - item.shape[1])))
+
+    vectors = jnp.stack([output_bias, first_gain, first_shift, down_bias, second_gain, second_shift])
+    pack = jnp.concatenate(
+        [
+            expand_bias,
+            padded(project_bias),
+            padded(vectors),
+            jnp.broadcast_to(alibi_slopes[:, None], (heads, units)),
+        ],
+        axis=0,
+    )
+    lengths = sequence_lengths.reshape(batches * 3)
+    vmem = pl.BlockSpec(memory_space=pltpu.VMEM)
+    hbm = pl.BlockSpec(memory_space=pl.ANY)
+    smem = pl.BlockSpec(memory_space=pltpu.SMEM)
+    dma = pltpu.SemaphoreType.DMA
+    full = pltpu.VMEM((8, tokens, width), BF)
+    outs = pl.pallas_call(
+        layer_kernel,
+        out_shape=(
+            jax.ShapeDtypeStruct((batches, tokens, width), BF),
+            jax.ShapeDtypeStruct((batches, tokens, width), F32),
+            jax.ShapeDtypeStruct((2, 2, shard, 512), BF),
+            jax.ShapeDtypeStruct((4, shard, 3 * part_units), BF),
+            jax.ShapeDtypeStruct((16, width), F32),
+        ),
+        in_specs=[vmem, vmem, hbm, hbm, vmem, smem],
+        out_specs=(vmem, vmem, vmem, vmem, vmem),
+        scratch_shapes=[
+            full, full, full, full,
+            pltpu.VMEM((width, 1024), BF),
+            pltpu.VMEM((2, width, 2 * part_units), BF),
+            pltpu.VMEM((width, 2 * part_units), BF),
+            pltpu.VMEM((2,) + pack.shape, F32),
+            pltpu.VMEM((2, 8, tokens, width), BF),
+            pltpu.VMEM((4, 2, 2, tokens, width // 2), BF),
+            pltpu.VMEM((4, 2, 2, tokens, width // 2), BF),
+            pltpu.VMEM((4, 2, 2, tokens, width // 2), BF),
+            pltpu.VMEM((6, rows, 64), BF),
+            pltpu.VMEM((6, rows, 64), BF),
+            pltpu.VMEM((6, rows, 64), BF),
+            pltpu.VMEM((6, rows, 64), BF),
+            pltpu.VMEM((6, rows, rows), BF),
+            pltpu.VMEM((6, rows, 64), F32),
+            pltpu.VMEM((2, rows, 256), BF),
+            pltpu.VMEM((2, rows, 768), BF),
+            pltpu.VMEM((rows, rows), BF),
+            pltpu.VMEM((3, 3, rows, 64), BF),
+            pltpu.VMEM((2, rows, rows), F32),
+            pltpu.VMEM((2 * rows, 2 * part_units), BF),
+            pltpu.VMEM((2 * rows, 2 * part_units), BF),
+            pltpu.VMEM((2 * rows, 2 * part_units), BF),
+            pltpu.VMEM((2, 2 * rows, 2 * part_units), BF),
+            pltpu.VMEM((8, part_units), F32),
+            pltpu.VMEM((2, tokens, width), F32),
+            pltpu.VMEM((2, tokens, width), F32),
+            pltpu.VMEM((2, tokens, 1), F32),
+            pltpu.VMEM((2, tokens, width), F32),
+            pltpu.VMEM((2, tokens, width), F32),
+            pltpu.VMEM((2, width, 3 * part_units), BF),
+            pltpu.VMEM((width, 3 * part_units), BF),
+            pltpu.VMEM((3, shard, 3 * part_units), BF),
+            pltpu.VMEM((2, width, 512), BF),
+            pltpu.VMEM((width, 512), BF),
+            pltpu.VMEM((3, shard, 512), BF),
+            pltpu.VMEM((shard, 512), BF),
+            pltpu.VMEM((16, width), F32),
+            pltpu.VMEM((10, 16, width), F32),
+            pltpu.VMEM((3, 8, 128), F32),
+            dma((4, 2, 4)), dma((4, 2, 4)),
+            dma((4, 2, 6)), dma((4, 2, 6)),
+            dma((2,)),
+            dma((4, 4)), dma((4, 4)),
+            dma((4, 3)), dma((4, 3)),
+            dma((8,)),
+            dma((3,)), dma((3,)),
+            dma((2,)), dma((2,)),
+            dma((2, 3)), dma((2, 3)),
+            dma((2, 4)), dma((3, 3)),
+            dma((5,)), dma((5,)),
+            dma((2, 2)), dma((2, 2)),
+        ],
+        compiler_params=pltpu.CompilerParams(
+            collective_id=0, has_side_effects=True, vmem_limit_bytes=VMEM_BYTES
+        ),
+        name="encoder_layer",
+    )(layer_input, layer_cotangent, wa, wf, pack, lengths)
+    layer_output, input_gradient, attn, feed, sums = outs
+    core = lax.axis_index("head")
+    even, odd = attn[0], attn[1]
+    low = jnp.concatenate([even[:, :, 0:192], odd[:, :, 64:256]], axis=2)
+    high = jnp.concatenate([even[:, :, 256:448], odd[:, :, 320:512]], axis=2)
+    project_grad = jnp.stack([low[0], high[0], low[1]], axis=1).astype(F32)
+    output_grad = high[1].T.astype(F32)
+    feed = feed.reshape(4, shard, 3, part_units)
+    feed = jnp.transpose(feed, (1, 2, 0, 3)).reshape(shard, 3, units)
+    expand_grad = feed[:, 0:2].astype(F32)
+    down_grad = feed[:, 2].T.astype(F32)
+    bias_rows = lax.dynamic_slice_in_dim(sums[6:14].reshape(2, 2, units), core, 1, 0)[0]
+    project_bias_grad = lax.dynamic_slice_in_dim(sums[14:16], core * half_width, half_width, 1)
+    return (
+        layer_output,
+        input_gradient,
+        project_grad,
+        project_bias_grad,
+        output_grad,
+        sums[0],
+        sums[1],
+        sums[2],
+        expand_grad,
+        bias_rows,
+        down_grad,
+        sums[3],
+        sums[4],
+        sums[5],
+    )
+
+
+def fits(mesh):
+    shape = dict(mesh.shape)
+    return shape["dp"] == 4 and shape["blk"] == 4 and shape["head"] == 2
+
+
 def solution(mesh):
     in_specs = (
         P(None, ("dp", "blk"), None),
@@ -391,4 +1259,5 @@
         P(),
         P(),
     )
-    return jax.shard_map(local, mesh=mesh, in_specs=in_specs, out_specs=out_specs, check_vma=False)
+    body = planes if fits(mesh) else general
+    return jax.shard_map(body, mesh=mesh, in_specs=in_specs, out_specs=out_specs, check_vma=False)

time: 767 us -> 275 us (0.36)
  waiting for transfers between devices: 436 us -> 0 us
  Pallas kernels: 0 us -> 234 us
  blocking collectives: 93.7 us -> 0 us
  matrix products: 71 us -> 0 us
  other arithmetic: 61.2 us -> 8.19 us
  local copies, waits for them, and re-layouts: 60.4 us -> 27.5 us
  starting transfers between devices: 19.5 us -> 0 us
  between operations: 15.7 us -> 0.74 us
    pallas_call x0 -> x1, Pallas kernels: none -> 234 us  [planes(): pl.pallas_call(layer_kernel, out_shape=(jax.ShapeDtypeStruct((batches, to...]
    all_gather x5 -> x0, waiting for transfers between devices: 201 us -> none  [the longest x1 90.1 us: local(): lax.all_gather(expand_weight, 'dp', axis=0, tiled=True)]
    reduce_scatter x3 -> x0, waiting for transfers between devices: 91.3 us -> none  [the longest x1 49.4 us: local(): lax.psum_scatter(down_part.astype(jnp.bfloat16), 'dp', scatter_dimension=...]
    ppermute x14 -> x0, waiting for transfers between devices: 87.1 us -> none  [shifted(): return lax.ppermute(value, axis, pairs)]
    psum x1 -> x0, blocking collectives: 76.8 us -> none  [local(): lax.psum((project_bias_grad, output_bias_grad, first_gain_grad, first_shi...]
    dot_general x34 -> x0, matrix products: 71 us -> none  [the longest x4 8.47 us: cycle_step(): jnp.einsum('mhqk,mkhd->mqhd', grad_score, keys_block, preferred_element_t...]
    psum x5 -> x0, waiting for transfers between devices: 55.2 us -> none  [the longest x1 18.4 us: local(): lax.psum(shards[0].astype(jnp.bfloat16), 'blk').astype(jnp.float32)]
    convert_element_type x25 -> x4, other arithmetic: 32.3 us -> 3.24 us  [the longest x1 1.15 us: planes(): down_grad = feed[:, 2].T.astype(F32)]
  transfers between devices with their start and end apart: 28 -> 0, of which waited for: 26 -> 0; matrix products, arithmetic and copies ran while one was open for 19% -> 0% of each run, Pallas kernels for 0% -> 0%
where the time goes in v1:
time: 275 us; the launch traced here: 271 us
  Pallas kernels  234 us (85%)
  local copies, waits for them, and re-layouts  27.5 us (10%)
  other arithmetic  8.19 us (3%)
    pallas_call x1, Pallas kernels, planes(): pl.pallas_call(layer_kernel, out_shape=(jax.ShapeDtypeStruct((batches, to...  234 us
    unnamed x13, local copies, waits for them, and re-layouts  6.95 us

profile of v1, /device:TPU:0, one launch (start us, length us, event | category | flops | bytes accessed | tf_op | source)
XLA Modules:
  0.0 270.9 jit_solution(5316903202287341305)
XLA Ops:
  0.6 0.0 copy-start.1
  0.7 0.8 pad.20.clone
  1.5 0.8 copy.38
  2.2 0.6 reshape.45.len_ref
  2.8 0.7 stack.24
  3.5 0.7 stack.25
  4.2 0.7 stack.26
  4.9 0.7 stack.27
  5.6 0.7 stack.28
  6.3 0.7 stack.29
  7.0 1.4 fusion.6.pack_ref
  8.5 0.0 copy-start.3
  8.5 2.0 pad_maximum_fusion.1.wa_ref
  10.5 0.0 copy-done.1
  10.5 0.1 copy.42
  10.6 0.0 copy-done.3
  10.6 1.4 pad_maximum_fusion.wf_ref
  12.0 234.5 %encoder_layer.1 = (bf16[4,128,768]{2,1,0:T(8,128)(2,1)}, f32[4,128,768]{2,1,0:T(8,128)}, bf16[2,2,192,512]{3,2,1,0:T(8,128)(2,1)}, bf16[4,192,1152]{2,1,0:T(8,128)(2,1)}, f32[16,768]{1,0:T(8,128)}) custom-call(bf16[4,128,768]{2,1,0:T(8,128)(2,1)} %x_ref.1, bf16[4,128,768]{2,1,0:T(8,128)(2,1)} %cot_ref.1, bf16[4,192,384]{2,1,0:T(8,128)(2,1)} %pad_maximum_fusion.1.wa_ref, ...), custom_call_target="tpu_custom_call" | custom-call | tf_op jit(solution)/shard_map/encoder_layer/pallas_call | solution.py:1121
  246.5 0.7 slice.69
  247.2 0.6 constant_dynamic-slice_fusion
  247.8 0.8 slice.75
  248.6 1.6 slice_reduce_fusion
  250.2 0.6 dynamic-slice_bitcast_fusion
  250.9 1.2 slice_bitcast_fusion.2
  252.0 0.2 fusion.9
  252.2 0.8 convert_bitcast_fusion.1
  253.1 0.1 fusion.3
  253.2 1.0 maximum_convert_fusion
  254.2 3.3 %reshape.46 = bf16[4,192,3,384]{3,2,1,0:T(4,128)(2,1)S(1)} reshape(bf16[4,192,1152]{2,1,0:T(8,128)(2,1)} %get-tuple-element.23) | data formatting | bytes 3538944 | tf_op jit(solution)/shard_map/reshape | solution.py:1198
  257.5 2.9 %copy.39 = bf16[192,3,4,384]{3,2,0,1:T(4,128)(2,1)} copy(bf16[192,3,4,384]{3,1,0,2:T(4,128)(2,1)S(1)} %bitcast.41) | data formatting | bytes 3538944 | tf_op jit(solution)/shard_map/transpose | solution.py:1199
  260.3 3.0 %reshape.47 = bf16[192,3,1536]{2,0,1:T(8,128)(2,1)S(1)} reshape(bf16[192,3,4,384]{3,2,0,1:T(4,128)(2,1)} %copy.39) | data formatting | bytes 3538944 | tf_op jit(solution)/shard_map/reshape | solution.py:1199
  263.4 1.1 convert_bitcast_fusion
  264.5 0.3 slice_convert_fusion
  264.8 0.0 copy-start.2
  264.8 3.2 %copy.40 = f32[192,2,1536]{2,1,0:T(2,128)} copy(f32[192,2,1536]{2,0,1:T(8,128)S(1)} %slice_convert_fusion) | data formatting | bytes 4718592
  268.1 0.0 copy-done.2
  268.1 0.0 copy-start
  268.1 0.9 copy.45
  268.9 0.8 copy-done
  269.7 1.1 copy.46
  (2 shorter events, 0.1 us)
Async XLA Ops:
  0.6 9.9 %copy-start.1 = (bf16[192,2,1536]{2,1,0:T(2,128)(2,1)S(1)}, bf16[192,2,1536]{2,1,0:T(2,128)(2,1)}, u32[]{:S(2)}) copy-start(bf16[192,2,1536]{2,1,0:T(2,128)(2,1)} %param.25) | copy-start | bytes 3538948
  8.5 2.2 copy-start.3
  264.8 3.2 %copy-start.2 = (bf16[4,128,768]{2,1,0:T(8,128)(2,1)S(1)}, bf16[4,128,768]{2,1,0:T(8,128)(2,1)}, u32[]{:S(2)}) copy-start(bf16[4,128,768]{2,1,0:T(8,128)(2,1)} %get-tuple-element.98) | copy-start | bytes 2359300
  268.1 1.7 copy-start

commit v2 on v0

--- a/solution.py
+++ b/solution.py
@@ -1,8 +1,11 @@
+import functools
 import math
 
 import jax
 import jax.numpy as jnp
 from jax import lax
+from jax.experimental import pallas as pl
+from jax.experimental.pallas import tpu as pltpu
 from jax.sharding import PartitionSpec as P
 
 EPSILON = 1e-12
@@ -70,7 +73,7 @@
     return lax.fori_loop(0, count_rows // block, step, state)
 
 
-def local(
+def general(
     layer_input,
     sequence_lengths,
     alibi_slopes,
@@ -356,6 +359,1050 @@
     )
 
 
+MESH = pl.DeviceIdType.MESH
+BF = jnp.bfloat16
+F32 = jnp.float32
+FAR = 1e33
+VMEM_BYTES = 63 << 20
+HEAD = 64
+
+
+def dot(a, b):
+    return lax.dot_general(a, b, (((1,), (0,)), ((), ())), preferred_element_type=F32)
+
+
+def dot_nt(a, b):
+    return lax.dot_general(a, b, (((1,), (1,)), ((), ())), preferred_element_type=F32)
+
+
+def dot_tn(a, b):
+    return lax.dot_general(a, b, (((0,), (0,)), ((), ())), preferred_element_type=F32)
+
+
+def column_sum(rows):
+    return jnp.sum(rows, axis=0, keepdims=True)
+
+
+def row_mean(rows):
+    return jnp.mean(rows, axis=-1, keepdims=True)
+
+
+def standardize(rows):
+    centered = rows - row_mean(rows)
+    inverse = lax.rsqrt(row_mean(centered * centered) + EPSILON)
+    return centered * inverse, inverse
+
+
+def standardize_back(grad, normal, inverse):
+    return inverse * (grad - row_mean(grad) - normal * row_mean(grad * normal))
+
+
+def layer_kernel(
+    x_ref, cot_ref, pw_ref, ow_ref, ew_ref, dw_ref, len_ref, slope_ref, pb_ref, eb_ref,
+    ob_ref, g1_ref, s1_ref, db_ref, g2_ref, s2_ref,
+    out_ref, ig_ref, ga_ref, gf_ref, early_ref, late_ref,
+    x_full, first_full, feed_full, branch_full,
+    w_attn, w_gu, w_down, packs, own_attn,
+    part, r1x, r1y, r2,
+    q_s, k_s, v_s, g_s, p_s, ctx_s, ctx_cat, dqkv, ds_s, dq_s, far_s,
+    act_s, upd_s, hid_s, dgu_s, eb_acc,
+    first_own, n1_s, a1_s, gr2_s, gr1_s,
+    dwf, dwf_in, dwf_z, dwa, dwa_in, dwa_z, fin_a,
+    early, late, slope_s,
+    ag_ss, ag_rs, rs_ss, rs_rs, pk_sem, wa_ss, wa_rs, wf_ss, wf_rs, wl_sem, wc_ss, wc_rs,
+    gc_ss, gc_rs, gz_ss, gz_rs, gp_ss, gp_rs, ge_ss, ge_rs, gl_ss, gl_rs, io_ss, io_rs,
+):
+    z, b, c = lax.axis_index("dp"), lax.axis_index("blk"), lax.axis_index("head")
+    half, odd = b // 2, b % 2
+    xor = jnp.bitwise_xor
+    other = 1 - c
+    bx, by, bd = xor(b, 1), xor(b, 2), xor(b, 3)
+    sib, xdev, ydev = (z, b, other), (z, bx, c), (z, by, c)
+    near, far, opposite = ((xor(z, k), b, c) for k in (1, 2, 3))
+    inner = jnp.logical_or(z == 1, z == 2)
+    outer = jnp.logical_not(inner)
+    T = x_ref.shape[1]
+    D = x_ref.shape[2]
+    H2 = D // 2
+    ROWS = 4 * T
+    DZ = pw_ref.shape[1]
+    UB = dw_ref.shape[1] // 4
+    HW = 3 * HEAD
+    lo, hi = pl.ds(0, H2), pl.ds(H2, H2)
+
+    def chunk(index, size):
+        return pl.ds(pl.multiple_of(index * size, size), size)
+
+    mine_z, near_z, far_z, opposite_z = (chunk(xor(z, k), DZ) for k in range(4))
+    started = []
+
+    def raw(src, dst, ss, rs, dev):
+        return pltpu.make_async_remote_copy(
+            src_ref=src, dst_ref=dst, send_sem=ss, recv_sem=rs, device_id=dev, device_id_type=MESH
+        )
+
+    class Copy:
+        def __init__(self, *args):
+            self.copy = raw(*args)
+            self.sent = self.received = False
+
+        def start(self):
+            self.copy.start()
+            started.append(self)
+
+        def wait_recv(self):
+            self.copy.wait_recv()
+            self.received = True
+
+        def wait_send(self):
+            self.copy.wait_send()
+            self.sent = True
+
+        def finish(self):
+            if not self.received:
+                self.wait_recv()
+            if not self.sent:
+                self.wait_send()
+
+    partners = [(z, xor(b, k), cc) for k in (1, 2, 3) for cc in (c, other)] + [sib]
+    partners += [(xor(z, k), b, cc) for k in (1, 2, 3) for cc in (c, other)]
+    barrier = pltpu.get_barrier_semaphore()
+    for dev in partners:
+        pl.semaphore_signal(barrier, inc=1, device_id=dev, device_id_type=MESH)
+    pl.semaphore_wait(barrier, len(partners))
+
+    class Gather:
+        def __init__(self, full, phase, m):
+            ss, rs = ag_ss.at[phase, m], ag_rs.at[phase, m]
+            own, sx, sy = m * 4 + b, m * 4 + bx, m * 4 + by
+            self.cx = Copy(full.at[own], full.at[own], ss.at[0], rs.at[0], xdev)
+            self.cy = Copy(full.at[own], full.at[own], ss.at[1], rs.at[1], ydev)
+            self.fx = Copy(full.at[sx, :, lo], full.at[sx, :, lo], ss.at[2], rs.at[2], ydev)
+            self.fy = Copy(full.at[sy, :, hi], full.at[sy, :, hi], ss.at[3], rs.at[3], xdev)
+
+        def start(self):
+            self.cx.start()
+            self.cy.start()
+
+        def mid(self):
+            self.cx.wait_recv()
+            self.fx.start()
+            self.cy.wait_recv()
+            self.fy.start()
+
+        def end(self):
+            self.fx.wait_recv()
+            self.fy.wait_recv()
+
+    class Scatter:
+        def __init__(self, phase, m):
+            ss, rs = rs_ss.at[phase, m], rs_rs.at[phase, m]
+            buf = part.at[phase % 2]
+            own, sx, sy, sd = m * 4 + b, m * 4 + bx, m * 4 + by, m * 4 + bd
+            ix, iy, i2 = r1x.at[phase, m], r1y.at[phase, m], r2.at[phase, m]
+            self.buf, self.own, self.sx, self.sy = buf, own, sx, sy
+            self.ix, self.iy, self.i2 = ix, iy, i2
+            self.xd = Copy(buf.at[sd, :, lo], ix.at[1], ss.at[0], rs.at[0], xdev)
+            self.yd = Copy(buf.at[sd, :, hi], iy.at[1], ss.at[1], rs.at[1], ydev)
+            self.xo = Copy(buf.at[sx, :, lo], ix.at[0], ss.at[2], rs.at[2], xdev)
+            self.yo = Copy(buf.at[sy, :, hi], iy.at[0], ss.at[3], rs.at[3], ydev)
+            self.y2 = Copy(buf.at[sy, :, lo], i2.at[0], ss.at[4], rs.at[4], ydev)
+            self.x2 = Copy(buf.at[sx, :, hi], i2.at[1], ss.at[5], rs.at[5], xdev)
+
+        def start(self):
+            for copy in (self.xd, self.yd, self.xo, self.yo):
+                copy.start()
+
+        def mid(self):
+            buf = self.buf
+            self.xd.wait_recv()
+            buf[self.sy, :, :H2] = (
+                buf[self.sy, :, :H2].astype(F32) + self.ix[1].astype(F32)
+            ).astype(BF)
+            self.y2.start()
+            self.yd.wait_recv()
+            buf[self.sx, :, H2:] = (
+                buf[self.sx, :, H2:].astype(F32) + self.iy[1].astype(F32)
+            ).astype(BF)
+            self.x2.start()
+
+        def end(self):
+            for copy in (self.xo, self.yo, self.y2, self.x2):
+                copy.wait_recv()
+            mine = self.buf[self.own].astype(F32)
+            low = mine[:, :H2] + self.ix[0].astype(F32) + self.i2[0].astype(F32)
+            high = mine[:, H2:] + self.iy[0].astype(F32) + self.i2[1].astype(F32)
+            return jnp.concatenate([low, high], axis=1)
+
+        def drain(self):
+            for copy in (self.xd, self.yd, self.xo, self.yo, self.y2, self.x2):
+                copy.wait_send()
+
+    gather_x = [Gather(x_full, 0, m) for m in (0, 1)]
+    gather_first = [Gather(first_full, 1, m) for m in (0, 1)]
+    gather_feed = [Gather(feed_full, 2, m) for m in (0, 1)]
+    gather_branch = [Gather(branch_full, 3, m) for m in (0, 1)]
+    sum_branch = [Scatter(0, m) for m in (0, 1)]
+    sum_feed = [Scatter(1, m) for m in (0, 1)]
+    sum_first = [Scatter(2, m) for m in (0, 1)]
+    sum_input = [Scatter(3, m) for m in (0, 1)]
+
+    class Column:
+        def __init__(self, pieces, ss, rs):
+            self.pieces, self.ss, self.rs = pieces, ss, rs
+
+        def copy(self, dz, index, src, dst, dev):
+            return raw(src, dst, self.ss.at[dz, index], self.rs.at[dz, index], dev)
+
+        def copies(self):
+            for dz in (2, 1, 3):
+                for index, (src, place_at, core) in enumerate(self.pieces):
+                    yield dz, self.copy(dz, index, src, place_at(mine_z), (xor(z, dz), b, core))
+
+        def send(self):
+            for dz, copy in self.copies():
+                if dz == 3:
+                    pl.when(inner)(copy.start)
+                else:
+                    copy.start()
+
+        def sent(self):
+            for dz, copy in self.copies():
+                if dz == 3:
+                    pl.when(inner)(copy.wait_send)
+                else:
+                    copy.wait_send()
+
+        def arrival(self, dz, index):
+            src, place_at, _ = self.pieces[index]
+            self.copy(dz, index, src, place_at(mine_z), near).wait_recv()
+
+        def passing(self, index):
+            rows = self.pieces[index][1](far_z)
+            return raw(rows, rows, self.ss.at[0, index], self.rs.at[3, index], near)
+
+        def relay(self, index):
+            self.arrival(2, index)
+            pl.when(inner)(self.passing(index).start)
+
+        def relay_all(self):
+            for index in range(len(self.pieces)):
+                self.relay(index)
+
+        def relayed(self, index):
+            pl.when(inner)(self.passing(index).wait_send)
+
+        def rest(self, index):
+            self.arrival(1, index)
+            self.arrival(3, index)
+
+    def attn_place(k):
+        return lambda rows: w_attn.at[rows, pl.ds(k * H2, H2)]
+
+    attn_pieces = [(own_attn.at[:, pl.ds(k * H2, H2)], attn_place(k), k) for k in (0, 1)]
+    attn_column = Column(attn_pieces, wa_ss, wa_rs)
+    attn_own = []
+    for index, (src, place_at, core) in enumerate(attn_pieces):
+        dst = place_at(mine_z)
+        cross = raw(src, dst, wa_ss.at[4, index], wa_rs.at[4, index], sib)
+        local = pltpu.make_async_copy(src, dst, wl_sem.at[index])
+        attn_own.append((cross, local))
+    gu_column = Column(
+        [
+            (ew_ref.at[0, :, chunk(b, UB)], lambda rows: w_gu.at[c, rows, pl.ds(0, UB)], c),
+            (ew_ref.at[1, :, chunk(b, UB)], lambda rows: w_gu.at[c, rows, pl.ds(UB, UB)], c),
+        ],
+        wf_ss.at[0],
+        wf_rs.at[0],
+    )
+    down_column = Column(
+        [(dw_ref.at[:, chunk(b, UB)], lambda rows: w_down.at[rows, chunk(c, UB)], c)],
+        wf_ss.at[1],
+        wf_rs.at[1],
+    )
+    feed_own = []
+    for index, (src, place_at, _) in enumerate(gu_column.pieces + down_column.pieces):
+        feed_own.append(pltpu.make_async_copy(src, place_at(mine_z), wl_sem.at[2 + index]))
+
+    for m in (0, 1):
+        x_full[m * 4 + b] = x_ref[2 * c + m]
+    gather_x[0].start()
+
+    @pl.when(c == half)
+    def _():
+        shards = [pw_ref[kind] for kind in range(3)] + [ow_ref[...]]
+        own_attn[...] = jnp.concatenate(
+            [jnp.where(odd == 0, item[:, 0:HW], item[:, HW : 2 * HW]) for item in shards], axis=1
+        )
+        attn_column.send()
+        for index, (cross, local) in enumerate(attn_own):
+            pl.when(c == index)(local.start)
+            pl.when(c != index)(cross.start)
+
+    for row in (0, 1):
+        packs[c, row : row + 1, :] = eb_ref[row : row + 1, :]
+        packs[c, row + 2 : row + 3, 0:H2] = pb_ref[row : row + 1, :]
+    for i in range(6):
+        packs[c, 10 + i : 11 + i, 0:128] = jnp.full((1, 128), slope_ref[i], F32)
+    pack_copy = Copy(packs.at[c], packs.at[c], pk_sem.at[0], pk_sem.at[1], sib)
+    pack_copy.start()
+    gather_x[1].start()
+    for copy in feed_own:
+        copy.start()
+
+    for m in (0, 1):
+        start_one = len_ref[0, 0, 2 * c + m]
+        start_two = start_one + len_ref[1, 0, 2 * c + m]
+        for rb in range(4):
+            rows = lax.broadcasted_iota(jnp.int32, (T, ROWS), 0) + rb * T
+            cols = lax.broadcasted_iota(jnp.int32, (T, ROWS), 1)
+            seq_r = (rows >= start_one).astype(jnp.int32) + (rows >= start_two).astype(jnp.int32)
+            seq_c = (cols >= start_one).astype(jnp.int32) + (cols >= start_two).astype(jnp.int32)
+            distance = jnp.abs(rows - cols).astype(F32)
+            far_s[m, pl.ds(rb * T, T), :] = jnp.where(seq_r == seq_c, distance, FAR)
+    early[...] = jnp.zeros_like(early)
+    late[...] = jnp.zeros_like(late)
+    eb_acc[...] = jnp.zeros_like(eb_acc)
+
+    for index in (0, 1):
+        pl.when(c == index)(functools.partial(attn_column.relay, index))
+    gu_column.send()
+    gather_x[0].mid()
+    gather_x[1].mid()
+    pack_copy.wait_recv()
+    for index, (cross, local) in enumerate(attn_own):
+
+        @pl.when(c == index)
+        def _():
+            pl.when(c == half)(local.wait)
+            pl.when(c != half)(cross.wait_recv)
+            attn_column.rest(index)
+
+    lanes = w_attn.at[:, chunk(c, H2)]
+    attn_share = Copy(lanes, lanes, wc_ss.at[0], wc_rs.at[0], sib)
+    attn_share.start()
+
+    for i in range(3):
+        low, high = packs[half, 10 + i : 11 + i, 0:128], packs[half, 13 + i : 14 + i, 0:128]
+        slope_s[i] = jnp.broadcast_to(jnp.where(odd == 0, low, high), (8, 128))
+
+    def vector(ref):
+        return ref[...].reshape(1, D)
+
+    def project(m):
+        biases = packs[half, 2:4, 0:H2]
+        biases = jnp.where(odd == 0, biases[:, 0:HW], biases[:, HW : 2 * HW])
+
+        def rows_of(t, _):
+            rows = x_full[pl.ds(m * 4 + t * 2, 2)].reshape(2 * T, D)
+            at = pl.ds(pl.multiple_of(t * 2 * T, 2 * T), 2 * T)
+            mixed = dot(rows, w_attn[:, 0 : 3 * HW])
+            query = (mixed[:, 0:HW] + biases[0:1]).astype(BF) * jnp.asarray(0.125, BF)
+            keys = mixed[:, HW : 2 * HW].astype(BF)
+            values = (mixed[:, 2 * HW : 3 * HW] + biases[1:2]).astype(BF)
+            for i in range(3):
+                cols = slice(i * HEAD, i * HEAD + HEAD)
+                q_s[m * 3 + i, at, :] = query[:, cols]
+                k_s[m * 3 + i, at, :] = keys[:, cols]
+                v_s[m * 3 + i, at, :] = values[:, cols]
+            return 0
+
+        lax.fori_loop(0, 2, rows_of, 0)
+
+    def attend(m, first, last):
+        def one(index, _):
+            i, rb = index // 4, index % 4
+            at = chunk(rb, T)
+            h = m * 3 + i
+            scores = dot_nt(q_s[h, at, :], k_s[h])
+            scores = scores - slope_s[i][0:1, 0:1] * far_s[m, at, :]
+            top = jnp.max(scores, axis=-1, keepdims=True)
+            weights = jnp.exp(scores - top)
+            total = jnp.sum(weights, axis=-1, keepdims=True)
+            probs = (weights * (1.0 / total)).astype(BF)
+            p_s[h, at, :] = probs
+            ctx_s[h, at, :] = dot(probs, v_s[h])
+            return 0
+
+        lax.fori_loop(first, last, one, 0)
+
+    def put_part(buf, m, t, rows):
+        buf[pl.ds(m * 4 + 2 * t, 2)] = rows.astype(BF).reshape(2, T, D)
+
+    def branch(m):
+        def rows_of(t, _):
+            at = pl.ds(pl.multiple_of(t * 2 * T, 2 * T), 2 * T)
+            cat = jnp.concatenate([ctx_s[m * 3 + i, at, :].astype(BF) for i in range(3)], axis=1)
+            ctx_cat[m, at, :] = cat
+            put_part(sum_branch[m].buf, m, t, dot_nt(cat, w_attn[:, 3 * HW : 4 * HW]))
+            return 0
+
+        lax.fori_loop(0, 2, rows_of, 0)
+
+    def first_norm(m):
+        rows = x_ref[2 * c + m].astype(F32) + sum_branch[m].end() + vector(ob_ref)
+        normal, inverse = standardize(rows)
+        first = normal * vector(g1_ref) + vector(s1_ref)
+        n1_s[m], a1_s[m] = normal, inverse
+        first_own[m] = first
+        first_full[m * 4 + b] = first.astype(BF)
+
+    def feed_forward(m):
+        def rows_of(t, _):
+            at = pl.ds(pl.multiple_of(m * ROWS + t * 2 * T, 2 * T), 2 * T)
+            rows = first_full[pl.ds(m * 4 + t * 2, 2)].reshape(2 * T, D)
+            for g in (0, 1):
+                cols = pl.ds(g * UB, UB)
+                bias = packs[g, 0:2, chunk(b, UB)]
+                both = dot(rows, w_gu[g])
+                gate = both[:, :UB] + bias[0:1]
+                up = both[:, UB:] + bias[1:2]
+                cdf = 0.5 + 0.5 * lax.erf(gate * 0.7071067811865476)
+                act = gate * cdf
+                slope = cdf + gate * (jnp.exp(-0.5 * gate * gate) * 0.3989422804014327)
+                hid_s[at, cols] = (act * up).astype(BF)
+                act_s[at, cols] = act.astype(BF)
+                upd_s[at, cols] = (up * slope).astype(BF)
+            return 0
+
+        lax.fori_loop(0, 2, rows_of, 0)
+
+    def feed_out(m):
+        def rows_of(t, _):
+            at = pl.ds(pl.multiple_of(m * ROWS + t * 2 * T, 2 * T), 2 * T)
+            put_part(sum_feed[m].buf, m, t, dot_nt(hid_s[at, :], w_down[...]))
+            return 0
+
+        lax.fori_loop(0, 2, rows_of, 0)
+
+    def add_early(row, rows):
+        early[0, row : row + 1, :] += column_sum(rows)
+
+    def second_norm(m):
+        rows = first_own[m] + sum_feed[m].end() + vector(db_ref)
+        normal, inverse = standardize(rows)
+        out_ref[2 * c + m] = (normal * vector(g2_ref) + vector(s2_ref)).astype(BF)
+        grad = cot_ref[2 * c + m].astype(F32)
+        add_early(4, grad * normal)
+        add_early(5, grad)
+        back = standardize_back(grad * vector(g2_ref), normal, inverse)
+        gr2_s[m] = back
+        low = back.astype(BF)
+        feed_full[m * 4 + b] = low
+        add_early(3, low.astype(F32))
+
+    def feed_backward(m):
+        def rows_of(t, _):
+            at = pl.ds(pl.multiple_of(m * ROWS + t * 2 * T, 2 * T), 2 * T)
+            rows = feed_full[pl.ds(m * 4 + t * 2, 2)].reshape(2 * T, D)
+            hidden = dot(rows, w_down[...])
+            dgate = (hidden * upd_s[at, :].astype(F32)).astype(BF)
+            dup = (hidden * act_s[at, :].astype(F32)).astype(BF)
+            for g in (0, 1):
+                cols = slice(g * UB, g * UB + UB)
+                dgu_s[g, at, 0:UB] = dgate[:, cols]
+                dgu_s[g, at, UB : 2 * UB] = dup[:, cols]
+                eb_acc[2 * g : 2 * g + 1, :] += column_sum(dgate[:, cols].astype(F32))
+                eb_acc[2 * g + 1 : 2 * g + 2, :] += column_sum(dup[:, cols].astype(F32))
+            back = dot_nt(dgu_s[0, at, :], w_gu[0]) + dot_nt(dgu_s[1, at, :], w_gu[1])
+            put_part(sum_first[m].buf, m, t, back)
+            return 0
+
+        lax.fori_loop(0, 2, rows_of, 0)
+
+    def down_weights():
+        def cols_of(t, _):
+            at = chunk(t, 256)
+            rows = feed_full[:, :, at].reshape(2 * ROWS, 256)
+            down = dot_tn(rows, hid_s[...]).astype(BF)
+            for g in (0, 1):
+                dwf[g, at, 2 * UB : 3 * UB] = down[:, g * UB : g * UB + UB]
+            return 0
+
+        lax.fori_loop(0, D // 256, cols_of, 0)
+
+    def expand_weights():
+        def cols_of(t, _):
+            at = chunk(t, 256)
+            rows = first_full[:, :, at].reshape(2 * ROWS, 256)
+            for g in (0, 1):
+                dwf[g, at, 0 : 2 * UB] = dot_tn(rows, dgu_s[g]).astype(BF)
+            return 0
+
+        lax.fori_loop(0, D // 256, cols_of, 0)
+
+    def first_back(m):
+        grad = gr2_s[m] + sum_first[m].end()
+        normal = n1_s[m]
+        add_early(1, grad * normal)
+        add_early(2, grad)
+        back = standardize_back(grad * vector(g1_ref), normal, a1_s[m])
+        gr1_s[m] = back
+        low = back.astype(BF)
+        branch_full[m * 4 + b] = low
+        add_early(0, low.astype(F32))
+
+    def context_back(m):
+        def rows_of(t, _):
+            at = pl.ds(pl.multiple_of(t * 2 * T, 2 * T), 2 * T)
+            rows = branch_full[pl.ds(m * 4 + t * 2, 2)].reshape(2 * T, D)
+            grads = dot(rows, w_attn[:, 3 * HW : 4 * HW]).astype(BF)
+            for i in range(3):
+                g_s[m * 3 + i, at, :] = grads[:, i * HEAD : i * HEAD + HEAD]
+            return 0
+
+        lax.fori_loop(0, 2, rows_of, 0)
+
+    def attend_back(m, first, last):
+        def one(i, _):
+            h = m * 3 + i
+
+            def block(rb, _):
+                at = chunk(rb, T)
+                rows = g_s[h, at, :]
+                delta = jnp.sum(rows.astype(F32) * ctx_s[h, at, :], axis=-1, keepdims=True)
+                probs = p_s[h, at, :].astype(F32)
+                score = (probs * (dot_nt(rows, v_s[h]) - delta)).astype(BF)
+                ds_s[at, :] = score
+                dq_s[0, i, at, :] = (dot(score, k_s[h]) * 0.125).astype(BF)
+                return 0
+
+            lax.fori_loop(0, 4, block, 0)
+            dq_s[1, i] = dot_tn(q_s[h], ds_s[...]).T.astype(BF)
+            dq_s[2, i] = dot_tn(g_s[h], p_s[h]).T.astype(BF)
+            return 0
+
+        lax.fori_loop(first, last, one, 0)
+
+    def collect(m):
+        for kind in range(3):
+            cat = jnp.concatenate([dq_s[kind, i] for i in range(3)], axis=1)
+            dqkv[m, :, kind * HW : kind * HW + HW] = cat
+            if kind != 1:
+                sums = column_sum(cat.astype(F32))
+                for h in (0, 1):
+                    lanes = pl.ds(pl.multiple_of(odd * H2, H2), HW)
+                    late[0, kind + h : kind + h + 1, lanes] += jnp.where(half == h, sums, 0.0)
+
+    def input_back(m):
+        def rows_of(t, _):
+            at = pl.ds(pl.multiple_of(t * 2 * T, 2 * T), 2 * T)
+            put_part(sum_input[m].buf, m, t, dot_nt(dqkv[m, at, :], w_attn[:, 0 : 3 * HW]))
+            return 0
+
+        lax.fori_loop(0, 2, rows_of, 0)
+
+    def attend_weights():
+        def cols_of(t, _):
+            at = chunk(t, 256)
+            rows = x_full[:, :, at].reshape(2 * ROWS, 256)
+            grads = dot_tn(rows, dqkv[...].reshape(2 * ROWS, 3 * HW)).astype(BF)
+            dwa[0, at, :] = grads[:, 0:H2]
+            dwa[1, at, 0:HW] = grads[:, H2 : 3 * HW]
+            rows = branch_full[:, :, at].reshape(2 * ROWS, 256)
+            outs = dot_tn(rows, ctx_cat[...].reshape(2 * ROWS, HW)).astype(BF)
+            dwa[1, at, HW : 2 * HW] = outs
+            return 0
+
+        lax.fori_loop(0, D // 256, cols_of, 0)
+
+    class Reduce:
+        def __init__(self, index, buf, incoming, zin):
+            self.buf, self.incoming, self.zin = buf, incoming, zin
+            self.swap = Copy(buf.at[other], incoming, gc_ss.at[index], gc_rs.at[index], sib)
+
+            def push(rows, slot, dev):
+                ss, rs = gz_ss.at[index, slot], gz_rs.at[index, slot]
+                return raw(buf.at[c, rows, :], zin.at[slot], ss, rs, dev)
+
+            self.to_near = push(near_z, 0, near)
+            self.to_far = push(far_z, 1, far)
+            self.to_opposite = push(opposite_z, 2, opposite)
+            self.by_near = push(opposite_z, 3, near)
+
+        def join(self):
+            self.swap.wait_recv()
+
+            def add(rows):
+                mine = self.buf[c, rows, :].astype(F32)
+                self.buf[c, rows, :] = (mine + self.incoming[rows, :].astype(F32)).astype(BF)
+
+            add(opposite_z)
+            pl.when(outer)(self.by_near.start)
+            pl.when(inner)(self.to_opposite.start)
+            add(far_z)
+            pl.when(outer)(self.to_far.start)
+            add(near_z)
+            self.to_near.start()
+            add(mine_z)
+
+        def relay(self):
+            @pl.when(inner)
+            def _():
+                self.by_near.wait_recv()
+                mine = self.buf[c, far_z, :].astype(F32)
+                self.buf[c, far_z, :] = (mine + self.zin[3].astype(F32)).astype(BF)
+                self.to_far.start()
+
+        def total(self, put):
+            self.to_near.wait_recv()
+            self.to_far.wait_recv()
+
+            def value():
+                low = self.buf[c, mine_z, :].astype(F32)
+                return low + self.zin[0].astype(F32) + self.zin[1].astype(F32)
+
+            @pl.when(inner)
+            def _():
+                self.to_opposite.wait_recv()
+                put((value() + self.zin[2].astype(F32)).astype(BF))
+
+            @pl.when(outer)
+            def _():
+                put(value().astype(BF))
+
+        def sent(self):
+            self.to_near.wait_send()
+            self.to_far.wait_send()
+            pl.when(inner)(self.to_opposite.wait_send)
+            pl.when(outer)(self.by_near.wait_send)
+
+    reduce_feed = Reduce(0, dwf, dwf_in, dwf_z)
+    reduce_attn = Reduce(1, dwa, dwa_in, dwa_z)
+
+    class Everywhere:
+        def __init__(self, buf, ss, rs, result):
+            devices = [sib, xdev, ydev, near, far]
+            self.buf, self.result = buf, result
+            self.copies = [
+                Copy(buf.at[2 * i], buf.at[2 * i + 1], ss.at[i], rs.at[i], dev)
+                for i, dev in enumerate(devices)
+            ]
+
+        def start(self):
+            self.copies[0].start()
+
+        def step(self, i):
+            self.copies[i].wait_recv()
+            value = self.buf[2 * i] + self.buf[2 * i + 1]
+            if i + 1 < len(self.copies):
+                self.buf[2 * i + 2] = value
+                self.copies[i + 1].start()
+            else:
+                self.result[...] = value
+
+    early_sum = Everywhere(early, ge_ss, ge_rs, early_ref)
+    late_sum = Everywhere(late, gl_ss, gl_rs, late_ref)
+
+    def early_start():
+        for g in (0, 1):
+            for kind in (0, 1):
+                row = 6 + (2 * g + kind) * 2
+                values = eb_acc[2 * g + kind : 2 * g + kind + 1, :]
+                for h in (0, 1):
+                    at = slice(row + h, row + h + 1)
+                    early[0, at, chunk(odd, UB)] = jnp.where(half == h, values, 0.0)
+        early_sum.start()
+
+    share_gu = Copy(w_gu.at[c], w_gu.at[c], wc_ss.at[1], wc_rs.at[1], sib)
+    down_lanes = w_down.at[:, chunk(c, UB)]
+    share_down = Copy(down_lanes, down_lanes, wc_ss.at[2], wc_rs.at[2], sib)
+
+    def take(column, own, share):
+        for index in range(len(column.pieces)):
+            column.rest(index)
+        for copy in own:
+            copy.wait()
+        share.start()
+
+    def send_rows(refs, index, m):
+        rows = refs.at[2 * c + m]
+        Copy(rows, rows, io_ss.at[index, m], io_rs.at[index, m], sib).start()
+
+    def finish_input(m):
+        ig_ref[2 * c + m] = gr1_s[m] + sum_input[m].end()
+        send_rows(ig_ref, 1, m)
+
+    class Spread:
+        def __init__(self):
+            top, bottom = pl.ds(0, DZ // 2), pl.ds(DZ // 2, DZ // 2)
+            ss, rs = gp_ss.at[0], gp_rs.at[0]
+            self.cx = Copy(gf_ref.at[b], gf_ref.at[b], ss.at[0], rs.at[0], xdev)
+            self.cy = Copy(gf_ref.at[b], gf_ref.at[b], ss.at[1], rs.at[1], ydev)
+            self.fx = Copy(gf_ref.at[bx, top], gf_ref.at[bx, top], ss.at[2], rs.at[2], ydev)
+            self.fy = Copy(gf_ref.at[by, bottom], gf_ref.at[by, bottom], ss.at[3], rs.at[3], xdev)
+
+        def start(self):
+            def put(value):
+                gf_ref[b] = value
+
+            reduce_feed.total(put)
+            self.cx.start()
+            self.cy.start()
+
+        def mid(self):
+            self.cx.wait_recv()
+            self.fx.start()
+            self.cy.wait_recv()
+            self.fy.start()
+
+    spread = Spread()
+
+    def finish_attn():
+        def put(value):
+            fin_a[...] = value
+
+        reduce_attn.total(put)
+        slot, rs = ga_ref.at[odd, c], gp_rs.at[1 + odd, c]
+        copies = [raw(fin_a, slot, gp_ss.at[1, k], rs, (z, xor(b, k), half)) for k in (3, 1, 2)]
+        cross = raw(fin_a, slot, gp_ss.at[1, 0], rs, sib)
+        for copy in copies:
+            copy.start()
+        pl.when(c != half)(cross.start)
+
+        @pl.when(c == half)
+        def _():
+            ga_ref[odd, c] = fin_a[...]
+
+        for parity in (0, 1):
+            for core in (0, 1):
+                own = jnp.logical_and(c == half, jnp.logical_and(odd == parity, c == core))
+                rs = gp_rs.at[1 + parity, core]
+                arrival = raw(fin_a, ga_ref.at[parity, core], gp_ss.at[1, 0], rs, sib)
+                pl.when(jnp.logical_not(own))(arrival.wait_recv)
+        pl.when(c != half)(cross.wait_send)
+        for copy in copies:
+            copy.wait_send()
+
+    steps = [
+        attn_share.wait_recv,
+        gather_x[0].end,
+        lambda: project(0),
+        lambda: attend(0, 0, 12),
+        lambda: branch(0),
+        sum_branch[0].start,
+        gather_x[1].end,
+        gu_column.relay_all,
+        down_column.send,
+        lambda: project(1),
+        lambda: attend(1, 0, 6),
+        sum_branch[0].mid,
+        lambda: attend(1, 6, 12),
+        lambda: branch(1),
+        sum_branch[1].start,
+        lambda: first_norm(0),
+        gather_first[0].start,
+        down_column.relay_all,
+        lambda: take(gu_column, feed_own[:2], share_gu),
+        sum_branch[1].mid,
+        gather_first[0].mid,
+        lambda: first_norm(1),
+        gather_first[1].start,
+        share_gu.wait_recv,
+        gather_first[0].end,
+        lambda: feed_forward(0),
+        lambda: take(down_column, feed_own[2:], share_down),
+        gather_first[1].mid,
+        share_down.wait_recv,
+        lambda: feed_out(0),
+        sum_feed[0].start,
+        gather_first[1].end,
+        lambda: feed_forward(1),
+        sum_feed[0].mid,
+        lambda: feed_out(1),
+        sum_feed[1].start,
+        lambda: second_norm(0),
+        gather_feed[0].start,
+        sum_feed[1].mid,
+        gather_feed[0].mid,
+        lambda: second_norm(1),
+        gather_feed[1].start,
+        lambda: send_rows(out_ref, 0, 0),
+        lambda: send_rows(out_ref, 0, 1),
+        gather_feed[0].end,
+        sum_branch[0].drain,
+        lambda: feed_backward(0),
+        sum_first[0].start,
+        gather_feed[1].mid,
+        gather_feed[1].end,
+        sum_branch[1].drain,
+        lambda: feed_backward(1),
+        sum_first[0].mid,
+        sum_first[1].start,
+        down_weights,
+        lambda: first_back(0),
+        gather_branch[0].start,
+        sum_first[1].mid,
+        expand_weights,
+        lambda: reduce_feed.swap.start(),
+        gather_branch[0].mid,
+        lambda: first_back(1),
+        gather_branch[1].start,
+        early_start,
+        reduce_feed.join,
+        gather_branch[0].end,
+        lambda: context_back(0),
+        lambda: attend_back(0, 0, 1),
+        lambda: gather_branch[1].mid(),
+        reduce_feed.relay,
+        lambda: early_sum.step(0),
+        lambda: attend_back(0, 1, 2),
+        lambda: early_sum.step(1),
+        lambda: attend_back(0, 2, 3),
+        lambda: collect(0),
+        sum_feed[0].drain,
+        lambda: input_back(0),
+        sum_input[0].start,
+        lambda: early_sum.step(2),
+        gather_branch[1].end,
+        lambda: context_back(1),
+        lambda: attend_back(1, 0, 1),
+        lambda: early_sum.step(3),
+        sum_input[0].mid,
+        lambda: attend_back(1, 1, 3),
+        lambda: early_sum.step(4),
+        lambda: collect(1),
+        sum_feed[1].drain,
+        lambda: input_back(1),
+        sum_input[1].start,
+        late_sum.start,
+        attend_weights,
+        lambda: reduce_attn.swap.start(),
+        lambda: late_sum.step(0),
+        sum_input[1].mid,
+        reduce_attn.join,
+        lambda: late_sum.step(1),
+        lambda: finish_input(0),
+        lambda: late_sum.step(2),
+        reduce_attn.relay,
+        spread.start,
+        lambda: late_sum.step(3),
+        lambda: finish_input(1),
+        lambda: late_sum.step(4),
+        spread.mid,
+        finish_attn,
+    ]
+    for step in steps:
+        step()
+
+    @pl.when(c == half)
+    def _():
+        attn_column.sent()
+        for index, (cross, _) in enumerate(attn_own):
+            pl.when(c != index)(cross.wait_send)
+
+    for index in (0, 1):
+        pl.when(c == index)(functools.partial(attn_column.relayed, index))
+    for column in (gu_column, down_column):
+        column.sent()
+        for index in range(len(column.pieces)):
+            column.relayed(index)
+    reduce_feed.sent()
+    reduce_attn.sent()
+    for copy in started:
+        copy.finish()
+
+
+def result_kernel(
+    ga_ref, gf_ref, early_ref, late_ref, out_in, ig_in,
+    out_ref, ig_ref, pw_ref, pb_ref, ow_ref, ob_ref, g1_ref, s1_ref,
+    ew_ref, eb_ref, dw_ref, db_ref, g2_ref, s2_ref,
+    gf_in, out_buf, ig_buf, ew_out, dw_out, in_sems, out_sems,
+):
+    loads = [pltpu.make_async_copy(gf_ref.at[n], gf_in.at[n], in_sems.at[n]) for n in range(4)]
+    loads.append(pltpu.make_async_copy(out_in, out_buf, in_sems.at[4]))
+    loads.append(pltpu.make_async_copy(ig_in, ig_buf, in_sems.at[5]))
+    stores = [
+        pltpu.make_async_copy(src, dst, out_sems.at[n])
+        for n, (src, dst) in enumerate(
+            ((out_buf, out_ref), (ig_buf, ig_ref), (ew_out, ew_ref), (dw_out, dw_ref))
+        )
+    ]
+    for copy in loads:
+        copy.start()
+    core = lax.axis_index("head")
+    UB = gf_ref.shape[2] // 3
+    HW = 3 * HEAD
+    for n in range(4):
+        loads[n].wait()
+        for kind in (0, 1):
+            ew_out[:, kind, n * UB : n * UB + UB] = gf_in[n, :, kind * UB : kind * UB + UB].astype(F32)
+        dw_out[:, n * UB : n * UB + UB] = gf_in[n, :, 2 * UB : 3 * UB].astype(F32)
+    stores[2].start()
+    stores[3].start()
+    for n in (0, 1):
+        loads[4 + n].wait()
+        stores[n].start()
+    sides = [
+        jnp.concatenate([ga_ref[parity, 0], ga_ref[parity, 1]], axis=1).astype(F32)
+        for parity in (0, 1)
+    ]
+    for kind in range(4):
+        cols = slice(kind * HW, kind * HW + HW)
+        both = jnp.concatenate([sides[0][:, cols], sides[1][:, cols]], axis=1)
+        if kind < 3:
+            pw_ref[kind] = both
+        else:
+            ow_ref[...] = both
+    D = early_ref.shape[1]
+    for kind in (0, 1):
+        first, second = late_ref[2 * kind : 2 * kind + 1], late_ref[2 * kind + 1 : 2 * kind + 2]
+        pair = jnp.where(core == 0, first, second)
+        pb_ref[kind : kind + 1, 0:HW] = pair[:, 0:HW]
+        pb_ref[kind : kind + 1, HW : 2 * HW] = pair[:, D // 2 : D // 2 + HW]
+        for h in (0, 1):
+            low, high = 6 + 2 * kind + h, 10 + 2 * kind + h
+            row = jnp.where(core == 0, early_ref[low : low + 1, :], early_ref[high : high + 1, :])
+            eb_ref[kind : kind + 1, h * D : h * D + D] = row
+    for row, ref in enumerate((ob_ref, g1_ref, s1_ref, db_ref, g2_ref, s2_ref)):
+        ref[...] = early_ref[row : row + 1, :].reshape(D)
+    for copy in stores:
+        copy.wait()
+
+
+def planes(
+    layer_input,
+    sequence_lengths,
+    alibi_slopes,
+    project_weight,
+    project_bias,
+    output_weight,
+    output_bias,
+    first_gain,
+    first_shift,
+    expand_weight,
+    expand_bias,
+    down_weight,
+    down_bias,
+    second_gain,
+    second_shift,
+    layer_cotangent,
+):
+    batches, tokens, width = layer_input.shape
+    units = expand_weight.shape[2]
+    shard = project_weight.shape[0]
+    half_width = project_weight.shape[2]
+    rows = 4 * tokens
+    unit = units // 4
+    vmem = pl.BlockSpec(memory_space=pltpu.VMEM)
+    hbm = pl.BlockSpec(memory_space=pl.ANY)
+    smem = pl.BlockSpec(memory_space=pltpu.SMEM)
+    dma = pltpu.SemaphoreType.DMA
+    full = pltpu.VMEM((8, tokens, width), BF)
+    head = pltpu.VMEM((6, rows, HEAD), BF)
+    own = pltpu.VMEM((2, tokens, width), F32)
+    hidden = pltpu.VMEM((2 * rows, 2 * unit), BF)
+    halves = pltpu.VMEM((4, 2, 2, tokens, width // 2), BF)
+    shape = jax.ShapeDtypeStruct
+    outs = pl.pallas_call(
+        layer_kernel,
+        out_shape=(
+            shape((batches, tokens, width), BF),
+            shape((batches, tokens, width), F32),
+            shape((2, 2, shard, half_width), BF),
+            shape((4, shard, 3 * unit), BF),
+            shape((16, width), F32),
+            shape((8, width), F32),
+        ),
+        in_specs=[vmem] * 4 + [hbm] * 2 + [smem] * 2 + [vmem] * 8,
+        out_specs=(vmem,) * 6,
+        scratch_shapes=[
+            full, full, full, full,
+            pltpu.VMEM((width, width), BF),
+            pltpu.VMEM((2, width, 2 * unit), BF),
+            pltpu.VMEM((width, 2 * unit), BF),
+            pltpu.VMEM((2, 16, units), F32),
+            pltpu.VMEM((shard, width), BF),
+            pltpu.VMEM((2, 8, tokens, width), BF),
+            halves, halves, halves,
+            head, head, head, head,
+            pltpu.VMEM((6, rows, rows), BF),
+            pltpu.VMEM((6, rows, HEAD), F32),
+            pltpu.VMEM((2, rows, 3 * HEAD), BF),
+            pltpu.VMEM((2, rows, 9 * HEAD), BF),
+            pltpu.VMEM((rows, rows), BF),
+            pltpu.VMEM((3, 3, rows, HEAD), BF),
+            pltpu.VMEM((2, rows, rows), F32),
+            hidden, hidden, hidden,
+            pltpu.VMEM((2, 2 * rows, 2 * unit), BF),
+            pltpu.VMEM((8, unit), F32),
+            own, own,
+            pltpu.VMEM((2, tokens, 1), F32),
+            own, own,
+            pltpu.VMEM((2, width, 3 * unit), BF),
+            pltpu.VMEM((width, 3 * unit), BF),
+            pltpu.VMEM((4, shard, 3 * unit), BF),
+            pltpu.VMEM((2, width, half_width), BF),
+            pltpu.VMEM((width, half_width), BF),
+            pltpu.VMEM((4, shard, half_width), BF),
+            pltpu.VMEM((shard, half_width), BF),
+            pltpu.VMEM((10, 16, width), F32),
+            pltpu.VMEM((10, 8, width), F32),
+            pltpu.VMEM((3, 8, 128), F32),
+            dma((4, 2, 4)), dma((4, 2, 4)),
+            dma((4, 2, 6)), dma((4, 2, 6)),
+            dma((2,)),
+            dma((5, 2)), dma((5, 2)),
+            dma((2, 4, 2)), dma((2, 4, 2)),
+            dma((5,)),
+            dma((3,)), dma((3,)),
+            dma((2,)), dma((2,)),
+            dma((2, 4)), dma((2, 4)),
+            dma((2, 4)), dma((3, 4)),
+            dma((5,)), dma((5,)),
+            dma((5,)), dma((5,)),
+            dma((2, 2)), dma((2, 2)),
+        ],
+        compiler_params=pltpu.CompilerParams(
+            collective_id=0, has_side_effects=True, vmem_limit_bytes=VMEM_BYTES
+        ),
+        name="encoder_layer",
+    )(
+        layer_input, layer_cotangent, jnp.transpose(project_weight, (1, 0, 2)), output_weight.T,
+        jnp.transpose(expand_weight, (1, 0, 2)), down_weight.T, jnp.transpose(sequence_lengths, (2, 1, 0)), alibi_slopes,
+        project_bias, expand_bias, output_bias, first_gain, first_shift, down_bias, second_gain, second_shift,
+    )
+    layer_output, input_gradient, attn, feed, early, late = outs
+    vector = shape((width,), F32)
+    results = pl.pallas_call(
+        result_kernel,
+        out_shape=(
+            shape((batches, tokens, width), BF),
+            shape((batches, tokens, width), F32),
+            shape((3, shard, half_width), F32),
+            shape(project_bias.shape, F32),
+            shape((shard, half_width), F32),
+            vector, vector, vector,
+            shape(expand_weight.shape, F32),
+            shape(expand_bias.shape, F32),
+            shape((shard, units), F32),
+            vector, vector, vector,
+        ),
+        in_specs=[vmem, hbm, vmem, vmem, hbm, hbm],
+        out_specs=(hbm,) * 2 + (vmem,) * 6 + (hbm, vmem, hbm) + (vmem,) * 3,
+        scratch_shapes=[
+            pltpu.VMEM(feed.shape, BF),
+            pltpu.VMEM(layer_output.shape, BF),
+            pltpu.VMEM(input_gradient.shape, F32),
+            pltpu.VMEM(expand_weight.shape, F32),
+            pltpu.VMEM((shard, units), F32),
+            dma((6,)), dma((4,)),
+        ],
+        compiler_params=pltpu.CompilerParams(vmem_limit_bytes=VMEM_BYTES),
+        name="gradient_results",
+    )(attn, feed, early, late, layer_output, input_gradient)
+    results = list(results)
+    results[2] = jnp.transpose(results[2], (1, 0, 2))
+    results[4] = results[4].T
+    results[10] = results[10].T
+    return tuple(results)
+
+
+def fits(mesh):
+    shape = dict(mesh.shape)
+    return shape["dp"] == 4 and shape["blk"] == 4 and shape["head"] == 2
+
+
 def solution(mesh):
     in_specs = (
         P(None, ("dp", "blk"), None),
@@ -391,4 +1438,5 @@
         P(),
         P(),
     )
-    return jax.shard_map(local, mesh=mesh, in_specs=in_specs, out_specs=out_specs, check_vma=False)
+    body = planes if fits(mesh) else general
+    return jax.shard_map(body, mesh=mesh, in_specs=in_specs, out_specs=out_specs, check_vma=False)

time: 767 us -> 198 us (0.26)
  waiting for transfers between devices: 436 us -> 0 us
  Pallas kernels: 0 us -> 192 us
  blocking collectives: 93.7 us -> 0 us
  matrix products: 71 us -> 0 us
  other arithmetic: 61.2 us -> 0 us
  local copies, waits for them, and re-layouts: 60.4 us -> 2.4 us
  starting transfers between devices: 19.5 us -> 0 us
  between operations: 15.7 us -> 0.81 us
    all_gather x5 -> x0, waiting for transfers between devices: 201 us -> none  [the longest x1 90.1 us: local(): lax.all_gather(expand_weight, 'dp', axis=0, tiled=True)]
    pallas_call x0 -> x2, Pallas kernels: none -> 192 us  [the longest x1 186 us: planes(): pl.pallas_call(layer_kernel, out_shape=(shape((batches, tokens, width), B...]
    reduce_scatter x3 -> x0, waiting for transfers between devices: 91.3 us -> none  [the longest x1 49.4 us: local(): lax.psum_scatter(down_part.astype(jnp.bfloat16), 'dp', scatter_dimension=...]
    ppermute x14 -> x0, waiting for transfers between devices: 87.1 us -> none  [shifted(): return lax.ppermute(value, axis, pairs)]
    psum x1 -> x0, blocking collectives: 76.8 us -> none  [local(): lax.psum((project_bias_grad, output_bias_grad, first_gain_grad, first_shi...]
    dot_general x34 -> x0, matrix products: 71 us -> none  [the longest x4 8.47 us: cycle_step(): jnp.einsum('mhqk,mkhd->mqhd', grad_score, keys_block, preferred_element_t...]
    psum x5 -> x0, waiting for transfers between devices: 55.2 us -> none  [the longest x1 18.4 us: local(): lax.psum(shards[0].astype(jnp.bfloat16), 'blk').astype(jnp.float32)]
    convert_element_type x25 -> x0, other arithmetic: 32.3 us -> none  [the longest x1 7.73 us: local(): hidden_low = hidden_act.astype(jnp.bfloat16)]
  transfers between devices with their start and end apart: 28 -> 0, of which waited for: 26 -> 0; matrix products, arithmetic and copies ran while one was open for 19% -> 0% of each run, Pallas kernels for 0% -> 0%
where the time goes in v2:
time: 198 us; the launch traced here: 195 us
  Pallas kernels  192 us (97%)
  local copies, waits for them, and re-layouts  2.4 us (1%)
    pallas_call x1, Pallas kernels, planes(): pl.pallas_call(layer_kernel, out_shape=(shape((batches, tokens, width), B...  186 us
    pallas_call x1, Pallas kernels, planes(): pl.pallas_call(result_kernel, out_shape=(shape((batches, tokens, width),...  6.45 us

profile of v2, /device:TPU:0, one launch (start us, length us, event | category | flops | bytes accessed | tf_op | source)
XLA Modules:
  0.0 195.2 jit_solution(4490268482098735489)
XLA Ops:
  0.6 2.4 %copy.32 = bf16[192,2,1536]{2,0,1:T(8,128)(2,1)} copy(bf16[192,2,1536]{2,1,0:T(2,128)(2,1)} %param.25) | data formatting | bytes 2359296 | tf_op args[9]
  3.0 185.6 %encoder_layer.1 = (bf16[4,128,768]{2,1,0:T(8,128)(2,1)}, f32[4,128,768]{2,1,0:T(8,128)}, bf16[2,2,192,384]{3,2,1,0:T(8,128)(2,1)}, bf16[4,192,1152]{2,1,0:T(8,1...) custom-call(bf16[4,128,768]{2,1,0:T(8,128)(2,1)} %x_ref.1, bf16[4,128,768]{2,1,0:T(8,128)(2,1)} %cot_ref.1, ...), custom_call_target="tpu_custom_call" | custom-call | tf_op jit(solution)/shard_map/encoder_layer/pallas_call | solution.py:1297
  188.6 6.4 %gradient_results.1 = (bf16[4,128,768]{2,1,0:T(8,128)(2,1)}, f32[4,128,768]{2,1,0:T(8,128)}, f32[3,192,384]{2,1,0:T(8,128)}, f32[2,384]{1,0:T(2,128)}, f32[192,3...) custom-call(bf16[2,2,192,384]{3,2,1,0:T(8,128)(2,1)} %get-tuple-elem, ...), custom_call_target="tpu_custom_call" | custom-call | tf_op jit(solution)/shard_map/gradient_results/pallas_call | solution.py:1367

commit v3 on v2

--- a/solution.py
+++ b/solution.py
@@ -407,7 +407,7 @@
     q_s, k_s, v_s, g_s, p_s, ctx_s, ctx_cat, dqkv, ds_s, dq_s, far_s,
     act_s, upd_s, hid_s, dgu_s, eb_acc,
     first_own, n1_s, a1_s, gr2_s, gr1_s,
-    dwf, dwf_in, dwf_z, dwa, dwa_in, dwa_z, fin_a,
+    dwd, dwd_in, dwd_z, dwe, dwe_in, dwe_z, dwa, dwa_in, dwa_z, fin_a,
     early, late, slope_s,
     ag_ss, ag_rs, rs_ss, rs_rs, pk_sem, wa_ss, wa_rs, wf_ss, wf_rs, wl_sem, wc_ss, wc_rs,
     gc_ss, gc_rs, gz_ss, gz_rs, gp_ss, gp_rs, ge_ss, ge_rs, gl_ss, gl_rs, io_ss, io_rs,
@@ -428,7 +428,8 @@
     DZ = pw_ref.shape[1]
     UB = dw_ref.shape[1] // 4
     HW = 3 * HEAD
-    lo, hi = pl.ds(0, H2), pl.ds(H2, H2)
+    S = T // 2
+    lo, hi, both = pl.ds(0, H2), pl.ds(H2, H2), pl.ds(0, D)
 
     def chunk(index, size):
         return pl.ds(pl.multiple_of(index * size, size), size)
@@ -469,83 +470,94 @@
     barrier = pltpu.get_barrier_semaphore()
     for dev in partners:
         pl.semaphore_signal(barrier, inc=1, device_id=dev, device_id_type=MESH)
-    pl.semaphore_wait(barrier, len(partners))
 
     class Gather:
-        def __init__(self, full, phase, m):
-            ss, rs = ag_ss.at[phase, m], ag_rs.at[phase, m]
-            own, sx, sy = m * 4 + b, m * 4 + bx, m * 4 + by
-            self.cx = Copy(full.at[own], full.at[own], ss.at[0], rs.at[0], xdev)
-            self.cy = Copy(full.at[own], full.at[own], ss.at[1], rs.at[1], ydev)
-            self.fx = Copy(full.at[sx, :, lo], full.at[sx, :, lo], ss.at[2], rs.at[2], ydev)
-            self.fy = Copy(full.at[sy, :, hi], full.at[sy, :, hi], ss.at[3], rs.at[3], xdev)
+        def __init__(self, full, phase, m, r):
+            ss, rs = ag_ss.at[phase, m, r], ag_rs.at[phase, m, r]
+            part_rows = pl.ds(r * S, S)
+
+            def send(slot, lanes, index, dev):
+                rows = full.at[m * 4 + slot, part_rows, lanes]
+                return Copy(rows, rows, ss.at[index], rs.at[index], dev)
+
+            self.cx, self.cy = send(b, both, 0, xdev), send(b, both, 1, ydev)
+            self.fx, self.fy = send(bx, lo, 2, ydev), send(by, hi, 3, xdev)
 
         def start(self):
             self.cx.start()
             self.cy.start()
 
-        def mid(self):
+        def mid_x(self):
             self.cx.wait_recv()
             self.fx.start()
+
+        def mid_y(self):
             self.cy.wait_recv()
             self.fy.start()
 
         def end(self):
-            self.fx.wait_recv()
-            self.fy.wait_recv()
+            for copy in (self.fx, self.fy):
+                if not copy.received:
+                    copy.wait_recv()
 
     class Scatter:
-        def __init__(self, phase, m):
-            ss, rs = rs_ss.at[phase, m], rs_rs.at[phase, m]
+        def __init__(self, phase, m, r):
+            ss, rs = rs_ss.at[phase, m, r], rs_rs.at[phase, m, r]
             buf = part.at[phase % 2]
-            own, sx, sy, sd = m * 4 + b, m * 4 + bx, m * 4 + by, m * 4 + bd
+            rows = pl.ds(r * S, S)
             ix, iy, i2 = r1x.at[phase, m], r1y.at[phase, m], r2.at[phase, m]
-            self.buf, self.own, self.sx, self.sy = buf, own, sx, sy
-            self.ix, self.iy, self.i2 = ix, iy, i2
-            self.xd = Copy(buf.at[sd, :, lo], ix.at[1], ss.at[0], rs.at[0], xdev)
-            self.yd = Copy(buf.at[sd, :, hi], iy.at[1], ss.at[1], rs.at[1], ydev)
-            self.xo = Copy(buf.at[sx, :, lo], ix.at[0], ss.at[2], rs.at[2], xdev)
-            self.yo = Copy(buf.at[sy, :, hi], iy.at[0], ss.at[3], rs.at[3], ydev)
-            self.y2 = Copy(buf.at[sy, :, lo], i2.at[0], ss.at[4], rs.at[4], ydev)
-            self.x2 = Copy(buf.at[sx, :, hi], i2.at[1], ss.at[5], rs.at[5], xdev)
+            self.own, self.sx, self.sy = m * 4 + b, m * 4 + bx, m * 4 + by
+            self.buf, self.rows, self.ix, self.iy, self.i2 = buf, rows, ix, iy, i2
+
+            def send(slot, lanes, into, at, index, dev):
+                src = buf.at[m * 4 + slot, rows, lanes]
+                return Copy(src, into.at[at, rows], ss.at[index], rs.at[index], dev)
+
+            self.xd = send(bd, lo, ix, 1, 0, xdev)
+            self.yd = send(bd, hi, iy, 1, 1, ydev)
+            self.xo = send(bx, lo, ix, 0, 2, xdev)
+            self.yo = send(by, hi, iy, 0, 3, ydev)
+            self.y2 = send(by, lo, i2, 0, 4, ydev)
+            self.x2 = send(bx, hi, i2, 1, 5, xdev)
 
         def start(self):
             for copy in (self.xd, self.yd, self.xo, self.yo):
                 copy.start()
 
-        def mid(self):
-            buf = self.buf
+        def add(self, slot, lanes, term):
+            value = self.buf[slot, self.rows, lanes].astype(F32) + term[1, self.rows].astype(F32)
+            self.buf[slot, self.rows, lanes] = value.astype(BF)
+
+        def mid_x(self):
             self.xd.wait_recv()
-            buf[self.sy, :, :H2] = (
-                buf[self.sy, :, :H2].astype(F32) + self.ix[1].astype(F32)
-            ).astype(BF)
+            self.add(self.sy, lo, self.ix)
             self.y2.start()
+
+        def mid_y(self):
             self.yd.wait_recv()
-            buf[self.sx, :, H2:] = (
-                buf[self.sx, :, H2:].astype(F32) + self.iy[1].astype(F32)
-            ).astype(BF)
+            self.add(self.sx, hi, self.iy)
             self.x2.start()
 
         def end(self):
             for copy in (self.xo, self.yo, self.y2, self.x2):
                 copy.wait_recv()
-            mine = self.buf[self.own].astype(F32)
-            low = mine[:, :H2] + self.ix[0].astype(F32) + self.i2[0].astype(F32)
-            high = mine[:, H2:] + self.iy[0].astype(F32) + self.i2[1].astype(F32)
+            mine = self.buf[self.own, self.rows].astype(F32)
+            rows = self.rows
+            low = mine[:, :H2] + self.ix[0, rows].astype(F32) + self.i2[0, rows].astype(F32)
+            high = mine[:, H2:] + self.iy[0, rows].astype(F32) + self.i2[1, rows].astype(F32)
             return jnp.concatenate([low, high], axis=1)
 
         def drain(self):
             for copy in (self.xd, self.yd, self.xo, self.yo, self.y2, self.x2):
                 copy.wait_send()
 
-    gather_x = [Gather(x_full, 0, m) for m in (0, 1)]
-    gather_first = [Gather(first_full, 1, m) for m in (0, 1)]
-    gather_feed = [Gather(feed_full, 2, m) for m in (0, 1)]
-    gather_branch = [Gather(branch_full, 3, m) for m in (0, 1)]
-    sum_branch = [Scatter(0, m) for m in (0, 1)]
-    sum_feed = [Scatter(1, m) for m in (0, 1)]
-    sum_first = [Scatter(2, m) for m in (0, 1)]
-    sum_input = [Scatter(3, m) for m in (0, 1)]
+    def chunks(kind, *args):
+        return [[kind(*args, m, r) for r in (0, 1)] for m in (0, 1)]
+
+    gather_x, gather_first = chunks(Gather, x_full, 0), chunks(Gather, first_full, 1)
+    gather_feed, gather_branch = chunks(Gather, feed_full, 2), chunks(Gather, branch_full, 3)
+    sum_branch, sum_feed = chunks(Scatter, 0), chunks(Scatter, 1)
+    sum_first, sum_input = chunks(Scatter, 2), chunks(Scatter, 3)
 
     class Column:
         def __init__(self, pieces, ss, rs):
@@ -561,10 +573,13 @@
 
         def send(self):
             for dz, copy in self.copies():
+                if dz != 3:
+                    copy.start()
+
+        def send_opposite(self):
+            for dz, copy in self.copies():
                 if dz == 3:
                     pl.when(inner)(copy.start)
-                else:
-                    copy.start()
 
         def sent(self):
             for dz, copy in self.copies():
@@ -588,6 +603,7 @@
         def relay_all(self):
             for index in range(len(self.pieces)):
                 self.relay(index)
+            self.send_opposite()
 
         def relayed(self, index):
             pl.when(inner)(self.passing(index).wait_send)
@@ -624,72 +640,80 @@
     for index, (src, place_at, _) in enumerate(gu_column.pieces + down_column.pieces):
         feed_own.append(pltpu.make_async_copy(src, place_at(mine_z), wl_sem.at[2 + index]))
 
-    for m in (0, 1):
-        x_full[m * 4 + b] = x_ref[2 * c + m]
-    gather_x[0].start()
-
-    @pl.when(c == half)
-    def _():
+    def prepare():
+        for copy in feed_own:
+            copy.start()
         shards = [pw_ref[kind] for kind in range(3)] + [ow_ref[...]]
         own_attn[...] = jnp.concatenate(
             [jnp.where(odd == 0, item[:, 0:HW], item[:, HW : 2 * HW]) for item in shards], axis=1
         )
-        attn_column.send()
-        for index, (cross, local) in enumerate(attn_own):
-            pl.when(c == index)(local.start)
-            pl.when(c != index)(cross.start)
-
-    for row in (0, 1):
-        packs[c, row : row + 1, :] = eb_ref[row : row + 1, :]
-        packs[c, row + 2 : row + 3, 0:H2] = pb_ref[row : row + 1, :]
-    for i in range(6):
-        packs[c, 10 + i : 11 + i, 0:128] = jnp.full((1, 128), slope_ref[i], F32)
+        for m in (0, 1):
+            x_full[m * 4 + b] = x_ref[2 * c + m]
+        for row in (0, 1):
+            packs[c, row : row + 1, :] = eb_ref[row : row + 1, :]
+            packs[c, row + 2 : row + 3, 0:H2] = pb_ref[row : row + 1, :]
+        for i in range(6):
+            packs[c, 10 + i : 11 + i, 0:128] = jnp.full((1, 128), slope_ref[i], F32)
+        pl.semaphore_wait(barrier, len(partners))
+
+    def start_attn():
+        @pl.when(c == half)
+        def _():
+            attn_column.send()
+            for index, (cross, local) in enumerate(attn_own):
+                pl.when(c == index)(local.start)
+                pl.when(c != index)(cross.start)
+
+        pack_copy.start()
+
     pack_copy = Copy(packs.at[c], packs.at[c], pk_sem.at[0], pk_sem.at[1], sib)
-    pack_copy.start()
-    gather_x[1].start()
-    for copy in feed_own:
-        copy.start()
-
-    for m in (0, 1):
-        start_one = len_ref[0, 0, 2 * c + m]
-        start_two = start_one + len_ref[1, 0, 2 * c + m]
-        for rb in range(4):
-            rows = lax.broadcasted_iota(jnp.int32, (T, ROWS), 0) + rb * T
-            cols = lax.broadcasted_iota(jnp.int32, (T, ROWS), 1)
-            seq_r = (rows >= start_one).astype(jnp.int32) + (rows >= start_two).astype(jnp.int32)
-            seq_c = (cols >= start_one).astype(jnp.int32) + (cols >= start_two).astype(jnp.int32)
-            distance = jnp.abs(rows - cols).astype(F32)
-            far_s[m, pl.ds(rb * T, T), :] = jnp.where(seq_r == seq_c, distance, FAR)
-    early[...] = jnp.zeros_like(early)
-    late[...] = jnp.zeros_like(late)
-    eb_acc[...] = jnp.zeros_like(eb_acc)
-
-    for index in (0, 1):
-        pl.when(c == index)(functools.partial(attn_column.relay, index))
-    gu_column.send()
-    gather_x[0].mid()
-    gather_x[1].mid()
-    pack_copy.wait_recv()
-    for index, (cross, local) in enumerate(attn_own):
-
-        @pl.when(c == index)
-        def _():
-            pl.when(c == half)(local.wait)
-            pl.when(c != half)(cross.wait_recv)
-            attn_column.rest(index)
+
+    def constants():
+        for m in (0, 1):
+            start_one = len_ref[0, 0, 2 * c + m]
+            start_two = start_one + len_ref[1, 0, 2 * c + m]
+            for rb in range(4):
+                rows = lax.broadcasted_iota(jnp.int32, (T, ROWS), 0) + rb * T
+                cols = lax.broadcasted_iota(jnp.int32, (T, ROWS), 1)
+                seq_r = (rows >= start_one).astype(jnp.int32) + (rows >= start_two).astype(jnp.int32)
+                seq_c = (cols >= start_one).astype(jnp.int32) + (cols >= start_two).astype(jnp.int32)
+                distance = jnp.abs(rows - cols).astype(F32)
+                far_s[m, pl.ds(rb * T, T), :] = jnp.where(seq_r == seq_c, distance, FAR)
+        early[...] = jnp.zeros_like(early)
+        late[...] = jnp.zeros_like(late)
+        eb_acc[...] = jnp.zeros_like(eb_acc)
+        pack_copy.wait_recv()
+        for i in range(3):
+            low, high = packs[half, 10 + i : 11 + i, 0:128], packs[half, 13 + i : 14 + i, 0:128]
+            slope_s[i] = jnp.broadcast_to(jnp.where(odd == 0, low, high), (8, 128))
+
+    def relay_attn():
+        for index in (0, 1):
+            pl.when(c == index)(functools.partial(attn_column.relay, index))
+        pl.when(c == half)(attn_column.send_opposite)
 
     lanes = w_attn.at[:, chunk(c, H2)]
     attn_share = Copy(lanes, lanes, wc_ss.at[0], wc_rs.at[0], sib)
-    attn_share.start()
-
-    for i in range(3):
-        low, high = packs[half, 10 + i : 11 + i, 0:128], packs[half, 13 + i : 14 + i, 0:128]
-        slope_s[i] = jnp.broadcast_to(jnp.where(odd == 0, low, high), (8, 128))
+
+    def share_attn():
+        for index, (cross, local) in enumerate(attn_own):
+
+            @pl.when(c == index)
+            def _():
+                pl.when(c == half)(local.wait)
+                pl.when(c != half)(cross.wait_recv)
+                attn_column.rest(index)
+
+        attn_share.start()
 
     def vector(ref):
         return ref[...].reshape(1, D)
 
     def project(m):
+        if m == 0:
+            attn_share.wait_recv()
+        for r in (0, 1):
+            gather_x[m][r].end()
         biases = packs[half, 2:4, 0:H2]
         biases = jnp.where(odd == 0, biases[:, 0:HW], biases[:, HW : 2 * HW])
 
@@ -709,140 +733,156 @@
 
         lax.fori_loop(0, 2, rows_of, 0)
 
-    def attend(m, first, last):
-        def one(index, _):
-            i, rb = index // 4, index % 4
-            at = chunk(rb, T)
-            h = m * 3 + i
-            scores = dot_nt(q_s[h, at, :], k_s[h])
-            scores = scores - slope_s[i][0:1, 0:1] * far_s[m, at, :]
-            top = jnp.max(scores, axis=-1, keepdims=True)
-            weights = jnp.exp(scores - top)
-            total = jnp.sum(weights, axis=-1, keepdims=True)
-            probs = (weights * (1.0 / total)).astype(BF)
-            p_s[h, at, :] = probs
-            ctx_s[h, at, :] = dot(probs, v_s[h])
+    def attend(m, r):
+        heads = [m * 3 + i for i in range(3)]
+
+        def one(slot, _):
+            at = pl.ds(pl.multiple_of(slot * T + r * S, S), S)
+            reach = far_s[m, at, :]
+            scores = [dot_nt(q_s[h, at, :], k_s[h]) for h in heads]
+            scores = [item - slope_s[i][0:1, 0:1] * reach for i, item in enumerate(scores)]
+            tops = [jnp.max(item, axis=-1, keepdims=True) for item in scores]
+            weights = [jnp.exp(item - top) for item, top in zip(scores, tops)]
+            totals = [jnp.sum(item, axis=-1, keepdims=True) for item in weights]
+            probs = [(item * (1.0 / total)).astype(BF) for item, total in zip(weights, totals)]
+            for h, item in zip(heads, probs):
+                p_s[h, at, :] = item
+                ctx_s[h, at, :] = dot(item, v_s[h])
             return 0
 
-        lax.fori_loop(first, last, one, 0)
-
-    def put_part(buf, m, t, rows):
-        buf[pl.ds(m * 4 + 2 * t, 2)] = rows.astype(BF).reshape(2, T, D)
-
-    def branch(m):
-        def rows_of(t, _):
-            at = pl.ds(pl.multiple_of(t * 2 * T, 2 * T), 2 * T)
+        lax.fori_loop(0, 4, one, 0)
+        for slot in range(4):
+            at = pl.ds(slot * T + r * S, S)
             cat = jnp.concatenate([ctx_s[m * 3 + i, at, :].astype(BF) for i in range(3)], axis=1)
-            ctx_cat[m, at, :] = cat
-            put_part(sum_branch[m].buf, m, t, dot_nt(cat, w_attn[:, 3 * HW : 4 * HW]))
-            return 0
-
-        lax.fori_loop(0, 2, rows_of, 0)
-
-    def first_norm(m):
-        rows = x_ref[2 * c + m].astype(F32) + sum_branch[m].end() + vector(ob_ref)
+            ctx_cat[m * 4 + slot, pl.ds(r * S, S), :] = cat
+        total = sum_branch[m][r]
+        put(total, m, r, dot_nt(take(ctx_cat, m, r), w_attn[:, 3 * HW : 4 * HW]))
+        total.start()
+
+    def put(total, m, r, rows):
+        total.buf[m * 4 : m * 4 + 4, pl.ds(r * S, S), :] = rows.astype(BF).reshape(4, S, D)
+
+    def take(refs, m, r):
+        rows = refs[m * 4 : m * 4 + 4, pl.ds(r * S, S), :]
+        return rows.reshape(4 * S, rows.shape[2])
+
+    def keep(refs, m, r, lanes, rows):
+        refs[m * 4 : m * 4 + 4, pl.ds(r * S, S), lanes] = rows.reshape(4, S, rows.shape[1])
+
+    def first_norm(m, r):
+        at = pl.ds(r * S, S)
+        rows = x_ref[2 * c + m, at, :].astype(F32) + sum_branch[m][r].end() + vector(ob_ref)
         normal, inverse = standardize(rows)
         first = normal * vector(g1_ref) + vector(s1_ref)
-        n1_s[m], a1_s[m] = normal, inverse
-        first_own[m] = first
-        first_full[m * 4 + b] = first.astype(BF)
-
-    def feed_forward(m):
-        def rows_of(t, _):
-            at = pl.ds(pl.multiple_of(m * ROWS + t * 2 * T, 2 * T), 2 * T)
-            rows = first_full[pl.ds(m * 4 + t * 2, 2)].reshape(2 * T, D)
-            for g in (0, 1):
-                cols = pl.ds(g * UB, UB)
-                bias = packs[g, 0:2, chunk(b, UB)]
-                both = dot(rows, w_gu[g])
-                gate = both[:, :UB] + bias[0:1]
-                up = both[:, UB:] + bias[1:2]
-                cdf = 0.5 + 0.5 * lax.erf(gate * 0.7071067811865476)
-                act = gate * cdf
-                slope = cdf + gate * (jnp.exp(-0.5 * gate * gate) * 0.3989422804014327)
-                hid_s[at, cols] = (act * up).astype(BF)
-                act_s[at, cols] = act.astype(BF)
-                upd_s[at, cols] = (up * slope).astype(BF)
-            return 0
-
-        lax.fori_loop(0, 2, rows_of, 0)
-
-    def feed_out(m):
-        def rows_of(t, _):
-            at = pl.ds(pl.multiple_of(m * ROWS + t * 2 * T, 2 * T), 2 * T)
-            put_part(sum_feed[m].buf, m, t, dot_nt(hid_s[at, :], w_down[...]))
-            return 0
-
-        lax.fori_loop(0, 2, rows_of, 0)
+        n1_s[m, at, :], a1_s[m, at, :] = normal, inverse
+        first_own[m, at, :] = first
+        first_full[m * 4 + b, at, :] = first.astype(BF)
+        gather_first[m][r].start()
+
+    def feed_forward(m, r):
+        if m + r == 0:
+            share_gu.wait_recv()
+        gather_first[m][r].end()
+        rows = take(first_full, m, r)
+        for g in (0, 1):
+            cols = pl.ds(g * UB, UB)
+            bias = packs[g, 0:2, chunk(b, UB)]
+            pair = dot(rows, w_gu[g])
+            gate = pair[:, :UB] + bias[0:1]
+            up = pair[:, UB:] + bias[1:2]
+            cdf = 0.5 + 0.5 * lax.erf(gate * 0.7071067811865476)
+            act = gate * cdf
+            slope = cdf + gate * (jnp.exp(-0.5 * gate * gate) * 0.3989422804014327)
+            keep(hid_s, m, r, cols, (act * up).astype(BF))
+            keep(act_s, m, r, cols, act.astype(BF))
+            keep(upd_s, m, r, cols, (up * slope).astype(BF))
+
+    def feed_out(m, r):
+        if m + r == 0:
+            share_down.wait_recv()
+        total = sum_feed[m][r]
+        put(total, m, r, dot_nt(take(hid_s, m, r), w_down[...]))
+        total.start()
 
     def add_early(row, rows):
         early[0, row : row + 1, :] += column_sum(rows)
 
-    def second_norm(m):
-        rows = first_own[m] + sum_feed[m].end() + vector(db_ref)
+    def second_norm(m, r):
+        at = pl.ds(r * S, S)
+        rows = first_own[m, at, :] + sum_feed[m][r].end() + vector(db_ref)
         normal, inverse = standardize(rows)
-        out_ref[2 * c + m] = (normal * vector(g2_ref) + vector(s2_ref)).astype(BF)
-        grad = cot_ref[2 * c + m].astype(F32)
+        out_ref[2 * c + m, at, :] = (normal * vector(g2_ref) + vector(s2_ref)).astype(BF)
+        grad = cot_ref[2 * c + m, at, :].astype(F32)
+        back = standardize_back(grad * vector(g2_ref), normal, inverse)
+        gr2_s[m, at, :] = back
+        low = back.astype(BF)
+        feed_full[m * 4 + b, at, :] = low
+        gather_feed[m][r].start()
         add_early(4, grad * normal)
         add_early(5, grad)
-        back = standardize_back(grad * vector(g2_ref), normal, inverse)
-        gr2_s[m] = back
-        low = back.astype(BF)
-        feed_full[m * 4 + b] = low
         add_early(3, low.astype(F32))
-
-    def feed_backward(m):
-        def rows_of(t, _):
-            at = pl.ds(pl.multiple_of(m * ROWS + t * 2 * T, 2 * T), 2 * T)
-            rows = feed_full[pl.ds(m * 4 + t * 2, 2)].reshape(2 * T, D)
-            hidden = dot(rows, w_down[...])
-            dgate = (hidden * upd_s[at, :].astype(F32)).astype(BF)
-            dup = (hidden * act_s[at, :].astype(F32)).astype(BF)
-            for g in (0, 1):
-                cols = slice(g * UB, g * UB + UB)
-                dgu_s[g, at, 0:UB] = dgate[:, cols]
-                dgu_s[g, at, UB : 2 * UB] = dup[:, cols]
-                eb_acc[2 * g : 2 * g + 1, :] += column_sum(dgate[:, cols].astype(F32))
-                eb_acc[2 * g + 1 : 2 * g + 2, :] += column_sum(dup[:, cols].astype(F32))
-            back = dot_nt(dgu_s[0, at, :], w_gu[0]) + dot_nt(dgu_s[1, at, :], w_gu[1])
-            put_part(sum_first[m].buf, m, t, back)
-            return 0
-
-        lax.fori_loop(0, 2, rows_of, 0)
+        if r == 1:
+            send_rows(out_ref, 0, m)
+
+    def feed_backward(m, r):
+        gather_feed[m][r].end()
+        sum_branch[m][r].drain()
+        hidden = dot(take(feed_full, m, r), w_down[...])
+        dgate = (hidden * take(upd_s, m, r).astype(F32)).astype(BF)
+        dup = (hidden * take(act_s, m, r).astype(F32)).astype(BF)
+        for g in (0, 1):
+            cols = slice(g * UB, g * UB + UB)
+            keep(dgu_s.at[g], m, r, pl.ds(0, UB), dgate[:, cols])
+            keep(dgu_s.at[g], m, r, pl.ds(UB, UB), dup[:, cols])
+        back = dot_nt(take(dgu_s.at[0], m, r), w_gu[0]) + dot_nt(take(dgu_s.at[1], m, r), w_gu[1])
+        total = sum_first[m][r]
+        put(total, m, r, back)
+        total.start()
+        for g in (0, 1):
+            cols = slice(g * UB, g * UB + UB)
+            eb_acc[2 * g : 2 * g + 1, :] += column_sum(dgate[:, cols].astype(F32))
+            eb_acc[2 * g + 1 : 2 * g + 2, :] += column_sum(dup[:, cols].astype(F32))
 
     def down_weights():
+        for m, r in ((0, 0), (0, 1), (1, 0), (1, 1)):
+            gather_feed[m][r].end()
+
         def cols_of(t, _):
             at = chunk(t, 256)
             rows = feed_full[:, :, at].reshape(2 * ROWS, 256)
-            down = dot_tn(rows, hid_s[...]).astype(BF)
+            down = dot_tn(rows, hid_s[...].reshape(2 * ROWS, 2 * UB)).astype(BF)
             for g in (0, 1):
-                dwf[g, at, 2 * UB : 3 * UB] = down[:, g * UB : g * UB + UB]
+                dwd[g, at, :] = down[:, g * UB : g * UB + UB]
             return 0
 
         lax.fori_loop(0, D // 256, cols_of, 0)
 
-    def expand_weights():
-        def cols_of(t, _):
-            at = chunk(t, 256)
-            rows = first_full[:, :, at].reshape(2 * ROWS, 256)
-            for g in (0, 1):
-                dwf[g, at, 0 : 2 * UB] = dot_tn(rows, dgu_s[g]).astype(BF)
+    def expand_weights(t):
+        at = pl.ds(t * 256, 256)
+        rows = first_full[:, :, at].reshape(2 * ROWS, 256)
+
+        def units_of(g, _):
+            dwe[g, at, :] = dot_tn(rows, dgu_s[g].reshape(2 * ROWS, 2 * UB)).astype(BF)
             return 0
 
-        lax.fori_loop(0, D // 256, cols_of, 0)
-
-    def first_back(m):
-        grad = gr2_s[m] + sum_first[m].end()
-        normal = n1_s[m]
+        lax.fori_loop(0, 2, units_of, 0)
+
+    def first_back(m, r):
+        at = pl.ds(r * S, S)
+        grad = gr2_s[m, at, :] + sum_first[m][r].end()
+        normal = n1_s[m, at, :]
+        back = standardize_back(grad * vector(g1_ref), normal, a1_s[m, at, :])
+        gr1_s[m, at, :] = back
+        low = back.astype(BF)
+        branch_full[m * 4 + b, at, :] = low
+        gather_branch[m][r].start()
         add_early(1, grad * normal)
         add_early(2, grad)
-        back = standardize_back(grad * vector(g1_ref), normal, a1_s[m])
-        gr1_s[m] = back
-        low = back.astype(BF)
-        branch_full[m * 4 + b] = low
         add_early(0, low.astype(F32))
 
     def context_back(m):
+        for r in (0, 1):
+            gather_branch[m][r].end()
         def rows_of(t, _):
             at = pl.ds(pl.multiple_of(t * 2 * T, 2 * T), 2 * T)
             rows = branch_full[pl.ds(m * 4 + t * 2, 2)].reshape(2 * T, D)
@@ -853,44 +893,44 @@
 
         lax.fori_loop(0, 2, rows_of, 0)
 
-    def attend_back(m, first, last):
-        def one(i, _):
-            h = m * 3 + i
-
-            def block(rb, _):
-                at = chunk(rb, T)
-                rows = g_s[h, at, :]
-                delta = jnp.sum(rows.astype(F32) * ctx_s[h, at, :], axis=-1, keepdims=True)
-                probs = p_s[h, at, :].astype(F32)
-                score = (probs * (dot_nt(rows, v_s[h]) - delta)).astype(BF)
-                ds_s[at, :] = score
+    def attend_back(m, part):
+        heads = [m * 3 + i for i in range(3)]
+
+        def block(rb, _):
+            at = chunk(rb, T)
+            rows = [g_s[h, at, :] for h in heads]
+            terms = [dot_nt(item, v_s[h]) for item, h in zip(rows, heads)]
+            deltas = [
+                jnp.sum(item.astype(F32) * ctx_s[h, at, :], axis=-1, keepdims=True)
+                for item, h in zip(rows, heads)
+            ]
+            for i, h in enumerate(heads):
+                score = (p_s[h, at, :].astype(F32) * (terms[i] - deltas[i])).astype(BF)
+                ds_s[i, at, :] = score
                 dq_s[0, i, at, :] = (dot(score, k_s[h]) * 0.125).astype(BF)
-                return 0
-
-            lax.fori_loop(0, 4, block, 0)
-            dq_s[1, i] = dot_tn(q_s[h], ds_s[...]).T.astype(BF)
-            dq_s[2, i] = dot_tn(g_s[h], p_s[h]).T.astype(BF)
             return 0
 
-        lax.fori_loop(first, last, one, 0)
-
-    def collect(m):
-        for kind in range(3):
-            cat = jnp.concatenate([dq_s[kind, i] for i in range(3)], axis=1)
-            dqkv[m, :, kind * HW : kind * HW + HW] = cat
-            if kind != 1:
-                sums = column_sum(cat.astype(F32))
-                for h in (0, 1):
-                    lanes = pl.ds(pl.multiple_of(odd * H2, H2), HW)
-                    late[0, kind + h : kind + h + 1, lanes] += jnp.where(half == h, sums, 0.0)
-
-    def input_back(m):
-        def rows_of(t, _):
-            at = pl.ds(pl.multiple_of(t * 2 * T, 2 * T), 2 * T)
-            put_part(sum_input[m].buf, m, t, dot_nt(dqkv[m, at, :], w_attn[:, 0 : 3 * HW]))
-            return 0
-
-        lax.fori_loop(0, 2, rows_of, 0)
+        if part < 2:
+            lax.fori_loop(2 * part, 2 * part + 2, block, 0)
+        else:
+            for i, h in enumerate(heads):
+                dq_s[1, i] = dot_tn(q_s[h], ds_s[i]).T.astype(BF)
+                dq_s[2, i] = dot_tn(g_s[h], p_s[h]).T.astype(BF)
+
+    def input_back(m, r):
+        if r == 0:
+            for kind in range(3):
+                cat = jnp.concatenate([dq_s[kind, i] for i in range(3)], axis=1)
+                dqkv[m * 4 : m * 4 + 4, :, kind * HW : kind * HW + HW] = cat.reshape(4, T, HW)
+                if kind != 1:
+                    sums = column_sum(cat.astype(F32))
+                    for h in (0, 1):
+                        lanes = pl.ds(pl.multiple_of(odd * H2, H2), HW)
+                        late[0, kind + h : kind + h + 1, lanes] += jnp.where(half == h, sums, 0.0)
+        total = sum_input[m][r]
+        sum_feed[m][r].drain()
+        put(total, m, r, dot_nt(take(dqkv, m, r), w_attn[:, 0 : 3 * HW]))
+        total.start()
 
     def attend_weights():
         def cols_of(t, _):
@@ -905,6 +945,7 @@
             return 0
 
         lax.fori_loop(0, D // 256, cols_of, 0)
+        reduce_attn.swap.start()
 
     class Reduce:
         def __init__(self, index, buf, incoming, zin):
@@ -967,12 +1008,13 @@
             pl.when(inner)(self.to_opposite.wait_send)
             pl.when(outer)(self.by_near.wait_send)
 
-    reduce_feed = Reduce(0, dwf, dwf_in, dwf_z)
-    reduce_attn = Reduce(1, dwa, dwa_in, dwa_z)
+    reduce_down = Reduce(0, dwd, dwd_in, dwd_z)
+    reduce_expand = Reduce(1, dwe, dwe_in, dwe_z)
+    reduce_attn = Reduce(2, dwa, dwa_in, dwa_z)
 
     class Everywhere:
         def __init__(self, buf, ss, rs, result):
-            devices = [sib, xdev, ydev, near, far]
+            devices = [near, far, sib, xdev, ydev]
             self.buf, self.result = buf, result
             self.copies = [
                 Copy(buf.at[2 * i], buf.at[2 * i + 1], ss.at[i], rs.at[i], dev)
@@ -1008,7 +1050,7 @@
     down_lanes = w_down.at[:, chunk(c, UB)]
     share_down = Copy(down_lanes, down_lanes, wc_ss.at[2], wc_rs.at[2], sib)
 
-    def take(column, own, share):
+    def take_weights(column, own, share):
         for index in range(len(column.pieces)):
             column.rest(index)
         for copy in own:
@@ -1019,24 +1061,30 @@
         rows = refs.at[2 * c + m]
         Copy(rows, rows, io_ss.at[index, m], io_rs.at[index, m], sib).start()
 
-    def finish_input(m):
-        ig_ref[2 * c + m] = gr1_s[m] + sum_input[m].end()
-        send_rows(ig_ref, 1, m)
+    def finish_input(m, r):
+        at = pl.ds(r * S, S)
+        ig_ref[2 * c + m, at, :] = gr1_s[m, at, :] + sum_input[m][r].end()
+        if r == 1:
+            send_rows(ig_ref, 1, m)
 
     class Spread:
-        def __init__(self):
-            top, bottom = pl.ds(0, DZ // 2), pl.ds(DZ // 2, DZ // 2)
-            ss, rs = gp_ss.at[0], gp_rs.at[0]
-            self.cx = Copy(gf_ref.at[b], gf_ref.at[b], ss.at[0], rs.at[0], xdev)
-            self.cy = Copy(gf_ref.at[b], gf_ref.at[b], ss.at[1], rs.at[1], ydev)
-            self.fx = Copy(gf_ref.at[bx, top], gf_ref.at[bx, top], ss.at[2], rs.at[2], ydev)
-            self.fy = Copy(gf_ref.at[by, bottom], gf_ref.at[by, bottom], ss.at[3], rs.at[3], xdev)
+        def __init__(self, index, reduce, lanes):
+            self.reduce, self.lanes = reduce, lanes
+            ss, rs = gp_ss.at[index], gp_rs.at[index]
+
+            def send(slot, rows, at, dev):
+                piece = gf_ref.at[slot, rows, lanes]
+                return Copy(piece, piece, ss.at[at], rs.at[at], dev)
+
+            every, top, bottom = pl.ds(0, DZ), pl.ds(0, DZ // 2), pl.ds(DZ // 2, DZ // 2)
+            self.cx, self.cy = send(b, every, 0, xdev), send(b, every, 1, ydev)
+            self.fx, self.fy = send(bx, top, 2, ydev), send(by, bottom, 3, xdev)
 
         def start(self):
-            def put(value):
-                gf_ref[b] = value
-
-            reduce_feed.total(put)
+            def put_sum(value):
+                gf_ref[b, :, self.lanes] = value
+
+            self.reduce.total(put_sum)
             self.cx.start()
             self.cy.start()
 
@@ -1046,16 +1094,17 @@
             self.cy.wait_recv()
             self.fy.start()
 
-    spread = Spread()
+    spread_down = Spread(0, reduce_down, pl.ds(2 * UB, UB))
+    spread_expand = Spread(1, reduce_expand, pl.ds(0, 2 * UB))
 
     def finish_attn():
-        def put(value):
+        def put_fin(value):
             fin_a[...] = value
 
-        reduce_attn.total(put)
-        slot, rs = ga_ref.at[odd, c], gp_rs.at[1 + odd, c]
-        copies = [raw(fin_a, slot, gp_ss.at[1, k], rs, (z, xor(b, k), half)) for k in (3, 1, 2)]
-        cross = raw(fin_a, slot, gp_ss.at[1, 0], rs, sib)
+        reduce_attn.total(put_fin)
+        slot, rs = ga_ref.at[odd, c], gp_rs.at[2 + odd, c]
+        copies = [raw(fin_a, slot, gp_ss.at[2, k], rs, (z, xor(b, k), half)) for k in (3, 1, 2)]
+        cross = raw(fin_a, slot, gp_ss.at[2, 0], rs, sib)
         for copy in copies:
             copy.start()
         pl.when(c != half)(cross.start)
@@ -1067,140 +1116,191 @@
         for parity in (0, 1):
             for core in (0, 1):
                 own = jnp.logical_and(c == half, jnp.logical_and(odd == parity, c == core))
-                rs = gp_rs.at[1 + parity, core]
-                arrival = raw(fin_a, ga_ref.at[parity, core], gp_ss.at[1, 0], rs, sib)
+                rs = gp_rs.at[2 + parity, core]
+                arrival = raw(fin_a, ga_ref.at[parity, core], gp_ss.at[2, 0], rs, sib)
                 pl.when(jnp.logical_not(own))(arrival.wait_recv)
         pl.when(c != half)(cross.wait_send)
         for copy in copies:
             copy.wait_send()
 
+    def finish():
+        @pl.when(c == half)
+        def _():
+            attn_column.sent()
+            for index, (cross, _) in enumerate(attn_own):
+                pl.when(c != index)(cross.wait_send)
+
+        for index in (0, 1):
+            pl.when(c == index)(functools.partial(attn_column.relayed, index))
+        for column in (gu_column, down_column):
+            column.sent()
+            for index in range(len(column.pieces)):
+                column.relayed(index)
+        for item in (reduce_down, reduce_expand, reduce_attn):
+            item.sent()
+        for copy in started:
+            copy.finish()
+
     steps = [
-        attn_share.wait_recv,
-        gather_x[0].end,
+        prepare,
+        start_attn,
+        gather_x[0][0].start,
+        gather_x[0][1].start,
+        gather_x[1][0].start,
+        gather_x[1][1].start,
+        constants,
+        gather_x[0][0].mid_x,
+        gather_x[0][0].mid_y,
+        gather_x[0][1].mid_x,
+        gather_x[0][1].mid_y,
+        relay_attn,
+        gu_column.send,
+        gather_x[1][0].mid_x,
+        gather_x[1][0].mid_y,
+        gather_x[1][1].mid_x,
+        gather_x[1][1].mid_y,
+        share_attn,
         lambda: project(0),
-        lambda: attend(0, 0, 12),
-        lambda: branch(0),
-        sum_branch[0].start,
-        gather_x[1].end,
+        lambda: attend(0, 0),
+        lambda: attend(0, 1),
+        lambda: project(1),
+        sum_branch[0][0].mid_x,
+        sum_branch[0][0].mid_y,
+        lambda: attend(1, 0),
+        sum_branch[0][1].mid_x,
+        sum_branch[0][1].mid_y,
         gu_column.relay_all,
+        lambda: first_norm(0, 0),
         down_column.send,
-        lambda: project(1),
-        lambda: attend(1, 0, 6),
-        sum_branch[0].mid,
-        lambda: attend(1, 6, 12),
-        lambda: branch(1),
-        sum_branch[1].start,
-        lambda: first_norm(0),
-        gather_first[0].start,
+        lambda: attend(1, 1),
+        sum_branch[1][0].mid_x,
+        sum_branch[1][0].mid_y,
+        lambda: first_norm(0, 1),
+        gather_first[0][0].mid_x,
+        gather_first[0][0].mid_y,
+        sum_branch[1][1].mid_x,
+        sum_branch[1][1].mid_y,
+        lambda: take_weights(gu_column, feed_own[:2], share_gu),
+        lambda: first_norm(1, 0),
+        gather_first[0][1].mid_x,
+        gather_first[0][1].mid_y,
+        lambda: feed_forward(0, 0),
+        lambda: first_norm(1, 1),
         down_column.relay_all,
-        lambda: take(gu_column, feed_own[:2], share_gu),
-        sum_branch[1].mid,
-        gather_first[0].mid,
-        lambda: first_norm(1),
-        gather_first[1].start,
-        share_gu.wait_recv,
-        gather_first[0].end,
-        lambda: feed_forward(0),
-        lambda: take(down_column, feed_own[2:], share_down),
-        gather_first[1].mid,
-        share_down.wait_recv,
-        lambda: feed_out(0),
-        sum_feed[0].start,
-        gather_first[1].end,
-        lambda: feed_forward(1),
-        sum_feed[0].mid,
-        lambda: feed_out(1),
-        sum_feed[1].start,
-        lambda: second_norm(0),
-        gather_feed[0].start,
-        sum_feed[1].mid,
-        gather_feed[0].mid,
-        lambda: second_norm(1),
-        gather_feed[1].start,
-        lambda: send_rows(out_ref, 0, 0),
-        lambda: send_rows(out_ref, 0, 1),
-        gather_feed[0].end,
-        sum_branch[0].drain,
-        lambda: feed_backward(0),
-        sum_first[0].start,
-        gather_feed[1].mid,
-        gather_feed[1].end,
-        sum_branch[1].drain,
-        lambda: feed_backward(1),
-        sum_first[0].mid,
-        sum_first[1].start,
+        gather_first[1][0].mid_x,
+        gather_first[1][0].mid_y,
+        lambda: feed_forward(0, 1),
+        gather_first[1][1].mid_x,
+        gather_first[1][1].mid_y,
+        lambda: take_weights(down_column, feed_own[2:], share_down),
+        lambda: feed_forward(1, 0),
+        lambda: feed_forward(1, 1),
+        lambda: feed_out(0, 0),
+        lambda: feed_out(0, 1),
+        lambda: feed_out(1, 0),
+        lambda: feed_out(1, 1),
+        sum_feed[0][0].mid_x,
+        sum_feed[0][0].mid_y,
+        sum_feed[0][1].mid_x,
+        sum_feed[0][1].mid_y,
+        sum_feed[1][0].mid_x,
+        sum_feed[1][0].mid_y,
+        sum_feed[1][1].mid_x,
+        sum_feed[1][1].mid_y,
+        lambda: second_norm(0, 0),
+        lambda: second_norm(0, 1),
+        lambda: second_norm(1, 0),
+        lambda: second_norm(1, 1),
+        gather_feed[0][0].mid_x,
+        gather_feed[0][0].mid_y,
+        gather_feed[0][1].mid_x,
+        gather_feed[0][1].mid_y,
+        gather_feed[1][0].mid_x,
+        gather_feed[1][0].mid_y,
+        gather_feed[1][1].mid_x,
+        gather_feed[1][1].mid_y,
+        lambda: feed_backward(0, 0),
+        lambda: feed_backward(0, 1),
         down_weights,
-        lambda: first_back(0),
-        gather_branch[0].start,
-        sum_first[1].mid,
-        expand_weights,
-        lambda: reduce_feed.swap.start(),
-        gather_branch[0].mid,
-        lambda: first_back(1),
-        gather_branch[1].start,
+        sum_first[0][0].mid_x,
+        sum_first[0][0].mid_y,
+        reduce_down.swap.start,
+        lambda: feed_backward(1, 0),
+        sum_first[0][1].mid_x,
+        sum_first[0][1].mid_y,
+        lambda: feed_backward(1, 1),
+        lambda: first_back(0, 0),
+        reduce_down.join,
+        sum_first[1][0].mid_x,
+        sum_first[1][0].mid_y,
+        lambda: expand_weights(0),
+        lambda: expand_weights(1),
+        sum_first[1][1].mid_x,
+        sum_first[1][1].mid_y,
+        lambda: first_back(0, 1),
+        lambda: expand_weights(2),
+        reduce_expand.swap.start,
+        gather_branch[0][0].mid_x,
+        gather_branch[0][0].mid_y,
+        lambda: first_back(1, 0),
+        reduce_down.relay,
+        lambda: first_back(1, 1),
         early_start,
-        reduce_feed.join,
-        gather_branch[0].end,
+        reduce_expand.join,
+        gather_branch[0][1].mid_x,
+        gather_branch[0][1].mid_y,
+        gather_branch[1][0].mid_x,
+        gather_branch[1][0].mid_y,
+        spread_down.start,
+        lambda: early_sum.step(0),
+        gather_branch[1][1].mid_x,
+        gather_branch[1][1].mid_y,
         lambda: context_back(0),
-        lambda: attend_back(0, 0, 1),
-        lambda: gather_branch[1].mid(),
-        reduce_feed.relay,
-        lambda: early_sum.step(0),
-        lambda: attend_back(0, 1, 2),
+        lambda: attend_back(0, 0),
+        lambda: attend_back(0, 1),
+        lambda: attend_back(0, 2),
+        lambda: input_back(0, 0),
+        spread_down.mid,
+        lambda: input_back(0, 1),
+        lambda: context_back(1),
+        lambda: attend_back(1, 0),
+        lambda: attend_back(1, 1),
+        sum_input[0][0].mid_x,
+        sum_input[0][0].mid_y,
+        lambda: attend_back(1, 2),
+        lambda: input_back(1, 0),
+        late_sum.start,
+        reduce_expand.relay,
+        sum_input[0][1].mid_x,
+        sum_input[0][1].mid_y,
+        lambda: input_back(1, 1),
+        attend_weights,
+        sum_input[1][0].mid_x,
+        sum_input[1][0].mid_y,
+        lambda: late_sum.step(0),
+        lambda: finish_input(0, 0),
         lambda: early_sum.step(1),
-        lambda: attend_back(0, 2, 3),
-        lambda: collect(0),
-        sum_feed[0].drain,
-        lambda: input_back(0),
-        sum_input[0].start,
+        lambda: finish_input(0, 1),
+        sum_input[1][1].mid_x,
+        sum_input[1][1].mid_y,
+        reduce_attn.join,
         lambda: early_sum.step(2),
-        gather_branch[1].end,
-        lambda: context_back(1),
-        lambda: attend_back(1, 0, 1),
+        lambda: finish_input(1, 0),
+        spread_expand.start,
+        lambda: late_sum.step(1),
+        lambda: finish_input(1, 1),
         lambda: early_sum.step(3),
-        sum_input[0].mid,
-        lambda: attend_back(1, 1, 3),
-        lambda: early_sum.step(4),
-        lambda: collect(1),
-        sum_feed[1].drain,
-        lambda: input_back(1),
-        sum_input[1].start,
-        late_sum.start,
-        attend_weights,
-        lambda: reduce_attn.swap.start(),
-        lambda: late_sum.step(0),
-        sum_input[1].mid,
-        reduce_attn.join,
-        lambda: late_sum.step(1),
-        lambda: finish_input(0),
         lambda: late_sum.step(2),
         reduce_attn.relay,
-        spread.start,
+        spread_expand.mid,
         lambda: late_sum.step(3),
-        lambda: finish_input(1),
+        lambda: early_sum.step(4),
+        finish_attn,
         lambda: late_sum.step(4),
-        spread.mid,
-        finish_attn,
+        finish,
     ]
     for step in steps:
         step()
-
-    @pl.when(c == half)
-    def _():
-        attn_column.sent()
-        for index, (cross, _) in enumerate(attn_own):
-            pl.when(c != index)(cross.wait_send)
-
-    for index in (0, 1):
-        pl.when(c == index)(functools.partial(attn_column.relayed, index))
-    for column in (gu_column, down_column):
-        column.sent()
-        for index in range(len(column.pieces)):
-            column.relayed(index)
-    reduce_feed.sent()
-    reduce_attn.sent()
-    for copy in started:
-        copy.finish()
 
 
 def result_kernel(
@@ -1291,7 +1391,7 @@
     full = pltpu.VMEM((8, tokens, width), BF)
     head = pltpu.VMEM((6, rows, HEAD), BF)
     own = pltpu.VMEM((2, tokens, width), F32)
-    hidden = pltpu.VMEM((2 * rows, 2 * unit), BF)
+    hidden = pltpu.VMEM((8, tokens, 2 * unit), BF)
     halves = pltpu.VMEM((4, 2, 2, tokens, width // 2), BF)
     shape = jax.ShapeDtypeStruct
     outs = pl.pallas_call(
@@ -1318,20 +1418,23 @@
             head, head, head, head,
             pltpu.VMEM((6, rows, rows), BF),
             pltpu.VMEM((6, rows, HEAD), F32),
-            pltpu.VMEM((2, rows, 3 * HEAD), BF),
-            pltpu.VMEM((2, rows, 9 * HEAD), BF),
-            pltpu.VMEM((rows, rows), BF),
+            pltpu.VMEM((8, tokens, 3 * HEAD), BF),
+            pltpu.VMEM((8, tokens, 9 * HEAD), BF),
+            pltpu.VMEM((3, rows, rows), BF),
             pltpu.VMEM((3, 3, rows, HEAD), BF),
             pltpu.VMEM((2, rows, rows), F32),
             hidden, hidden, hidden,
-            pltpu.VMEM((2, 2 * rows, 2 * unit), BF),
+            pltpu.VMEM((2, 8, tokens, 2 * unit), BF),
             pltpu.VMEM((8, unit), F32),
             own, own,
             pltpu.VMEM((2, tokens, 1), F32),
             own, own,
-            pltpu.VMEM((2, width, 3 * unit), BF),
-            pltpu.VMEM((width, 3 * unit), BF),
-            pltpu.VMEM((4, shard, 3 * unit), BF),
+            pltpu.VMEM((2, width, unit), BF),
+            pltpu.VMEM((width, unit), BF),
+            pltpu.VMEM((4, shard, unit), BF),
+            pltpu.VMEM((2, width, 2 * unit), BF),
+            pltpu.VMEM((width, 2 * unit), BF),
+            pltpu.VMEM((4, shard, 2 * unit), BF),
             pltpu.VMEM((2, width, half_width), BF),
             pltpu.VMEM((width, half_width), BF),
             pltpu.VMEM((4, shard, half_width), BF),
@@ -1339,16 +1442,16 @@
             pltpu.VMEM((10, 16, width), F32),
             pltpu.VMEM((10, 8, width), F32),
             pltpu.VMEM((3, 8, 128), F32),
-            dma((4, 2, 4)), dma((4, 2, 4)),
-            dma((4, 2, 6)), dma((4, 2, 6)),
+            dma((4, 2, 2, 4)), dma((4, 2, 2, 4)),
+            dma((4, 2, 2, 6)), dma((4, 2, 2, 6)),
             dma((2,)),
             dma((5, 2)), dma((5, 2)),
             dma((2, 4, 2)), dma((2, 4, 2)),
             dma((5,)),
             dma((3,)), dma((3,)),
-            dma((2,)), dma((2,)),
-            dma((2, 4)), dma((2, 4)),
-            dma((2, 4)), dma((3, 4)),
+            dma((3,)), dma((3,)),
+            dma((3, 4)), dma((3, 4)),
+            dma((3, 4)), dma((4, 4)),
             dma((5,)), dma((5,)),
             dma((5,)), dma((5,)),
             dma((2, 2)), dma((2, 2)),

time: 198 us -> 168 us (0.85); the launches traced: 195 us -> 168 us
  Pallas kernels: 192 us -> 165 us
    pallas_call x1, Pallas kernels: 186 us -> 158 us  [planes(): pl.pallas_call(layer_kernel, out_shape=(shape((batches, tokens, width), B...]
where the time goes in v3:
time: 168 us
  Pallas kernels  165 us (98%)
  local copies, waits for them, and re-layouts  2.4 us (1%)
    pallas_call x1, Pallas kernels, planes(): pl.pallas_call(layer_kernel, out_shape=(shape((batches, tokens, width), B...  158 us
    pallas_call x1, Pallas kernels, planes(): pl.pallas_call(result_kernel, out_shape=(shape((batches, tokens, width),...  6.45 us

profile of v3, /device:TPU:0, one launch (start us, length us, event | category | flops | bytes accessed | tf_op | source)
XLA Modules:
  0.0 167.9 jit_solution(1992275503465947498)
XLA Ops:
  0.6 2.4 %copy.32 = bf16[192,2,1536]{2,0,1:T(8,128)(2,1)} copy(bf16[192,2,1536]{2,1,0:T(2,128)(2,1)} %param.25) | data formatting | bytes 2359296 | tf_op args[9]
  3.0 158.3 %encoder_layer.1 = (bf16[4,128,768]{2,1,0:T(8,128)(2,1)}, f32[4,128,768]{2,1,0:T(8,128)}, bf16[2,2,192,384]{3,2,1,0:T(8,128)(2,1)}, bf16[4,192,1152]{2,1,0:T(8,1...) custom-call(bf16[4,128,768]{2,1,0:T(8,128)(2,1)} %x_ref.1, bf16[4,128,768]{2,1,0:T(8,128)(2,1)} %cot_ref.1, ...), custom_call_target="tpu_custom_call" | custom-call | tf_op jit(solution)/shard_map/encoder_layer/pallas_call | solution.py:1397
  161.3 6.4 %gradient_results.1 = (bf16[4,128,768]{2,1,0:T(8,128)(2,1)}, f32[4,128,768]{2,1,0:T(8,128)}, f32[3,192,384]{2,1,0:T(8,128)}, f32[2,384]{1,0:T(2,128)}, f32[192,3...) custom-call(bf16[2,2,192,384]{3,2,1,0:T(8,128)(2,1)} %get-tuple-elem, ...), custom_call_target="tpu_custom_call" | custom-call | tf_op jit(solution)/shard_map/gradient_results/pallas_call | solution.py:1470

commit v4 on v3

--- a/solution.py
+++ b/solution.py
@@ -408,9 +408,9 @@
     act_s, upd_s, hid_s, dgu_s, eb_acc,
     first_own, n1_s, a1_s, gr2_s, gr1_s,
     dwd, dwd_in, dwd_z, dwe, dwe_in, dwe_z, dwa, dwa_in, dwa_z, fin_a,
-    early, late, slope_s,
+    early, late, slope_s, out_s, ig_s, gf_s, ew_s, own_gu,
     ag_ss, ag_rs, rs_ss, rs_rs, pk_sem, wa_ss, wa_rs, wf_ss, wf_rs, wl_sem, wc_ss, wc_rs,
-    gc_ss, gc_rs, gz_ss, gz_rs, gp_ss, gp_rs, ge_ss, ge_rs, gl_ss, gl_rs, io_ss, io_rs,
+    gc_ss, gc_rs, gz_ss, gz_rs, gp_ss, gp_rs, ge_ss, ge_rs, gl_ss, gl_rs, io_ss, io_rs, st_sem,
 ):
     z, b, c = lax.axis_index("dp"), lax.axis_index("blk"), lax.axis_index("head")
     half, odd = b // 2, b % 2
@@ -436,6 +436,13 @@
 
     mine_z, near_z, far_z, opposite_z = (chunk(xor(z, k), DZ) for k in range(4))
     started = []
+    earlier = {}
+    stored = []
+
+    def store(src, dst, index):
+        copy = pltpu.make_async_copy(src, dst, st_sem.at[index])
+        copy.start()
+        stored.append(copy)
 
     def raw(src, dst, ss, rs, dev):
         return pltpu.make_async_remote_copy(
@@ -473,8 +480,10 @@
 
     class Gather:
         def __init__(self, full, phase, m, r):
-            ss, rs = ag_ss.at[phase, m, r], ag_rs.at[phase, m, r]
+            ss, rs = ag_ss.at[m, r], ag_rs.at[m, r]
             part_rows = pl.ds(r * S, S)
+            self.before = earlier.get((Gather, m, r))
+            earlier[Gather, m, r] = self
 
             def send(slot, lanes, index, dev):
                 rows = full.at[m * 4 + slot, part_rows, lanes]
@@ -484,6 +493,9 @@
             self.fx, self.fy = send(bx, lo, 2, ydev), send(by, hi, 3, xdev)
 
         def start(self):
+            if self.before is not None:
+                for copy in (self.before.cx, self.before.cy, self.before.fx, self.before.fy):
+                    copy.wait_send()
             self.cx.start()
             self.cy.start()
 
@@ -502,7 +514,9 @@
 
     class Scatter:
         def __init__(self, phase, m, r):
-            ss, rs = rs_ss.at[phase, m, r], rs_rs.at[phase, m, r]
+            ss, rs = rs_ss.at[m, r], rs_rs.at[m, r]
+            self.before = earlier.get((Scatter, m, r))
+            earlier[Scatter, m, r] = self
             buf = part.at[phase % 2]
             rows = pl.ds(r * S, S)
             ix, iy, i2 = r1x.at[phase, m], r1y.at[phase, m], r2.at[phase, m]
@@ -521,6 +535,8 @@
             self.x2 = send(bx, hi, i2, 1, 5, xdev)
 
         def start(self):
+            if self.before is not None:
+                self.before.drain()
             for copy in (self.xd, self.yd, self.xo, self.yo):
                 copy.start()
 
@@ -549,7 +565,8 @@
 
         def drain(self):
             for copy in (self.xd, self.yd, self.xo, self.yo, self.y2, self.x2):
-                copy.wait_send()
+                if not copy.sent:
+                    copy.wait_send()
 
     def chunks(kind, *args):
         return [[kind(*args, m, r) for r in (0, 1)] for m in (0, 1)]
@@ -566,27 +583,26 @@
         def copy(self, dz, index, src, dst, dev):
             return raw(src, dst, self.ss.at[dz, index], self.rs.at[dz, index], dev)
 
-        def copies(self):
+        def copies(self, index):
+            src, place_at, core = self.pieces[index]
             for dz in (2, 1, 3):
-                for index, (src, place_at, core) in enumerate(self.pieces):
-                    yield dz, self.copy(dz, index, src, place_at(mine_z), (xor(z, dz), b, core))
+                yield self.copy(dz, index, src, place_at(mine_z), (xor(z, dz), b, core))
 
         def send(self):
-            for dz, copy in self.copies():
-                if dz != 3:
-                    copy.start()
-
-        def send_opposite(self):
-            for dz, copy in self.copies():
-                if dz == 3:
-                    pl.when(inner)(copy.start)
+            for index in range(len(self.pieces)):
+                to_far, to_near, _ = self.copies(index)
+                to_far.start()
+                to_near.start()
+
+        def send_opposite(self, index):
+            pl.when(inner)(list(self.copies(index))[2].start)
 
         def sent(self):
-            for dz, copy in self.copies():
-                if dz == 3:
-                    pl.when(inner)(copy.wait_send)
-                else:
-                    copy.wait_send()
+            for index in range(len(self.pieces)):
+                to_far, to_near, to_opposite = self.copies(index)
+                to_far.wait_send()
+                to_near.wait_send()
+                pl.when(inner)(to_opposite.wait_send)
 
         def arrival(self, dz, index):
             src, place_at, _ = self.pieces[index]
@@ -600,10 +616,9 @@
             self.arrival(2, index)
             pl.when(inner)(self.passing(index).start)
 
-        def relay_all(self):
-            for index in range(len(self.pieces)):
-                self.relay(index)
-            self.send_opposite()
+        def pass_on(self, index):
+            self.relay(index)
+            self.send_opposite(index)
 
         def relayed(self, index):
             pl.when(inner)(self.passing(index).wait_send)
@@ -625,8 +640,8 @@
         attn_own.append((cross, local))
     gu_column = Column(
         [
-            (ew_ref.at[0, :, chunk(b, UB)], lambda rows: w_gu.at[c, rows, pl.ds(0, UB)], c),
-            (ew_ref.at[1, :, chunk(b, UB)], lambda rows: w_gu.at[c, rows, pl.ds(UB, UB)], c),
+            (own_gu.at[0], lambda rows: w_gu.at[c, rows, pl.ds(0, UB)], c),
+            (own_gu.at[1], lambda rows: w_gu.at[c, rows, pl.ds(UB, UB)], c),
         ],
         wf_ss.at[0],
         wf_rs.at[0],
@@ -640,9 +655,17 @@
     for index, (src, place_at, _) in enumerate(gu_column.pieces + down_column.pieces):
         feed_own.append(pltpu.make_async_copy(src, place_at(mine_z), wl_sem.at[2 + index]))
 
+    expand_copy = pltpu.make_async_copy(ew_ref.at[:, :, chunk(b, UB)], ew_s, wl_sem.at[5])
+
+    def relay_out():
+        expand_copy.wait()
+        for kind in (0, 1):
+            own_gu[kind] = ew_s[:, kind, :].astype(F32).astype(BF)
+            feed_own[kind].start()
+
     def prepare():
-        for copy in feed_own:
-            copy.start()
+        expand_copy.start()
+        feed_own[2].start()
         shards = [pw_ref[kind] for kind in range(3)] + [ow_ref[...]]
         own_attn[...] = jnp.concatenate(
             [jnp.where(odd == 0, item[:, 0:HW], item[:, HW : 2 * HW]) for item in shards], axis=1
@@ -690,7 +713,8 @@
     def relay_attn():
         for index in (0, 1):
             pl.when(c == index)(functools.partial(attn_column.relay, index))
-        pl.when(c == half)(attn_column.send_opposite)
+        for index in (0, 1):
+            pl.when(c == half)(functools.partial(attn_column.send_opposite, index))
 
     lanes = w_attn.at[:, chunk(c, H2)]
     attn_share = Copy(lanes, lanes, wc_ss.at[0], wc_rs.at[0], sib)
@@ -811,7 +835,7 @@
         at = pl.ds(r * S, S)
         rows = first_own[m, at, :] + sum_feed[m][r].end() + vector(db_ref)
         normal, inverse = standardize(rows)
-        out_ref[2 * c + m, at, :] = (normal * vector(g2_ref) + vector(s2_ref)).astype(BF)
+        out_s[m, at, :] = (normal * vector(g2_ref) + vector(s2_ref)).astype(BF)
         grad = cot_ref[2 * c + m, at, :].astype(F32)
         back = standardize_back(grad * vector(g2_ref), normal, inverse)
         gr2_s[m, at, :] = back
@@ -822,7 +846,7 @@
         add_early(5, grad)
         add_early(3, low.astype(F32))
         if r == 1:
-            send_rows(out_ref, 0, m)
+            send_rows(out_s, out_ref, 0, m)
 
     def feed_backward(m, r):
         gather_feed[m][r].end()
@@ -1057,36 +1081,40 @@
             copy.wait()
         share.start()
 
-    def send_rows(refs, index, m):
+    def send_rows(buf, refs, index, m):
         rows = refs.at[2 * c + m]
-        Copy(rows, rows, io_ss.at[index, m], io_rs.at[index, m], sib).start()
+        Copy(buf.at[m], rows, io_ss.at[index, m], io_rs.at[index, m], sib).start()
+        store(buf.at[m], rows, 2 * index + m)
 
     def finish_input(m, r):
         at = pl.ds(r * S, S)
-        ig_ref[2 * c + m, at, :] = gr1_s[m, at, :] + sum_input[m][r].end()
+        ig_s[m, at, :] = gr1_s[m, at, :] + sum_input[m][r].end()
         if r == 1:
-            send_rows(ig_ref, 1, m)
+            send_rows(ig_s, ig_ref, 1, m)
 
     class Spread:
         def __init__(self, index, reduce, lanes):
-            self.reduce, self.lanes = reduce, lanes
+            self.index, self.reduce, self.lanes = index, reduce, lanes
             ss, rs = gp_ss.at[index], gp_rs.at[index]
 
-            def send(slot, rows, at, dev):
+            def send(src, slot, rows, at, dev):
                 piece = gf_ref.at[slot, rows, lanes]
-                return Copy(piece, piece, ss.at[at], rs.at[at], dev)
+                return Copy(piece if src is None else src, piece, ss.at[at], rs.at[at], dev)
 
             every, top, bottom = pl.ds(0, DZ), pl.ds(0, DZ // 2), pl.ds(DZ // 2, DZ // 2)
-            self.cx, self.cy = send(b, every, 0, xdev), send(b, every, 1, ydev)
-            self.fx, self.fy = send(bx, top, 2, ydev), send(by, bottom, 3, xdev)
+            self.mine = gf_s.at[:, lanes]
+            self.cx = send(self.mine, b, every, 0, xdev)
+            self.cy = send(self.mine, b, every, 1, ydev)
+            self.fx, self.fy = send(None, bx, top, 2, ydev), send(None, by, bottom, 3, xdev)
 
         def start(self):
             def put_sum(value):
-                gf_ref[b, :, self.lanes] = value
+                gf_s[:, self.lanes] = value
 
             self.reduce.total(put_sum)
             self.cx.start()
             self.cy.start()
+            store(self.mine, gf_ref.at[b, :, self.lanes], 4 + self.index)
 
         def mid(self):
             self.cx.wait_recv()
@@ -1109,10 +1137,8 @@
             copy.start()
         pl.when(c != half)(cross.start)
 
-        @pl.when(c == half)
-        def _():
-            ga_ref[odd, c] = fin_a[...]
-
+        local = pltpu.make_async_copy(fin_a, slot, st_sem.at[6])
+        pl.when(c == half)(local.start)
         for parity in (0, 1):
             for core in (0, 1):
                 own = jnp.logical_and(c == half, jnp.logical_and(odd == parity, c == core))
@@ -1120,6 +1146,7 @@
                 arrival = raw(fin_a, ga_ref.at[parity, core], gp_ss.at[2, 0], rs, sib)
                 pl.when(jnp.logical_not(own))(arrival.wait_recv)
         pl.when(c != half)(cross.wait_send)
+        pl.when(c == half)(local.wait)
         for copy in copies:
             copy.wait_send()
 
@@ -1140,6 +1167,8 @@
             item.sent()
         for copy in started:
             copy.finish()
+        for copy in stored:
+            copy.wait()
 
     steps = [
         prepare,
@@ -1149,55 +1178,57 @@
         gather_x[1][0].start,
         gather_x[1][1].start,
         constants,
+        relay_out,
         gather_x[0][0].mid_x,
         gather_x[0][0].mid_y,
         gather_x[0][1].mid_x,
         gather_x[0][1].mid_y,
         relay_attn,
-        gu_column.send,
         gather_x[1][0].mid_x,
         gather_x[1][0].mid_y,
         gather_x[1][1].mid_x,
         gather_x[1][1].mid_y,
         share_attn,
+        gu_column.send,
         lambda: project(0),
         lambda: attend(0, 0),
         lambda: attend(0, 1),
-        lambda: project(1),
+        lambda: gu_column.pass_on(0),
         sum_branch[0][0].mid_x,
         sum_branch[0][0].mid_y,
+        lambda: project(1),
         lambda: attend(1, 0),
         sum_branch[0][1].mid_x,
         sum_branch[0][1].mid_y,
-        gu_column.relay_all,
+        lambda: gu_column.pass_on(1),
+        down_column.send,
         lambda: first_norm(0, 0),
-        down_column.send,
         lambda: attend(1, 1),
         sum_branch[1][0].mid_x,
         sum_branch[1][0].mid_y,
         lambda: first_norm(0, 1),
+        lambda: take_weights(gu_column, feed_own[:2], share_gu),
         gather_first[0][0].mid_x,
         gather_first[0][0].mid_y,
         sum_branch[1][1].mid_x,
         sum_branch[1][1].mid_y,
-        lambda: take_weights(gu_column, feed_own[:2], share_gu),
         lambda: first_norm(1, 0),
         gather_first[0][1].mid_x,
         gather_first[0][1].mid_y,
+        lambda: down_column.pass_on(0),
         lambda: feed_forward(0, 0),
         lambda: first_norm(1, 1),
-        down_column.relay_all,
         gather_first[1][0].mid_x,
         gather_first[1][0].mid_y,
         lambda: feed_forward(0, 1),
+        lambda: take_weights(down_column, feed_own[2:], share_down),
         gather_first[1][1].mid_x,
         gather_first[1][1].mid_y,
-        lambda: take_weights(down_column, feed_own[2:], share_down),
         lambda: feed_forward(1, 0),
-        lambda: feed_forward(1, 1),
         lambda: feed_out(0, 0),
         lambda: feed_out(0, 1),
         lambda: feed_out(1, 0),
+        lambda: feed_forward(1, 1),
         lambda: feed_out(1, 1),
         sum_feed[0][0].mid_x,
         sum_feed[0][0].mid_y,
@@ -1240,27 +1271,28 @@
         lambda: first_back(0, 1),
         lambda: expand_weights(2),
         reduce_expand.swap.start,
+        reduce_down.relay,
         gather_branch[0][0].mid_x,
         gather_branch[0][0].mid_y,
         lambda: first_back(1, 0),
-        reduce_down.relay,
         lambda: first_back(1, 1),
         early_start,
         reduce_expand.join,
         gather_branch[0][1].mid_x,
         gather_branch[0][1].mid_y,
+        spread_down.start,
+        lambda: early_sum.step(0),
         gather_branch[1][0].mid_x,
         gather_branch[1][0].mid_y,
-        spread_down.start,
-        lambda: early_sum.step(0),
         gather_branch[1][1].mid_x,
         gather_branch[1][1].mid_y,
         lambda: context_back(0),
         lambda: attend_back(0, 0),
         lambda: attend_back(0, 1),
+        reduce_expand.relay,
+        spread_down.mid,
         lambda: attend_back(0, 2),
         lambda: input_back(0, 0),
-        spread_down.mid,
         lambda: input_back(0, 1),
         lambda: context_back(1),
         lambda: attend_back(1, 0),
@@ -1268,34 +1300,33 @@
         sum_input[0][0].mid_x,
         sum_input[0][0].mid_y,
         lambda: attend_back(1, 2),
+        sum_input[0][1].mid_x,
+        sum_input[0][1].mid_y,
         lambda: input_back(1, 0),
         late_sum.start,
-        reduce_expand.relay,
-        sum_input[0][1].mid_x,
-        sum_input[0][1].mid_y,
         lambda: input_back(1, 1),
+        lambda: finish_input(0, 0),
         attend_weights,
         sum_input[1][0].mid_x,
         sum_input[1][0].mid_y,
-        lambda: late_sum.step(0),
-        lambda: finish_input(0, 0),
+        lambda: finish_input(0, 1),
         lambda: early_sum.step(1),
-        lambda: finish_input(0, 1),
+        spread_expand.start,
         sum_input[1][1].mid_x,
         sum_input[1][1].mid_y,
+        lambda: late_sum.step(0),
         reduce_attn.join,
+        lambda: finish_input(1, 0),
         lambda: early_sum.step(2),
-        lambda: finish_input(1, 0),
-        spread_expand.start,
         lambda: late_sum.step(1),
-        lambda: finish_input(1, 1),
-        lambda: early_sum.step(3),
         lambda: late_sum.step(2),
         reduce_attn.relay,
         spread_expand.mid,
+        lambda: finish_input(1, 1),
+        lambda: early_sum.step(3),
         lambda: late_sum.step(3),
+        finish_attn,
         lambda: early_sum.step(4),
-        finish_attn,
         lambda: late_sum.step(4),
         finish,
     ]
@@ -1405,7 +1436,7 @@
             shape((8, width), F32),
         ),
         in_specs=[vmem] * 4 + [hbm] * 2 + [smem] * 2 + [vmem] * 8,
-        out_specs=(vmem,) * 6,
+        out_specs=(hbm,) * 4 + (vmem,) * 2,
         scratch_shapes=[
             full, full, full, full,
             pltpu.VMEM((width, width), BF),
@@ -1442,12 +1473,17 @@
             pltpu.VMEM((10, 16, width), F32),
             pltpu.VMEM((10, 8, width), F32),
             pltpu.VMEM((3, 8, 128), F32),
-            dma((4, 2, 2, 4)), dma((4, 2, 2, 4)),
-            dma((4, 2, 2, 6)), dma((4, 2, 2, 6)),
+            pltpu.VMEM((2, tokens, width), BF),
+            own,
+            pltpu.VMEM((shard, 3 * unit), BF),
+            pltpu.VMEM((shard, 2, unit), BF),
+            pltpu.VMEM((2, shard, unit), BF),
+            dma((2, 2, 4)), dma((2, 2, 4)),
+            dma((2, 2, 6)), dma((2, 2, 6)),
             dma((2,)),
             dma((5, 2)), dma((5, 2)),
             dma((2, 4, 2)), dma((2, 4, 2)),
-            dma((5,)),
+            dma((6,)),
             dma((3,)), dma((3,)),
             dma((3,)), dma((3,)),
             dma((3, 4)), dma((3, 4)),
@@ -1455,6 +1491,7 @@
             dma((5,)), dma((5,)),
             dma((5,)), dma((5,)),
             dma((2, 2)), dma((2, 2)),
+            dma((7,)),
         ],
         compiler_params=pltpu.CompilerParams(
             collective_id=0, has_side_effects=True, vmem_limit_bytes=VMEM_BYTES
@@ -1462,7 +1499,7 @@
         name="encoder_layer",
     )(
         layer_input, layer_cotangent, jnp.transpose(project_weight, (1, 0, 2)), output_weight.T,
-        jnp.transpose(expand_weight, (1, 0, 2)), down_weight.T, jnp.transpose(sequence_lengths, (2, 1, 0)), alibi_slopes,
+        expand_weight, down_weight.T, jnp.transpose(sequence_lengths, (2, 1, 0)), alibi_slopes,
         project_bias, expand_bias, output_bias, first_gain, first_shift, down_bias, second_gain, second_shift,
     )
     layer_output, input_gradient, attn, feed, early, late = outs

time: 168 us -> 155 us (0.923)
  Pallas kernels: 165 us -> 154 us
  local copies, waits for them, and re-layouts: 2.4 us -> 0 us
    pallas_call x1, Pallas kernels: 158 us -> 148 us  [planes(): pl.pallas_call(layer_kernel, out_shape=(shape((batches, tokens, width), B...]
    unnamed x1 -> x0, local copies, waits for them, and re-layouts: 2.4 us -> none
where the time goes in v4:
time: 155 us
  Pallas kernels  154 us (99%)
    pallas_call x1, Pallas kernels, planes(): pl.pallas_call(layer_kernel, out_shape=(shape((batches, tokens, width), B...  148 us
    pallas_call x1, Pallas kernels, planes(): pl.pallas_call(result_kernel, out_shape=(shape((batches, tokens, width),...  6.45 us

profile of v4, /device:TPU:0, one launch (start us, length us, event | category | flops | bytes accessed | tf_op | source)
XLA Modules:
  0.0 155.0 jit_solution(5820497841868697096)
XLA Ops:
  0.7 147.7 %encoder_layer.1 = (bf16[4,128,768]{2,1,0:T(8,128)(2,1)}, f32[4,128,768]{2,1,0:T(8,128)}, bf16[2,2,192,384]{3,2,1,0:T(8,128)(2,1)}, bf16[4,192,1152]{2,1,0:T(8,1...) custom-call(bf16[4,128,768]{2,1,0:T(8,128)(2,1)} %x_ref.1, bf16[4,128,768]{2,1,0:T(8,128)(2,1)} %cot_ref.1, ...), custom_call_target="tpu_custom_call" | custom-call | tf_op jit(solution)/shard_map/encoder_layer/pallas_call | solution.py:1428
  148.3 6.4 %gradient_results.1 = (bf16[4,128,768]{2,1,0:T(8,128)(2,1)}, f32[4,128,768]{2,1,0:T(8,128)}, f32[3,192,384]{2,1,0:T(8,128)}, f32[2,384]{1,0:T(2,128)}, f32[192,3...) custom-call(bf16[2,2,192,384]{3,2,1,0:T(8,128)(2,1)} %get-tuple-elem, ...), custom_call_target="tpu_custom_call" | custom-call | tf_op jit(solution)/shard_map/gradient_results/pallas_call | solution.py:1507
